TPU v7x, 128 devices: a whole 4x4x4 slice. The times are simulated.
128 devices in a mesh: tiles: 32 (over x, y, core), views: 4 (over z).
Axes of the slice: x: 4, y: 4, z: 4, core: 2. Of those that a mesh axis runs over, the one named last changes fastest.
Arguments:
- params: float32 [59, 262144], P(None, 'tiles'), may hold values from -7 to 5, as said below
- camera: float32 [4, 4], P('views'), may hold values from -0.03 to 0.03
- tile_lists: int32 [4, 256, 1024], P('views', 'tiles'), may hold values from 0 to 262143, as said below
- tile_counts: int32 [4, 256], P('views', 'tiles'), may hold values from 256 to 1024
- d_image: float32 [4, 256, 3, 256], P('views', 'tiles'), may hold values from -6 to 6
Outputs:
- image: float32 [4, 256, 3, 256], P('views', 'tiles')
- grads: float32 [59, 262144], P(None, ('tiles', 'views'))
Inputs may be any that keep to these rules, and one draw needn't show every extreme that they name: `params`: each column is one Gaussian: mean (rows 0 to 2, the third 3 or more), log scales (rows 3 to 5), a quaternion (rows 6 to 9) whose first entry is 1 or more, an opacity logit (row 10), and 16 spherical-harmonic coefficients for each of 3 colors (row 11 + 3 k + c for coefficient k of color c). `tile_lists`: gaussian g belongs to shard g // 8192. Entries past a tile's count are 0. Among the live entries of the 8 tiles of one device, at most 384 name Gaussians of one shard; in every view one shard is named exactly 384 times by every device.
All inputs are finite; a program needn't handle non-finite values.
Results may differ from a plain program's by a relative error of at most 0.0003.
Values sent between devices are 32-bit elements; how exact they have to be, the bound alone decides.
No kernel may reach another device: no remote copies, remote signals or barrier semaphores. Data moves between devices by JAX's collectives and lax.ppermute only.
A program may use at most 128 MiB of HBM per device.

v0:
```python
import jax
import jax.numpy as jnp
from jax import lax
from jax.sharding import PartitionSpec as P

focal_px = 600.0
lowpass = 0.3
highest = lax.Precision.HIGHEST
harmonic_zero = 0.28209479177387814
harmonic_one = 0.4886025119029199
harmonic_two = (
    1.0925484305920792,
    -1.0925484305920792,
    0.31539156525252005,
    -1.0925484305920792,
    0.5462742152960396,
)
harmonic_three = (
    -0.5900435899266435,
    2.890611442640554,
    -0.4570457994644658,
    0.3731763325901154,
    -0.4570457994644658,
    1.445305721320277,
    -0.5900435899266435,
)


def project(gauss_rows, camera_row, center_x, center_y):
    cosine = jnp.cos(camera_row[0])
    sine_val = jnp.sin(camera_row[0])
    cam_x = cosine * gauss_rows[0] + sine_val * gauss_rows[2] + camera_row[1]
    cam_y = gauss_rows[1] + camera_row[2]
    cam_z = cosine * gauss_rows[2] - sine_val * gauss_rows[0] + camera_row[3]
    inverse_z = 1.0 / cam_z
    pos_u = focal_px * cam_x * inverse_z + center_x
    pos_v = focal_px * cam_y * inverse_z + center_y
    jac_a = focal_px * inverse_z
    jac_b = -focal_px * cam_x * inverse_z * inverse_z
    jac_c = -focal_px * cam_y * inverse_z * inverse_z
    first_row = (jac_a * cosine - jac_b * sine_val, jac_a * sine_val + jac_b * cosine)
    second_row = (-jac_c * sine_val, jac_a, jac_c * cosine)
    quaternion = gauss_rows[6:10]
    quaternion = quaternion / jnp.sqrt(jnp.sum(quaternion * quaternion, axis=0))
    quat_w, quat_x, quat_y, quat_z = (quaternion[0], quaternion[1], quaternion[2], quaternion[3])
    rotation = (
        (
            1.0 - 2.0 * (quat_y * quat_y + quat_z * quat_z),
            2.0 * (quat_x * quat_y - quat_w * quat_z),
            2.0 * (quat_x * quat_z + quat_w * quat_y),
        ),
        (
            2.0 * (quat_x * quat_y + quat_w * quat_z),
            1.0 - 2.0 * (quat_x * quat_x + quat_z * quat_z),
            2.0 * (quat_y * quat_z - quat_w * quat_x),
        ),
        (
            2.0 * (quat_x * quat_z - quat_w * quat_y),
            2.0 * (quat_y * quat_z + quat_w * quat_x),
            1.0 - 2.0 * (quat_x * quat_x + quat_y * quat_y),
        ),
    )
    scales = jnp.exp(gauss_rows[3:6])
    upper_a = [
        (first_row[0] * rotation[0][entry] + first_row[1] * rotation[2][entry]) * scales[entry]
        for entry in range(3)
    ]
    lower_a = [
        (
            second_row[0] * rotation[0][entry]
            + second_row[1] * rotation[1][entry]
            + second_row[2] * rotation[2][entry]
        )
        * scales[entry]
        for entry in range(3)
    ]
    cov_a = upper_a[0] * upper_a[0] + upper_a[1] * upper_a[1] + upper_a[2] * upper_a[2] + lowpass
    cov_b = upper_a[0] * lower_a[0] + upper_a[1] * lower_a[1] + upper_a[2] * lower_a[2]
    cov_c = lower_a[0] * lower_a[0] + lower_a[1] * lower_a[1] + lower_a[2] * lower_a[2] + lowpass
    determinant = cov_a * cov_c - cov_b * cov_b
    conic_a = cov_c / determinant
    conic_b = -cov_b / determinant
    conic_c = cov_a / determinant
    opacity = jax.nn.sigmoid(gauss_rows[10])
    dir_x = cosine * cam_x - sine_val * cam_z
    dir_y = cam_y
    dir_z = sine_val * cam_x + cosine * cam_z
    inv_len = 1.0 / jnp.sqrt(dir_x * dir_x + dir_y * dir_y + dir_z * dir_z)
    dir_x = dir_x * inv_len
    dir_y = dir_y * inv_len
    dir_z = dir_z * inv_len
    sq_x = dir_x * dir_x
    sq_y = dir_y * dir_y
    sq_z = dir_z * dir_z
    harmonics = jnp.stack(
        [
            jnp.full_like(dir_x, harmonic_zero),
            -harmonic_one * dir_y,
            harmonic_one * dir_z,
            -harmonic_one * dir_x,
            harmonic_two[0] * dir_x * dir_y,
            harmonic_two[1] * dir_y * dir_z,
            harmonic_two[2] * (2.0 * sq_z - sq_x - sq_y),
            harmonic_two[3] * dir_x * dir_z,
            harmonic_two[4] * (sq_x - sq_y),
            harmonic_three[0] * dir_y * (3.0 * sq_x - sq_y),
            harmonic_three[1] * dir_x * dir_y * dir_z,
            harmonic_three[2] * dir_y * (4.0 * sq_z - sq_x - sq_y),
            harmonic_three[3] * dir_z * (2.0 * sq_z - 3.0 * sq_x - 3.0 * sq_y),
            harmonic_three[4] * dir_x * (4.0 * sq_z - sq_x - sq_y),
            harmonic_three[5] * dir_z * (sq_x - sq_y),
            harmonic_three[6] * dir_x * (sq_x - 3.0 * sq_y),
        ]
    )
    coeffs = gauss_rows[11:59].reshape(16, 3, gauss_rows.shape[1])
    colors = jnp.sum(harmonics[:, None, :] * coeffs, axis=0) + 0.5
    return jnp.concatenate(
        [jnp.stack([pos_u, pos_v, conic_a, conic_b, conic_c, opacity]), colors], axis=0
    )


def strictly_upper(length):
    steps_idx = jnp.arange(length, dtype=jnp.int32)
    return (steps_idx[:, None] < steps_idx[None, :]).astype(jnp.float32)


def render(compact, live_count, tile_row, tile_col):
    slot_count = compact.shape[1]
    pixel_index = jnp.arange(256, dtype=jnp.int32)
    pix_x = (tile_col * 16 + pixel_index % 16).astype(jnp.float32) + 0.5
    pix_y = (tile_row * 16 + pixel_index // 16).astype(jnp.float32) + 0.5
    delta_x = pix_x[:, None] - compact[0][None, :]
    delta_y = pix_y[:, None] - compact[1][None, :]
    exponent = -0.5 * (
        compact[2][None, :] * delta_x * delta_x
        + 2.0 * compact[3][None, :] * delta_x * delta_y
        + compact[4][None, :] * delta_y * delta_y
    )
    live_slot = jnp.arange(slot_count, dtype=jnp.int32) < live_count
    alphas = jnp.where(live_slot[None, :], compact[5][None, :] * jnp.exp(exponent), 0.0)
    log_keep = jnp.log1p(-alphas).reshape(256, slot_count // 128, 128)
    within = jnp.einsum("pbj,ji->pbi", log_keep, strictly_upper(128), precision=highest)
    totals = jnp.sum(log_keep, axis=2)
    before = jnp.einsum("pb,bc->pc", totals, strictly_upper(slot_count // 128), precision=highest)
    transmit = jnp.exp((within + before[:, :, None]).reshape(256, slot_count))
    weight = transmit * alphas
    return jnp.einsum("pi,ci->cp", weight, compact[6:9], precision=highest)


def bucket_positions(owner_hits):
    slot_total = owner_hits.shape[0]
    block_count = slot_total // 128
    blocks = owner_hits.reshape(block_count, 128, owner_hits.shape[1])
    lower_tri = jnp.transpose(strictly_upper(128))
    within = jnp.einsum("ij,bjo->bio", lower_tri, blocks, precision=highest)
    totals = jnp.sum(blocks, axis=1)
    before = jnp.dot(jnp.transpose(strictly_upper(block_count)), totals, precision=highest)
    earlier = (within + before[:, None, :]).reshape(slot_total, owner_hits.shape[1])
    return jnp.sum(earlier * owner_hits, axis=1).astype(jnp.int32)


def body(params, camera, tile_lists, tile_counts, d_image):
    owners = lax.axis_size("tiles")
    shard_size = params.shape[1]
    tiles_here = tile_lists.shape[1]
    slot_count = tile_lists.shape[2]
    slot_total = tiles_here * slot_count
    capacity = 3 * slot_total // (2 * owners)
    bucket_total = owners * capacity
    row_here = lax.axis_index("tiles")
    center_x = tiles_here * 8.0
    center_y = owners * 8.0
    view_camera = camera[0]
    counts = tile_counts[0]
    gauss_ids = tile_lists[0].reshape(slot_total)
    live_slot = (jnp.arange(slot_count, dtype=jnp.int32)[None, :] < counts[:, None]).reshape(
        slot_total
    )
    owner_rank = jnp.where(live_slot, gauss_ids // shard_size, 0)
    local_index = gauss_ids % shard_size
    owner_hits = (
        (owner_rank[:, None] == jnp.arange(owners, dtype=jnp.int32)[None, :]) & live_slot[:, None]
    ).astype(jnp.float32)
    bucket_pos = bucket_positions(owner_hits)
    flat_dest = jnp.where(live_slot, owner_rank * capacity + bucket_pos, bucket_total)
    requests = (
        jnp.zeros((bucket_total + 1,), jnp.int32)
        .at[flat_dest]
        .set(local_index)[:bucket_total]
        .reshape(owners, capacity)
    )
    slot_of_bucket = (
        jnp.zeros((bucket_total + 1,), jnp.int32)
        .at[flat_dest]
        .set(jnp.arange(slot_total, dtype=jnp.int32))[:bucket_total]
    )
    bucket_filled = jnp.zeros((bucket_total + 1,), jnp.bool_).at[flat_dest].set(True)[:bucket_total]

    def lift_rows(tile_columns):
        return project(tile_columns, view_camera, center_x, center_y)

    channels = params.shape[0]
    table_rows = jnp.transpose(params)
    asked_ids = lax.all_to_all(requests, "tiles", split_axis=0, concat_axis=0, tiled=True)
    picked = table_rows[asked_ids]
    fetched = lax.all_to_all(picked, "tiles", split_axis=0, concat_axis=0, tiled=True)
    source_row = jnp.where(live_slot, owner_rank * capacity + bucket_pos, 0)
    slot_rows = fetched.reshape(bucket_total, channels)[source_row]

    def picture(rows_in):
        stacked = jnp.transpose(rows_in.reshape(tiles_here, slot_count, channels), (0, 2, 1))

        def one_tile(tile_columns, live_count, column):
            return render(lift_rows(tile_columns), live_count, row_here, column)

        return jax.vmap(one_tile)(stacked, counts, jnp.arange(tiles_here, dtype=jnp.int32))

    picture_out, pull_tiles = jax.vjp(picture, slot_rows)
    (row_grads,) = pull_tiles(d_image[0])
    outgoing = jnp.where(bucket_filled[:, None], row_grads[slot_of_bucket], 0.0).reshape(
        owners, capacity, channels
    )
    returned = lax.all_to_all(outgoing, "tiles", split_axis=0, concat_axis=0, tiled=True)
    owner_rows = (
        jnp.zeros((shard_size, channels), jnp.float32)
        .at[asked_ids.reshape(bucket_total)]
        .add(returned.reshape(bucket_total, channels))
    )
    owner_grads = jnp.transpose(owner_rows)
    summed = lax.psum_scatter(owner_grads, "views", scatter_dimension=1, tiled=True)
    return (picture_out[None], summed)


def solution(mesh):
    placed = (
        P(None, "tiles"),
        P("views", None),
        P("views", "tiles", None),
        P("views", "tiles"),
        P("views", "tiles", None, None),
    )
    return jax.shard_map(
        body,
        mesh=mesh,
        in_specs=placed,
        out_specs=(P("views", "tiles", None, None), P(None, ("tiles", "views"))),
        check_vma=False,
    )
```

profile of v0, /device:TPU:1, one launch (start us, length us, event | category | flops | bytes accessed | tf_op | source)
XLA Modules:
  0.0 587.5 jit_solution(2199348076521222412)
XLA Ops:
  13.3 30.5 %scatter_custom_fusion = s32[12289]{0:T(1024)S(1)} fusion(s32[8192]{0:T(1024)S(1)} %bitcast.444, s32[8192]{0:T(1024)S(1)} %add_select_fusion, s32[]{:T(128)} %constant.43.clone.1), kind=kCustom, calls=%fused_computation.313 | custom fusion | bytes 49160 | tf_op jit(solution)/shard_map/scatter | solution.py:189
  44.4 8.6 %all-to-all-start = ((s32[32,1,384]{2,1,0:T(1,128)}), s32[32,1,384]{2,1,0:T(1,128)S(1)}, u32[]{:S(2)}, u32[]{:S(2)}) async-start(s32[32,1,384]{2,1,0:T(1,128)} %bitcast.6), calls=%async_computation | async-start | bytes 98304 | tf_op jit(solution)/shard_map/all_to_all | solution.py:204
  53.0 3.9 copy.76
  57.0 3.4 all-to-all-done
  60.4 43.3 %gather_fusion = f32[12288,59]{1,0:T(8,128)} fusion(f32[8192,59]{1,0:T(8,128)} %bitcast.350, s32[12288]{0:T(1024)S(1)} %broadcast_clamp_fusion), kind=kCustom, calls=%fused_computation | custom fusion | bytes 5849088 | tf_op jit(solution)/shard_map/gather | solution.py:205
  103.7 6.3 %copy.78 = f32[32,384,59]{1,2,0:T(8,128)} copy(f32[32,384,59]{2,1,0:T(8,128)} %bitcast.353) | data formatting | bytes 5799936 | tf_op jit(solution)/shard_map/gather | solution.py:205
  110.0 4.1 all-to-all-start.1
  116.2 30.5 %scatter_custom_fusion.2 = s32[12289]{0:T(1024)S(1)} fusion(s32[8192]{0:T(1024)S(1)} %bitcast.445, s32[8192]{0:T(1024)S(1)} %iota.76, s32[]{:T(128)} %constant.43.clone.1), kind=kCustom, calls=%fused_computation.311 | custom fusion | bytes 49160 | tf_op jit(solution)/shard_map/scatter | solution.py:195
  146.7 34.8 %scatter_custom_fusion.1 = pred[12289]{0:T(1024)(128)(4,1)S(1)} fusion(s32[8192]{0:T(1024)S(1)} %bitcast.446, pred[8192]{0:T(1024)(128)(4,1)S(1)} %broadcast.2121, pred[]{:T(512)} %constant.140.clone.1), kind=kCustom, calls=%fused_computation.315 | custom fusion | bytes 12290 | tf_op jit(solution)/shard_map/scatter | solution.py:197
  183.0 4.2 copy.79
  187.2 30.5 %gather_fusion.1 = f32[8192,59]{1,0:T(8,128)} fusion(f32[12288,59]{1,0:T(8,128)} %bitcast.352, s32[8192]{0:T(1024)S(1)} %broadcast_clamp_fusion.1), kind=kCustom, calls=%fused_computation.1 | custom fusion | bytes 3899392 | tf_op jit(solution)/shard_map/gather | solution.py:208
  217.7 2.9 copy.81
  223.7 2.3 multiply_add_fusion.20
  232.2 2.5 copy.83
  241.8 9.1 %fusion.28 = f32[8,256,8]{1,2,0:T(8,128)S(1)} fusion(f32[8,8,128]{2,1,0:T(8,128)S(1)} %bitcast.430, f32[8,8,128]{2,1,0:T(8,128)S(1)} %bitcast.432, f32[256]{0:T(256)S(1)} %fusion.104, f32[8,8,128]{2,1,0:T(8,128)S(1)} %bitcast.434, f32[8,8,128]{2,1,0:T(8,128)S(1)} %bitcast.436, f32[8,256]{1,0:T(8,128)S(1)} %convert_add_fusion, f32[8,8,128]{2,1,0:T(8,128)S(1)} %bitcast.438, ...), kind=kLoop, calls=%fused_computation.61 | loop fusion | flops 31440896 | bytes 279552 | tf_op jit(solution)/shard_map/jvp(vmap())/reduce_sum | solution.py:143
  251.2 12.6 %add_exponential_fusion = f32[8,256,8,128]{1,3,2,0:T(8,128)S(1)} fusion(f32[8,256,8]{1,2,0:T(8,128)S(1)} %fusion.100, f32[8,8,128]{2,1,0:T(8,128)S(1)} %bitcast.431, f32[8,8,128]{2,1,0:T(8,128)S(1)} %bitcast.433, f32[256]{0:T(256)S(1)} %fusion.104, f32[8,8,128]{2,1,0:T(8,128)S(1)} %bitcast.435, f32[8,8,128]{2,1,0:T(8,128)S(1)} %bitcast.437, ...), kind=kOutput, calls=%fused_computation.59 | convolution fusion | flops 3252699136 | bytes 8668160 | tf_op jit(solution)/shard_map/jvp(vmap(pbj,ji->pbi))/dot_general | solution.py:142
  263.9 20.5 %bitcast_reduce_fusion = (f32[8,256,8]{1,2,0:T(8,128)S(1)}, f32[8,256,1024]{1,2,0:T(8,128)S(1)}, f32[8,1024,256]{2,1,0:T(8,128)}) fusion(f32[8,256,8,128]{1,3,2,0:T(8,128)S(1)} %add_exponential_fusion, f32[8,1024]{1,0:T(8,128)S(1)} %bitcast.384, f32[8,1024]{1,0:T(8,128)S(1)} %bitcast.387, f32[256]{0:T(256)S(1)} %fusion.104, f32[8,1024]{1,0:T(8,128)S(1)} %bitcast.390, ...), kind=kOutput, calls=%fused_computation.359 | convolution fusion | flops 109035520 | bytes 25568256 | tf_op jit(solution)/shard_map/transpose(jvp(vmap(pi,ci->cp)))/dot_general | solution.py:147
  284.6 5.4 broadcast_add_fusion
  290.0 12.3 %fusion.26 = (f32[8,256,1024]{1,2,0:T(8,128)S(1)}, f32[8,256,1024]{1,2,0:T(8,128)S(1)}) fusion(f32[8,256,8,128]{1,3,2,0:T(8,128)S(1)} %broadcast_add_fusion, f32[8,1024,256]{2,1,0:T(8,128)} %get-tuple-element.177, f32[8,256,8,128]{1,3,2,0:T(8,128)} %copy-done.5, f32[8,1024]{1,0:T(8,128)} %bitcast.385, f32[8,1024]{1,0:T(8,128)} %bitcast.388, ...), kind=kLoop, calls=%fused_computation.51 | loop fusion | flops 44040192 | bytes 42157056 | tf_op jit(solution)/shard_map/transpose(jvp(vmap(jit(_where))))/select_n | solution.py:140
  302.3 21.5 %fusion.21 = (f32[8,1024]{1,0:T(8,128)S(1)}, f32[8,1024]{1,0:T(8,128)S(1)}, f32[8,1024]{1,0:T(8,128)S(1)}, f32[8,1024]{1,0:T(8,128)S(1)}, f32[8,1024]{1,0:T(8,128)S(1)}, /*index=5*/f32[8,1024]{1,0:T(8,128)S(1)}) fusion(f32[8,1024]{1,0:T(8,128)} %bitcast.389, f32[256]{0:T(256)S(1)} %fusion.104, f32[8,1024]{1,0:T(8,128)} %bitcast.386, f32[8,1024]{1,0:T(8,128)} %bitcast.392, ...), kind=kLoop, calls=%fused_computation.45 | loop fusion | flops 75448320 | bytes 8791040 | tf_op jit(solution)/shard_map/transpose(jvp(vmap()))/reduce_sum | solution.py:137
  324.2 7.1 %convolution_bitcast_fusion = f32[8,3,1024]{2,1,0:T(4,128)S(1)} fusion(f32[8,256,1024]{1,2,0:T(8,128)S(1)} %get-tuple-element.111, f32[8,3,256]{2,0,1:T(8,128)S(1)} %bitcast.348), kind=kOutput, calls=%fused_computation.73 | convolution fusion | flops 75497472 | bytes 8511488 | tf_op jit(solution)/shard_map/transpose(jvp(vmap(pi,ci->cp)))/dot_general | solution.py:147
  337.0 3.6 negate_multiply_fusion
  347.6 2.8 copy.128
  350.4 43.3 %gather_fusion.2 = f32[12288,59]{1,0:T(8,128)} fusion(f32[8192,59]{1,0:T(8,128)} %bitcast.351, s32[12288]{0:T(1024)S(1)} %copy-done.38), kind=kCustom, calls=%fused_computation.2 | custom fusion | bytes 5849088 | tf_op jit(solution)/shard_map/gather | solution.py:220
  393.7 4.5 copy.112
  400.2 7.5 %all-to-all-start.2 = ((f32[32,384,59]{1,2,0:T(8,128)}), f32[32,384,59]{1,2,0:T(8,128)S(1)}, u32[]{:S(2)}, u32[]{:S(2)}) async-start(f32[32,384,59]{1,2,0:T(8,128)} %broadcast_select_fusion), calls=%async_computation.2 | async-start | bytes 6291456 | tf_op jit(solution)/shard_map/all_to_all | solution.py:223
  407.9 39.6 %all-to-all-done.2 = f32[32,384,59]{1,2,0:T(8,128)S(1)} async-done(((f32[32,384,59]{1,2,0:T(8,128)}), f32[32,384,59]{1,2,0:T(8,128)S(1)}, u32[]{:S(2)}, u32[]{:S(2)}) %all-to-all-start.2) | async-done | bytes 2900000 | tf_op jit(solution)/shard_map/all_to_all | solution.py:223
  447.5 4.2 copy.129
  451.7 79.2 %scatter_custom_fusion.3 = f32[8192,59]{1,0:T(8,128)} fusion(s32[12288]{0:T(1024)S(1)} %bitcast.443, f32[12288,59]{1,0:T(8,128)} %bitcast.374, f32[]{:T(128)} %constant.49.clone.1), kind=kCustom, calls=%fused_computation.64 | custom fusion | flops 724992 | bytes 1933824 | tf_op jit(solution)/shard_map/scatter-add | solution.py:227
  530.9 6.4 %convolution_bitcast_fusion.1 = f32[1,8,3,256]{3,2,1,0:T(4,128)S(1)} fusion(f32[8,256,1024]{1,2,0:T(8,128)} %copy-done.1, f32[8,3,1024]{2,0,1:T(8,128)S(1)} %broadcast_add_fusion.1), kind=kOutput, calls=%fused_computation.74 | convolution fusion | flops 75497472 | bytes 8511488 | tf_op jit(solution)/shard_map/jvp(vmap(pi,ci->cp))/dot_general | solution.py:147
  538.0 39.9 %reduce-scatter.2.cloned.1.call-done = f32[59,2048]{0,1:T(8,128)} async-done(((f32[59,8192]{0,1:T(8,128)}), f32[59,2048]{0,1:T(8,128)}) %reduce-scatter.2.cloned.1.call-update) | async-done | bytes 483344 | tf_op jit(solution)/shard_map/reduce_scatter | solution.py:230
  577.8 2.4 copy.116
  (186 shorter events, 40.8 us)
Async XLA Ops:
  7.2 256.7 %copy-start = (f32[1,8,3,256]{3,1,2,0:T(8,128)S(1)}, f32[1,8,3,256]{3,1,2,0:T(8,128)}, u32[]{:S(2)}) copy-start(f32[1,8,3,256]{3,1,2,0:T(8,128)} %param.9) | copy-start | bytes 73732
  44.4 15.9 %all-to-all-start = ((s32[32,1,384]{2,1,0:T(1,128)}), s32[32,1,384]{2,1,0:T(1,128)S(1)}, u32[]{:S(2)}, u32[]{:S(2)}) async-start(s32[32,1,384]{2,1,0:T(1,128)} %bitcast.6), calls=%async_computation | async-start | bytes 98304 | tf_op jit(solution)/shard_map/all_to_all | solution.py:204
  60.3 43.4 %copy-start.18 = (s32[32,1,384]{2,1,0:T(1,128)}, s32[32,1,384]{2,1,0:T(1,128)S(1)}, u32[]{:S(2)}) copy-start(s32[32,1,384]{2,1,0:T(1,128)S(1)} %all-to-all-done) | copy-start | bytes 147460
  103.7 10.4 %copy-start.43 = (f32[1,4]{1,0:T(1,128)S(1)}, f32[1,4]{1,0:T(1,128)}, u32[]{:S(2)}) copy-start(f32[1,4]{1,0:T(1,128)} %param.6) | copy-start | bytes 52
  103.7 78.0 %copy-start.44 = (s32[1,8]{1,0:T(1,128)S(1)}, s32[1,8]{1,0:T(1,128)}, u32[]{:S(2)}) copy-start(s32[1,8]{1,0:T(1,128)} %param.8) | copy-start | bytes 100
  110.0 73.0 %all-to-all-start.1 = ((f32[32,384,59]{1,2,0:T(8,128)}), f32[32,384,59]{1,2,0:T(8,128)S(1)}, u32[]{:S(2)}, u32[]{:S(2)}) async-start(f32[32,384,59]{1,2,0:T(8,128)} %copy.78), calls=%async_computation.1 | async-start | bytes 6291456 | tf_op jit(solution)/shard_map/all_to_all | solution.py:206
  220.7 30.3 %copy-start.4 = (f32[8,1024,59]{1,2,0:T(8,128)}, f32[8,1024,59]{1,2,0:T(8,128)S(1)}, u32[]{:S(2)}) copy-start(f32[8,1024,59]{1,2,0:T(8,128)S(1)} %copy.81) | copy-start | bytes 5799940
  226.0 14.4 %copy-start.10 = (f32[8,1,1024]{2,1,0:T(1,128)}, f32[8,1,1024]{2,1,0:T(1,128)S(1)}, u32[]{:S(2)}) copy-start(f32[8,1,1024]{2,1,0:T(1,128)S(1)} %get-tuple-element.74) | copy-start | bytes 98308
  226.0 14.4 %copy-start.12 = (f32[8,1,1024]{2,1,0:T(1,128)}, f32[8,1,1024]{2,1,0:T(1,128)S(1)}, u32[]{:S(2)}) copy-start(f32[8,1,1024]{2,1,0:T(1,128)S(1)} %get-tuple-element.76) | copy-start | bytes 98308
  226.0 14.4 %copy-start.26 = (f32[8,1,1024]{2,1,0:T(1,128)}, f32[8,1,1024]{2,1,0:T(1,128)S(1)}, u32[]{:S(2)}) copy-start(f32[8,1,1024]{2,1,0:T(1,128)S(1)} %get-tuple-element.75) | copy-start | bytes 98308
  226.0 14.4 %copy-start.29 = (f32[8,1,1024]{2,1,0:T(1,128)}, f32[8,1,1024]{2,1,0:T(1,128)S(1)}, u32[]{:S(2)}) copy-start(f32[8,1,1024]{2,1,0:T(1,128)S(1)} %get-tuple-element.78) | copy-start | bytes 98308
  226.0 25.0 %copy-start.24 = (f32[8,1,1024]{2,1,0:T(1,128)}, f32[8,1,1024]{2,1,0:T(1,128)S(1)}, u32[]{:S(2)}) copy-start(f32[8,1,1024]{2,1,0:T(1,128)S(1)} %get-tuple-element.114) | copy-start | bytes 98308
  232.2 31.6 %copy-start.6 = (f32[8,16,1024]{2,0,1:T(8,128)}, f32[8,16,1024]{2,0,1:T(8,128)S(1)}, u32[]{:S(2)}) copy-start(f32[8,16,1024]{2,0,1:T(8,128)S(1)} %copy.82) | copy-start | bytes 1572868
  241.5 9.7 %copy-start.42 = (pred[8,8,128]{2,1,0:T(8,128)(4,1)S(1)}, pred[8,8,128]{2,1,0:T(8,128)(4,1)}, u32[]{:S(2)}) copy-start(pred[8,8,128]{2,1,0:T(8,128)(4,1)} %broadcast_compare_fusion) | copy-start | bytes 24580
  241.7 22.2 %copy-start.32 = (f32[8,1,1024]{2,0,1:T(8,128)}, f32[8,1,1024]{2,0,1:T(8,128)S(1)}, u32[]{:S(2)}) copy-start(f32[8,1,1024]{2,0,1:T(8,128)S(1)} %copy.263) | copy-start | bytes 98308
  241.7 22.1 %copy-start.33 = (f32[8,1,1024]{2,0,1:T(8,128)}, f32[8,1,1024]{2,0,1:T(8,128)S(1)}, u32[]{:S(2)}) copy-start(f32[8,1,1024]{2,0,1:T(8,128)S(1)} %copy.264) | copy-start | bytes 98308
  241.7 22.1 %copy-start.34 = (f32[8,1,1024]{2,0,1:T(8,128)}, f32[8,1,1024]{2,0,1:T(8,128)S(1)}, u32[]{:S(2)}) copy-start(f32[8,1,1024]{2,0,1:T(8,128)S(1)} %copy.265) | copy-start | bytes 98308
  241.8 22.1 %copy-start.35 = (f32[8,1,1024]{2,0,1:T(8,128)}, f32[8,1,1024]{2,0,1:T(8,128)S(1)}, u32[]{:S(2)}) copy-start(f32[8,1,1024]{2,0,1:T(8,128)S(1)} %copy.266) | copy-start | bytes 98308
  241.8 22.1 %copy-start.36 = (f32[8,1,1024]{2,0,1:T(8,128)}, f32[8,1,1024]{2,0,1:T(8,128)S(1)}, u32[]{:S(2)}) copy-start(f32[8,1,1024]{2,0,1:T(8,128)S(1)} %copy.267) | copy-start | bytes 98308
  241.8 22.1 %copy-start.37 = (f32[8,1,1024]{2,0,1:T(8,128)}, f32[8,1,1024]{2,0,1:T(8,128)S(1)}, u32[]{:S(2)}) copy-start(f32[8,1,1024]{2,0,1:T(8,128)S(1)} %copy.268) | copy-start | bytes 98308
  251.2 12.7 %copy-start.41 = (pred[8,1024]{1,0:T(8,128)(4,1)S(1)}, pred[8,1024]{1,0:T(8,128)(4,1)}, u32[]{:S(2)}) copy-start(pred[8,1024]{1,0:T(8,128)(4,1)} %get-tuple-element.171) | copy-start | bytes 24580
  263.8 20.6 %copy-start.5 = (f32[8,256,8,128]{1,3,2,0:T(8,128)}, f32[8,256,8,128]{1,3,2,0:T(8,128)S(1)}, u32[]{:S(2)}) copy-start(f32[8,256,8,128]{1,3,2,0:T(8,128)S(1)} %add_exponential_fusion) | copy-start | bytes 25165828
  302.3 29.0 %copy-start.1 = (f32[8,256,1024]{1,2,0:T(8,128)}, f32[8,256,1024]{1,2,0:T(8,128)S(1)}, u32[]{:S(2)}) copy-start(f32[8,256,1024]{1,2,0:T(8,128)S(1)} %get-tuple-element.111) | copy-start | bytes 25165828
  302.3 29.5 %copy-start.3 = (f32[8,48,1024]{2,0,1:T(8,128)S(1)}, f32[8,48,1024]{2,0,1:T(8,128)}, u32[]{:S(2)}) copy-start(f32[8,48,1024]{2,0,1:T(8,128)} %copy-done.2) | copy-start | bytes 4718596
  302.3 29.5 %copy-start.7 = (f32[8,16,1024]{2,0,1:T(8,128)S(1)}, f32[8,16,1024]{2,0,1:T(8,128)}, u32[]{:S(2)}) copy-start(f32[8,16,1024]{2,0,1:T(8,128)} %copy-done.6) | copy-start | bytes 1572868
  331.3 10.1 %copy-start.39 = (f32[8,1024]{1,0:T(8,128)S(1)}, f32[8,1024]{1,0:T(8,128)}, u32[]{:S(2)}) copy-start(f32[8,1024]{1,0:T(8,128)} %get-tuple-element.169) | copy-start | bytes 98308
  331.3 11.3 %copy-start.23 = (f32[8,1024]{1,0:T(8,128)S(1)}, f32[8,1024]{1,0:T(8,128)}, u32[]{:S(2)}) copy-start(f32[8,1024]{1,0:T(8,128)} %copy-done.22) | copy-start | bytes 98308
  331.3 11.4 %copy-start.21 = (f32[8,1024]{1,0:T(8,128)S(1)}, f32[8,1024]{1,0:T(8,128)}, u32[]{:S(2)}) copy-start(f32[8,1024]{1,0:T(8,128)} %copy-done.20) | copy-start | bytes 98308
  331.5 12.4 %copy-start.25 = (f32[8,1,1024]{2,1,0:T(1,128)S(1)}, f32[8,1,1024]{2,1,0:T(1,128)}, u32[]{:S(2)}) copy-start(f32[8,1,1024]{2,1,0:T(1,128)} %copy-done.24) | copy-start | bytes 98308
  334.3 16.0 %copy-start.38 = (s32[12288]{0:T(1024)S(1)}, s32[12288]{0:T(1024)}, u32[]{:S(2)}) copy-start(s32[12288]{0:T(1024)} %fusion.51) | copy-start | bytes 147460
  400.2 47.3 %all-to-all-start.2 = ((f32[32,384,59]{1,2,0:T(8,128)}), f32[32,384,59]{1,2,0:T(8,128)S(1)}, u32[]{:S(2)}, u32[]{:S(2)}) async-start(f32[32,384,59]{1,2,0:T(8,128)} %broadcast_select_fusion), calls=%async_computation.2 | async-start | bytes 6291456 | tf_op jit(solution)/shard_map/all_to_all | solution.py:223
  407.7 170.1 %reduce-scatter.2.cloned.1.call-start = ((), (), s32[]{:S(2)}) async-start(), calls=%async_computation.4 | async-start | bytes 5242880 | tf_op jit(solution)/shard_map/reduce_scatter | solution.py:230
  (17 other events, 104.0 us)
Sparse Core Ops, SparseCore 0:
  531.1 46.7 reduce-scatter.1
where the time goes:
time: 596 us; the launch traced here: 587 us
  local copies, waits for them, and re-layouts  260 us (44%)
  other arithmetic  154 us (26%)
  waiting for transfers between devices  82.9 us (14%)
  matrix products  53.2 us (9%)
  starting transfers between devices  20.2 us (3%)
  between operations  17 us (3%)
    scatter-add x1, other arithmetic, body(): owner_rows = jnp.zeros((shard_size, channels), jnp.float32).at[asked_ids....  79.2 us
    gather x2, local copies, waits for them, and re-layouts, body(): picked = table_rows[asked_ids]  49.6 us
    gather x2, local copies, waits for them, and re-layouts, body(): row_grads[slot_of_bucket]  47.8 us
    reduce_scatter x1, waiting for transfers between devices, body(): lax.psum_scatter(owner_grads, 'views', scatter_dimension=1, tiled=True)  39.9 us
    all_to_all x1, waiting for transfers between devices, body(): lax.all_to_all(outgoing, 'tiles', split_axis=0, concat_axis=0, tiled=True)  39.6 us
    scatter x1, local copies, waits for them, and re-layouts, body(): jnp.zeros((bucket_total + 1,), jnp.bool_).at[flat_dest].set(True)  34.8 us
    dot_general x3, matrix products, render(): return jnp.einsum('pi,ci->cp', weight, compact[6:9], precision=highest)  34 us
    gather x1, local copies, waits for them, and re-layouts, body(): slot_rows = fetched.reshape(bucket_total, channels)[source_row]  30.5 us
  transfers between devices with their start and end apart: 4, of which 3 were waited for; matrix products, arithmetic and copies ran while one was open for 13% of the time, Pallas kernels for 0%

commit v1 on v0

v1 whole, which is shorter than its diff:
```python
import functools
import math

import jax
import jax.numpy as jnp
from jax import lax
from jax.experimental import pallas as pl
from jax.experimental.pallas import tpu as pltpu
from jax.sharding import PartitionSpec as P

focal_px = 600.0
lowpass = 0.3
harmonic_zero = 0.28209479177387814
harmonic_one = 0.4886025119029199
harmonic_two = (
    1.0925484305920792,
    -1.0925484305920792,
    0.31539156525252005,
    -1.0925484305920792,
    0.5462742152960396,
)
harmonic_three = (
    -0.5900435899266435,
    2.890611442640554,
    -0.4570457994644658,
    0.3731763325901154,
    -0.4570457994644658,
    1.445305721320277,
    -0.5900435899266435,
)
bf16 = jnp.bfloat16
f32 = jnp.float32
i32 = jnp.int32
log2_e = 1.0 / math.log(2.0)
ln_2 = math.log(2.0)
nt_dims = (((1,), (1,)), ((), ()))
vmem_bytes = 56 * 1024 * 1024
fields = 9


def split_two(values):
    upper = values.astype(bf16)
    lower = (values - upper.astype(f32)).astype(bf16)
    return upper, lower


def split_three(values):
    upper = values.astype(bf16)
    rest = values - upper.astype(f32)
    middle = rest.astype(bf16)
    lower = (rest - middle.astype(f32)).astype(bf16)
    return upper, middle, lower


def project(gauss_rows, camera_row, center_x, center_y):
    cosine, sine_val, shift_x, shift_y, shift_z = camera_row
    cam_x = cosine * gauss_rows[0] + sine_val * gauss_rows[2] + shift_x
    cam_y = gauss_rows[1] + shift_y
    cam_z = cosine * gauss_rows[2] - sine_val * gauss_rows[0] + shift_z
    inverse_z = 1.0 / cam_z
    jac_a = focal_px * inverse_z
    pos_u = jac_a * cam_x + center_x
    pos_v = jac_a * cam_y + center_y
    jac_b = -jac_a * cam_x * inverse_z
    jac_c = -jac_a * cam_y * inverse_z
    first_row = (jac_a * cosine - jac_b * sine_val, jac_a * sine_val + jac_b * cosine)
    second_row = (-jac_c * sine_val, jac_a, jac_c * cosine)
    quaternion = gauss_rows[6:10]
    inv_norm = lax.rsqrt(
        quaternion[0] * quaternion[0]
        + quaternion[1] * quaternion[1]
        + quaternion[2] * quaternion[2]
        + quaternion[3] * quaternion[3]
    )
    quat_w, quat_x, quat_y, quat_z = (entry * inv_norm for entry in quaternion)
    rotation = (
        (
            1.0 - 2.0 * (quat_y * quat_y + quat_z * quat_z),
            2.0 * (quat_x * quat_y - quat_w * quat_z),
            2.0 * (quat_x * quat_z + quat_w * quat_y),
        ),
        (
            2.0 * (quat_x * quat_y + quat_w * quat_z),
            1.0 - 2.0 * (quat_x * quat_x + quat_z * quat_z),
            2.0 * (quat_y * quat_z - quat_w * quat_x),
        ),
        (
            2.0 * (quat_x * quat_z - quat_w * quat_y),
            2.0 * (quat_y * quat_z + quat_w * quat_x),
            1.0 - 2.0 * (quat_x * quat_x + quat_y * quat_y),
        ),
    )
    scales = [jnp.exp(entry) for entry in gauss_rows[3:6]]
    upper_a = [
        (first_row[0] * rotation[0][entry] + first_row[1] * rotation[2][entry]) * scales[entry]
        for entry in range(3)
    ]
    lower_a = [
        (
            second_row[0] * rotation[0][entry]
            + second_row[1] * rotation[1][entry]
            + second_row[2] * rotation[2][entry]
        )
        * scales[entry]
        for entry in range(3)
    ]
    cov_a = upper_a[0] * upper_a[0] + upper_a[1] * upper_a[1] + upper_a[2] * upper_a[2] + lowpass
    cov_b = upper_a[0] * lower_a[0] + upper_a[1] * lower_a[1] + upper_a[2] * lower_a[2]
    cov_c = lower_a[0] * lower_a[0] + lower_a[1] * lower_a[1] + lower_a[2] * lower_a[2] + lowpass
    inv_det = 1.0 / (cov_a * cov_c - cov_b * cov_b)
    coef_a = (-0.5 * log2_e) * cov_c * inv_det
    coef_b = log2_e * cov_b * inv_det
    coef_c = (-0.5 * log2_e) * cov_a * inv_det
    log_opacity = -log2_e * jnp.log(1.0 + jnp.exp(-gauss_rows[10]))
    dir_x = cosine * cam_x - sine_val * cam_z
    dir_y = cam_y
    dir_z = sine_val * cam_x + cosine * cam_z
    inv_len = lax.rsqrt(dir_x * dir_x + dir_y * dir_y + dir_z * dir_z)
    dir_x = dir_x * inv_len
    dir_y = dir_y * inv_len
    dir_z = dir_z * inv_len
    sq_x = dir_x * dir_x
    sq_y = dir_y * dir_y
    sq_z = dir_z * dir_z
    harmonics = (
        harmonic_zero,
        -harmonic_one * dir_y,
        harmonic_one * dir_z,
        -harmonic_one * dir_x,
        harmonic_two[0] * dir_x * dir_y,
        harmonic_two[1] * dir_y * dir_z,
        harmonic_two[2] * (2.0 * sq_z - sq_x - sq_y),
        harmonic_two[3] * dir_x * dir_z,
        harmonic_two[4] * (sq_x - sq_y),
        harmonic_three[0] * dir_y * (3.0 * sq_x - sq_y),
        harmonic_three[1] * dir_x * dir_y * dir_z,
        harmonic_three[2] * dir_y * (4.0 * sq_z - sq_x - sq_y),
        harmonic_three[3] * dir_z * (2.0 * sq_z - 3.0 * sq_x - 3.0 * sq_y),
        harmonic_three[4] * dir_x * (4.0 * sq_z - sq_x - sq_y),
        harmonic_three[5] * dir_z * (sq_x - sq_y),
        harmonic_three[6] * dir_x * (sq_x - 3.0 * sq_y),
    )
    colors = []
    for channel in range(3):
        total = harmonics[0] * gauss_rows[11 + channel] + 0.5
        for basis in range(1, 16):
            total = total + harmonics[basis] * gauss_rows[11 + 3 * basis + channel]
        colors.append(total)
    return (pos_u, pos_v, coef_a, coef_b, coef_c, log_opacity, *colors)


def project_kernel(camera_ref, params_ref, table_ref):
    rows = params_ref.shape[1]
    camera_row = [camera_ref[entry] for entry in range(5)]
    center_x, center_y = camera_ref[5], camera_ref[6]

    def step(part, carry):
        at = pl.multiple_of(part * 16, 16)
        gauss_rows = [params_ref[channel, pl.ds(at, 16), :] for channel in range(params_ref.shape[0])]
        outputs = project(gauss_rows, camera_row, center_x, center_y)
        for field, values in enumerate(outputs):
            pieces = split_three(values)
            table_ref[pl.ds(field * rows + at, 16), :] = pieces[0]
            table_ref[pl.ds((fields + field) * rows + at, 16), :] = pieces[1]
            if field < 2:
                table_ref[pl.ds((2 * fields + field) * rows + at, 16), :] = pieces[2]
        return carry

    lax.fori_loop(0, rows // 16, step, 0)


def bucket_kernel(counts_ref, lists_ref, requests_ref, rank_ref, hits_ref, earlier_ref, *, owners, capacity, shift):
    tiles, slots = lists_ref.shape
    blocks = slots // 256
    upper = (
        lax.broadcasted_iota(i32, (256, 256), 0) < lax.broadcasted_iota(i32, (256, 256), 1)
    ).astype(f32).astype(bf16)
    owner_rows = lax.broadcasted_iota(i32, (owners, 256), 0)
    lane = lax.broadcasted_iota(i32, (1, 256), 1)
    for tile in range(tiles):
        for block in range(blocks):
            ids = lists_ref[tile : tile + 1, block * 256 : block * 256 + 256]
            owner = jnp.where(lane + block * 256 < counts_ref[tile], ids >> shift, -1)
            at = (tile * blocks + block) * owners
            hits_ref[at : at + owners, :] = jnp.where(owner_rows == owner, 1.0, 0.0).astype(bf16)
    earlier_ref[...] = jnp.dot(hits_ref[...], upper, preferred_element_type=f32)
    rank_rows = lax.broadcasted_iota(i32, (capacity, 256), 0)
    carry = jnp.zeros((owners, 1), f32)
    total = jnp.zeros((2 * owners, capacity), f32)
    for tile in range(tiles):
        for block in range(blocks):
            at = (tile * blocks + block) * owners
            hits = hits_ref[at : at + owners, :].astype(f32)
            earlier = earlier_ref[at : at + owners, :]
            rank = jnp.sum(hits * (earlier + carry), axis=0, keepdims=True)
            live = lane + block * 256 < counts_ref[tile]
            rank = jnp.where(live, rank, -1.0).astype(i32)
            rank_ref[tile : tile + 1, block * 256 : block * 256 + 256] = rank
            carry = carry + earlier[:, 255:256] + hits[:, 255:256]
            ids = lists_ref[tile : tile + 1, block * 256 : block * 256 + 256]
            local = (ids & ((1 << shift) - 1)) + 1
            coarse = (local >> 7).astype(f32)
            fine = (local & 127).astype(f32)
            placed = jnp.concatenate([hits * coarse, hits * fine], axis=0).astype(bf16)
            at_rank = jnp.where(rank_rows == rank, 1.0, 0.0).astype(bf16)
            total = total + lax.dot_general(placed, at_rank, nt_dims, preferred_element_type=f32)
    requests = (total[:owners] * 128.0 + total[owners:]).astype(i32) - 1
    for owner in range(owners):
        requests_ref[owner] = requests[owner : owner + 1]


def lookup_kernel(asked_ref, table_ref, found_ref, *, group):
    askers, _, capacity = asked_ref.shape
    rows = table_ref.shape[0] // (2 * fields + 2)
    width = group * capacity
    low_rows = lax.broadcasted_iota(i32, (256, width), 0)
    high_rows = lax.broadcasted_iota(i32, (rows, width), 0)

    def step(part, carry):
        asked = jnp.concatenate([asked_ref[group * part + k] for k in range(group)], axis=1)
        pick = jnp.where(low_rows == (asked & 255), 1.0, 0.0).astype(bf16)
        mask = high_rows == (asked >> 8)
        result = jnp.dot(table_ref[...], pick, preferred_element_type=f32)
        for field in range(fields):
            values = result[field * rows : (field + 1) * rows]
            values = values + result[(fields + field) * rows : (fields + field + 1) * rows]
            if field < 2:
                at = (2 * fields + field) * rows
                values = values + result[at : at + rows]
            found = jnp.sum(jnp.where(mask, values, 0.0), axis=0, keepdims=True)
            for k in range(group):
                found_ref[group * part + k, :, field * capacity : (field + 1) * capacity] = found[
                    :, k * capacity : (k + 1) * capacity
                ]
        return carry

    lax.fori_loop(0, askers // group, step, 0)


def collect_kernel(camera_ref, asked_ref, returned_ref, sums_ref, total_ref, *, rows, group):
    askers, _, capacity = asked_ref.shape
    views = sums_ref.shape[0]
    width = group * capacity
    low_rows = lax.broadcasted_iota(i32, (256, width), 0)
    high_rows = lax.broadcasted_iota(i32, (rows, width), 0)
    total_ref[...] = jnp.zeros_like(total_ref)

    def step(part, carry):
        asked = jnp.concatenate([asked_ref[group * part + k] for k in range(group)], axis=1)
        pick = jnp.where(low_rows == (asked & 255), 1.0, 0.0).astype(bf16)
        mask = high_rows == (asked >> 8)
        uppers = []
        lowers = []
        for field in range(fields):
            values = jnp.concatenate(
                [
                    returned_ref[group * part + k, :, field * capacity : (field + 1) * capacity]
                    for k in range(group)
                ],
                axis=1,
            )
            upper = values.astype(bf16).astype(f32)
            uppers.append(jnp.where(mask, upper, 0.0).astype(bf16))
            lowers.append(jnp.where(mask, values - upper, 0.0).astype(bf16))
        placed = jnp.concatenate(uppers + lowers, axis=0)
        total_ref[...] += lax.dot_general(placed, pick, nt_dims, preferred_element_type=f32)
        return carry

    lax.fori_loop(0, askers // group, step, 0)
    part_rows = rows // views
    for view in range(views):
        for field in range(fields):
            at = field * rows + view * part_rows
            sums_ref[view, field * part_rows : (field + 1) * part_rows, :] = (
                total_ref[at : at + part_rows, :]
                + total_ref[fields * rows + at : fields * rows + at + part_rows, :]
            )
        for entry in range(8):
            at = fields * part_rows + entry
            sums_ref[view, at : at + 1, :] = jnp.full((1, 256), camera_ref[entry], f32)


def pull_kernel(place_ref, sums_ref, params_ref, grads_ref):
    views = sums_ref.shape[0]
    part_rows = params_ref.shape[1]
    channels = params_ref.shape[0]
    gauss_rows = [params_ref[channel] for channel in range(channels)]
    totals = None
    for view in range(views):
        at = fields * part_rows
        camera_row = [
            jnp.broadcast_to(sums_ref[view, at + entry : at + entry + 1, :], (part_rows, 256))
            for entry in range(5)
        ]
        _, pull = jax.vjp(lambda rows_in: project(rows_in, camera_row, 0.0, 0.0), gauss_rows)
        (one,) = pull(
            tuple(
                sums_ref[view, field * part_rows : (field + 1) * part_rows, :]
                for field in range(fields)
            )
        )
        totals = one if totals is None else [x + y for x, y in zip(totals, one)]
    for channel in range(channels):
        for row in range(part_rows):
            grads_ref[channel : channel + 1, row * 256 : row * 256 + 256] = totals[channel][
                row : row + 1
            ]


def monomial(index, pix_x, pix_y):
    pix_x = pix_x.astype(f32) - 7.5
    pix_y = pix_y.astype(f32) - 7.5
    values = jnp.where(index == 0, 1.0, 0.0)
    values = jnp.where(index == 1, pix_x, values)
    values = jnp.where(index == 2, pix_y, values)
    values = jnp.where(index == 3, pix_x * pix_x, values)
    values = jnp.where(index == 4, pix_x * pix_y, values)
    return jnp.where(index == 5, pix_y * pix_y, values)


def render_kernel(
    counts_ref,
    place_ref,
    lists_ref,
    rank_ref,
    fetched_ref,
    d_image_ref,
    image_ref,
    outgoing_ref,
    fetch_ref,
    value_ref,
    blend_ref,
    ratio_ref,
    color_grad_ref,
    placed_ref,
    at_rank_ref,
    outgo_ref,
    *,
    shift,
):
    tiles, slots = lists_ref.shape
    owners, _, width = fetched_ref.shape
    capacity = width // fields
    blocks = slots // 256
    pixels = d_image_ref.shape[2]
    for field in range(fields):
        values = fetched_ref[:, 0, field * capacity : (field + 1) * capacity]
        pieces = split_three(values)
        fetch_ref[field * owners : (field + 1) * owners, :] = pieces[0]
        fetch_ref[(fields + field) * owners : (fields + field + 1) * owners, :] = pieces[1]
        if field < 2:
            at = (2 * fields + field) * owners
            fetch_ref[at : at + owners, :] = pieces[2]
    outgo_ref[...] = jnp.zeros_like(outgo_ref)
    row_index = lax.broadcasted_iota(i32, (256, 256), 0)
    lane_index = lax.broadcasted_iota(i32, (256, 256), 1)
    before = (row_index < lane_index).astype(f32).astype(bf16)
    after = (row_index > lane_index).astype(f32).astype(bf16)
    pixel_row = lax.broadcasted_iota(i32, (pixels, 24), 0)
    monomials = monomial(
        lax.broadcasted_iota(i32, (pixels, 24), 1) & 7, pixel_row & 15, pixel_row >> 4
    ).astype(bf16)
    pixel_lane = lax.broadcasted_iota(i32, (16, pixels), 1)
    moments_of = monomial(
        lax.broadcasted_iota(i32, (16, pixels), 0), pixel_lane & 15, pixel_lane >> 4
    ).astype(bf16)
    rank_rows = lax.broadcasted_iota(i32, (capacity, 256), 0)
    owner_rows = lax.broadcasted_iota(i32, (owners, 256), 0)
    lane = lax.broadcasted_iota(i32, (1, 256), 1)
    center_v = place_ref[0].astype(f32) * 16.0 + 8.0

    def one_tile(tile, carry):
        live_count = counts_ref[tile]
        live_blocks = (live_count + 255) // 256
        center_u = tile.astype(f32) * 16.0 + 8.0
        d_rows = d_image_ref[tile]
        d_pieces = split_two(d_rows)
        d_upper, d_lower = d_pieces[0].astype(f32), d_pieces[1].astype(f32)
        zeros = jnp.zeros((4, pixels), f32)
        d_stack = jnp.concatenate([d_upper, d_lower, d_upper, d_lower, zeros], axis=0)
        d_columns = jnp.transpose(d_stack).astype(bf16)
        d_left = jnp.concatenate(
            [d_upper, d_lower, jnp.zeros((10, pixels), f32)], axis=0
        ).astype(bf16)

        def owner_and_rank(block):
            at = pl.multiple_of(block * 256, 256)
            owner = lists_ref[pl.ds(tile, 1), pl.ds(at, 256)] >> shift
            return owner, rank_ref[pl.ds(tile, 1), pl.ds(at, 256)]

        def forward(block, carried):
            earlier, picture = carried
            at = pl.multiple_of(block * 256, 256)
            owner, rank = owner_and_rank(block)
            live = rank >= 0
            at_rank = jnp.where(rank_rows == rank, 1.0, 0.0).astype(bf16)
            at_rank_ref[:, pl.ds(at, 256)] = at_rank
            fetched = jnp.dot(fetch_ref[...], at_rank, preferred_element_type=f32)
            mask = owner_rows == owner
            found = []
            for field in range(fields):
                values = fetched[field * owners : (field + 1) * owners]
                low = (fields + field) * owners
                values = values + fetched[low : low + owners]
                if field < 2:
                    low = (2 * fields + field) * owners
                    values = values + fetched[low : low + owners]
                found.append(jnp.sum(jnp.where(mask, values, 0.0), axis=0, keepdims=True))
            pos_u = found[0] - center_u
            pos_v = found[1] - center_v
            coef_a, coef_b, coef_c, log_opacity = found[2:6]
            log_opacity = jnp.where(live, log_opacity, -1.0e4)
            value_ref[0:1, pl.ds(at, 256)] = pos_u
            value_ref[1:2, pl.ds(at, 256)] = pos_v
            for field in range(2, 5):
                value_ref[field : field + 1, pl.ds(at, 256)] = found[field]
            slope_u = coef_a * pos_u * 2.0 + coef_b * pos_v
            slope_v = coef_c * pos_v * 2.0 + coef_b * pos_u
            constant = log_opacity + 0.5 * (slope_u * pos_u + slope_v * pos_v)
            blank = jnp.zeros((2, 256), f32)
            polynomial = jnp.concatenate(
                [constant, -slope_u, -slope_v, coef_a, coef_b, coef_c, blank], axis=0
            )
            pieces = [piece.astype(f32) for piece in split_three(polynomial)]
            exponent = jnp.dot(
                monomials,
                jnp.concatenate(pieces, axis=0).astype(bf16),
                preferred_element_type=f32,
            )
            alpha = jnp.exp2(exponent)
            keep = 1.0 - alpha
            log_keep = jnp.log2(keep)
            upper, lower = split_two(log_keep)
            within = jnp.dot(upper, before, preferred_element_type=f32) + jnp.dot(
                lower, before, preferred_element_type=f32
            )
            weight = jnp.exp2(within + earlier) * alpha
            earlier = earlier + within[:, 255:256] + log_keep[:, 255:256]
            colors = jnp.concatenate(found[6:9], axis=0)
            color_pieces = [piece.astype(f32) for piece in split_two(colors)]
            blank = jnp.zeros((4, 256), f32)
            color_rows = jnp.concatenate(
                [
                    color_pieces[0],
                    color_pieces[0],
                    color_pieces[1],
                    color_pieces[1],
                    blank,
                ],
                axis=0,
            ).astype(bf16)
            color_left = jnp.concatenate(
                [color_pieces[0], color_pieces[1], jnp.zeros((10, 256), f32)], axis=0
            ).astype(bf16)
            pull = jnp.dot(d_columns, color_rows, preferred_element_type=f32)
            blend_ref[:, pl.ds(at, 256)] = weight * pull
            ratio_ref[:, pl.ds(at, 256)] = alpha / keep
            upper, lower = split_two(weight)
            one = jnp.dot(d_left, upper, preferred_element_type=f32)
            two = jnp.dot(d_left, lower, preferred_element_type=f32)
            color_grad_ref[0:3, pl.ds(at, 256)] = one[0:3] + one[3:6] + two[0:3]
            one = lax.dot_general(color_left, upper, nt_dims, preferred_element_type=f32)
            two = lax.dot_general(color_left, lower, nt_dims, preferred_element_type=f32)
            picture = picture + one[0:3] + one[3:6] + two[0:3]
            return earlier, picture

        _, picture = lax.fori_loop(
            0,
            live_blocks,
            forward,
            (jnp.zeros((pixels, 1), f32), jnp.zeros((3, pixels), f32)),
        )
        image_ref[tile] = picture

        def backward(step, later):
            block = live_blocks - 1 - step
            at = pl.multiple_of(block * 256, 256)
            owner, rank = owner_and_rank(block)
            blend = blend_ref[:, pl.ds(at, 256)]
            upper, lower = split_two(blend)
            within = jnp.dot(upper, after, preferred_element_type=f32) + jnp.dot(
                lower, after, preferred_element_type=f32
            )
            gradient = blend - (within + later) * ratio_ref[:, pl.ds(at, 256)]
            later = later + within[:, 0:1] + blend[:, 0:1]
            pieces = split_three(gradient)
            moments = (
                jnp.dot(moments_of, pieces[0], preferred_element_type=f32)
                + jnp.dot(moments_of, pieces[1], preferred_element_type=f32)
                + jnp.dot(moments_of, pieces[2], preferred_element_type=f32)
            ) * ln_2
            plain, first_x, first_y = moments[0:1], moments[1:2], moments[2:3]
            pos_u = value_ref[0:1, pl.ds(at, 256)]
            pos_v = value_ref[1:2, pl.ds(at, 256)]
            coef_a = value_ref[2:3, pl.ds(at, 256)]
            coef_b = value_ref[3:4, pl.ds(at, 256)]
            coef_c = value_ref[4:5, pl.ds(at, 256)]
            from_u = first_x - pos_u * plain
            from_v = first_y - pos_v * plain
            outputs = [
                -2.0 * coef_a * from_u - coef_b * from_v,
                -2.0 * coef_c * from_v - coef_b * from_u,
                moments[3:4] - pos_u * (first_x + from_u),
                moments[4:5] - pos_v * first_x - pos_u * from_v,
                moments[5:6] - pos_v * (first_y + from_v),
                plain,
            ] + [color_grad_ref[k : k + 1, pl.ds(at, 256)] for k in range(3)]
            mask = owner_rows == jnp.where(rank >= 0, owner, -1)
            for field, values in enumerate(outputs):
                upper = values.astype(bf16).astype(f32)
                row = field * owners
                placed_ref[row : row + owners, pl.ds(at, 256)] = jnp.where(mask, upper, 0.0).astype(bf16)
                row = (fields + field) * owners
                placed_ref[row : row + owners, pl.ds(at, 256)] = jnp.where(
                    mask, values - upper, 0.0
                ).astype(bf16)
            return later

        lax.fori_loop(0, live_blocks, backward, jnp.zeros((pixels, 1), f32))

        def send(block, carried):
            at = pl.multiple_of(block * 256, 256)
            outgo_ref[...] += lax.dot_general(
                placed_ref[:, pl.ds(at, 256)],
                at_rank_ref[:, pl.ds(at, 256)],
                nt_dims,
                preferred_element_type=f32,
            )
            return carried

        return lax.fori_loop(0, live_blocks, send, carry)

    lax.fori_loop(0, tiles, one_tile, 0)
    for owner in range(owners):
        for field in range(fields):
            row = field * owners + owner
            low = fields * owners + row
            outgoing_ref[owner, :, field * capacity : (field + 1) * capacity] = (
                outgo_ref[row : row + 1, :] + outgo_ref[low : low + 1, :]
            )


def body(params, camera, tile_lists, tile_counts, d_image):
    owners = lax.axis_size("tiles")
    views = lax.axis_size("views")
    channels, shard_size = params.shape
    shift = shard_size.bit_length() - 1
    tiles, slots = tile_lists.shape[1:]
    pixels = d_image.shape[3]
    capacity = 3 * tiles * slots // (2 * owners)
    rows = shard_size // 256
    part_rows = rows // views
    center = jnp.array([tiles * 8.0, owners * 8.0, 0.0], f32)
    camera_row = jnp.concatenate([jnp.cos(camera[0, :1]), jnp.sin(camera[0, :1]), camera[0, 1:4], center])
    counts = tile_counts[0]
    lists = tile_lists[0]
    tile_row = lax.axis_index("tiles").astype(i32).reshape(1)
    view_here = lax.axis_index("views").astype(i32).reshape(1)
    smem = pl.BlockSpec(memory_space=pltpu.SMEM)
    vmem = pl.BlockSpec(memory_space=pltpu.VMEM)
    settings = pltpu.CompilerParams(vmem_limit_bytes=vmem_bytes)

    requests, rank = pl.pallas_call(
        functools.partial(bucket_kernel, owners=owners, capacity=capacity, shift=shift),
        out_shape=(
            jax.ShapeDtypeStruct((owners, 1, capacity), i32),
            jax.ShapeDtypeStruct((tiles, slots), i32),
        ),
        in_specs=[smem, vmem],
        out_specs=(vmem, vmem),
        scratch_shapes=[
            pltpu.VMEM((tiles * slots // 256 * owners, 256), bf16),
            pltpu.VMEM((tiles * slots // 256 * owners, 256), f32),
        ],
        compiler_params=settings,
        name="bucket",
    )(counts, lists)
    asked = lax.all_to_all(requests, "tiles", split_axis=0, concat_axis=0, tiled=True)
    dense_params = params.reshape(channels, rows, 256)
    table = pl.pallas_call(
        project_kernel,
        out_shape=jax.ShapeDtypeStruct(((2 * fields + 2) * rows, 256), bf16),
        in_specs=[smem, vmem],
        out_specs=vmem,
        compiler_params=settings,
        name="project",
    )(camera_row, dense_params)
    found = pl.pallas_call(
        functools.partial(lookup_kernel, group=4),
        out_shape=jax.ShapeDtypeStruct((owners, 1, fields * capacity), f32),
        in_specs=[vmem, vmem],
        out_specs=vmem,
        compiler_params=settings,
        name="lookup",
    )(asked, table)
    fetched = lax.all_to_all(found, "tiles", split_axis=0, concat_axis=0, tiled=True)
    picture, outgoing = pl.pallas_call(
        functools.partial(render_kernel, shift=shift),
        out_shape=(
            jax.ShapeDtypeStruct((tiles, 3, pixels), f32),
            jax.ShapeDtypeStruct((owners, 1, fields * capacity), f32),
        ),
        in_specs=[smem, smem, vmem, vmem, vmem, vmem],
        out_specs=(vmem, vmem),
        scratch_shapes=[
            pltpu.VMEM(((2 * fields + 2) * owners, capacity), bf16),
            pltpu.VMEM((8, slots), f32),
            pltpu.VMEM((pixels, slots), f32),
            pltpu.VMEM((pixels, slots), f32),
            pltpu.VMEM((8, slots), f32),
            pltpu.VMEM((2 * fields * owners, slots), bf16),
            pltpu.VMEM((capacity, slots), bf16),
            pltpu.VMEM((2 * fields * owners, capacity), f32),
        ],
        compiler_params=settings,
        name="render",
    )(counts, tile_row, lists, rank, fetched, d_image[0])
    returned = lax.all_to_all(outgoing, "tiles", split_axis=0, concat_axis=0, tiled=True)
    sums = pl.pallas_call(
        functools.partial(collect_kernel, rows=rows, group=2),
        out_shape=jax.ShapeDtypeStruct((views, fields * part_rows + 8, 256), f32),
        in_specs=[smem, vmem, vmem],
        out_specs=vmem,
        scratch_shapes=[pltpu.VMEM((2 * fields * rows, 256), f32)],
        compiler_params=settings,
        name="collect",
    )(camera_row, asked, returned)
    all_sums = lax.all_to_all(sums, "views", split_axis=0, concat_axis=0, tiled=True)
    grads = pl.pallas_call(
        pull_kernel,
        out_shape=jax.ShapeDtypeStruct((channels, part_rows * 256), f32),
        grid_spec=pltpu.PrefetchScalarGridSpec(
            num_scalar_prefetch=1,
            grid=(1,),
            in_specs=[
                pl.BlockSpec((views, fields * part_rows + 8, 256), lambda step, place: (0, 0, 0)),
                pl.BlockSpec((channels, part_rows, 256), lambda step, place: (0, place[0], 0)),
            ],
            out_specs=pl.BlockSpec((channels, part_rows * 256), lambda step, place: (0, 0)),
        ),
        compiler_params=settings,
        name="pull",
    )(view_here, all_sums, dense_params)
    return picture[None], grads


def solution(mesh):
    placed = (
        P(None, "tiles"),
        P("views", None),
        P("views", "tiles", None),
        P("views", "tiles"),
        P("views", "tiles", None, None),
    )
    return jax.shard_map(
        body,
        mesh=mesh,
        in_specs=placed,
        out_specs=(P("views", "tiles", None, None), P(None, ("tiles", "views"))),
        check_vma=False,
    )
```

time: 596 us -> 149 us (0.25); the launches traced: 587 us -> 148 us
  local copies, waits for them, and re-layouts: 260 us -> 7.72 us
  other arithmetic: 154 us -> 1.32 us
  Pallas kernels: 0 us -> 75.7 us
  waiting for transfers between devices: 82.9 us -> 17 us
  matrix products: 53.2 us -> 0 us
  blocking collectives: 0 us -> 24.2 us
  between operations: 17 us -> 2.12 us
    gather x5 -> x0, local copies, waits for them, and re-layouts: 128 us -> none  [the longest x2 49.6 us: body(): picked = table_rows[asked_ids]]
    scatter x3 -> x0, local copies, waits for them, and re-layouts: 95.8 us -> none  [the longest x1 34.8 us: body(): jnp.zeros((bucket_total + 1,), jnp.bool_).at[flat_dest].set(True)]
    scatter-add x1 -> x0, other arithmetic: 79.2 us -> none  [body(): owner_rows = jnp.zeros((shard_size, channels), jnp.float32).at[asked_ids....]
    pallas_call x0 -> x6, Pallas kernels: none -> 75.7 us  [the longest x1 49.9 us: body(): pl.pallas_call(functools.partial(render_kernel, shift=shift), out_shape=(...]
    dot_general x9 -> x0, matrix products: 53.2 us -> none  [the longest x3 34 us: render(): return jnp.einsum('pi,ci->cp', weight, compact[6:9], precision=highest)]
    reduce_scatter x1 -> x0, waiting for transfers between devices: 39.9 us -> none  [body(): lax.psum_scatter(owner_grads, 'views', scatter_dimension=1, tiled=True)]
    reduce_sum x6 -> x0, other arithmetic: 32.6 us -> none  [the longest x1 21.5 us: render(): compact[4][None, :] * delta_y * delta_y]
    all_to_all x0 -> x1, blocking collectives: none -> 24.2 us  [body(): lax.all_to_all(outgoing, 'tiles', split_axis=0, concat_axis=0, tiled=True)]
  transfers between devices with their start and end apart: 4 -> 3, of which waited for: 3 -> 2; matrix products, arithmetic and copies ran while one was open for 13% -> 5% of each run, Pallas kernels for 0% -> 2%
where the time goes in v1:
time: 149 us; the launch traced here: 148 us
  Pallas kernels  75.7 us (51%)
  blocking collectives  24.2 us (16%)
  starting transfers between devices  20.1 us (13%)
  waiting for transfers between devices  17 us (11%)
  local copies, waits for them, and re-layouts  7.72 us (5%)
  between operations  2.12 us (1%)
    pallas_call x1, Pallas kernels, body(): pl.pallas_call(functools.partial(render_kernel, shift=shift), out_shape=(...  49.9 us
    all_to_all x1, blocking collectives, body(): lax.all_to_all(outgoing, 'tiles', split_axis=0, concat_axis=0, tiled=True)  24.2 us
    all_to_all x1, waiting for transfers between devices, body(): lax.all_to_all(found, 'tiles', split_axis=0, concat_axis=0, tiled=True)  10.2 us
    pallas_call x1, Pallas kernels, body(): pl.pallas_call(functools.partial(collect_kernel, rows=rows, group=2), out...  8.96 us
    all_to_all x1, starting transfers between devices, body(): lax.all_to_all(requests, 'tiles', split_axis=0, concat_axis=0, tiled=True)  8.59 us
    all_to_all x1, starting transfers between devices, body(): lax.all_to_all(found, 'tiles', split_axis=0, concat_axis=0, tiled=True)  7.38 us
    pallas_call x1, Pallas kernels, body(): pl.pallas_call(functools.partial(lookup_kernel, group=4), out_shape=jax.S...  7.34 us
    all_to_all x1, waiting for transfers between devices, body(): lax.all_to_all(sums, 'views', split_axis=0, concat_axis=0, tiled=True)  6.87 us
  transfers between devices with their start and end apart: 3, of which 2 were waited for; matrix products, arithmetic and copies ran while one was open for 5% of the time, Pallas kernels for 2%

profile of v1, /device:TPU:1, one launch (start us, length us, event | category | flops | bytes accessed | tf_op | source)
XLA Modules:
  0.0 148.2 jit_solution(13328703661131810969)
XLA Ops:
  0.6 3.9 %bucket.1 = (s32[32,1,384]{2,1,0:T(1,128)}, s32[8,1024]{1,0:T(8,128)}) custom-call(s32[8]{0:T(128)} %bitcast.22, s32[8,1024]{1,0:T(8,128)} %bitcast.19), custom_call_target="tpu_custom_call" | custom-call | tf_op jit(solution)/shard_map/bucket/pallas_call | solution.py:563
  4.6 8.6 %all-to-all-start = ((s32[32,1,384]{2,1,0:T(1,128)}), s32[32,1,384]{2,1,0:T(1,128)S(1)}, u32[]{:S(2)}, u32[]{:S(2)}) async-start(s32[32,1,384]{2,1,0:T(1,128)} %get-tuple-element.7), calls=%async_computation | async-start | bytes 98304 | tf_op jit(solution)/shard_map/all_to_all | solution.py:578
  14.6 0.7 slice_bitcast_fusion
  15.3 1.3 pad_maximum_fusion.camera_ref
  16.7 2.2 %copy.10 = f32[8,8,32,256]{3,2,1,0:T(8,128)S(1)} copy(f32[8,8,32,256]{3,1,2,0:T(8,128)} %bitcast.17) | data formatting | bytes 4194304
  18.9 1.4 slice.9.params_ref
  20.3 0.0 copy-start.4
  20.3 2.7 %project.1.table_ref = bf16[640,256]{1,0:T(8,128)(2,1)} custom-call(f32[8]{0:T(128)} %pad_maximum_fusion.camera_ref, f32[59,32,256]{2,1,0:T(8,128)} %slice.9.params_ref), custom_call_target="tpu_custom_call" | custom-call | tf_op jit(solution)/shard_map/project/pallas_call | solution.py:580
  23.0 0.0 all-to-all-done.asked_ref
  23.0 0.0 copy-start.2
  23.0 0.6 copy-done.2
  23.6 7.3 %lookup.1 = f32[32,1,3456]{2,1,0:T(1,128)} custom-call(s32[32,1,384]{2,1,0:T(1,128)} %copy-done.2, bf16[640,256]{1,0:T(8,128)(2,1)} %project.1.table_ref), custom_call_target="tpu_custom_call" | custom-call | tf_op jit(solution)/shard_map/lookup/pallas_call | solution.py:588
  31.0 7.4 %all-to-all-start.1 = ((f32[32,1,3456]{2,1,0:T(1,128)}), f32[32,1,3456]{2,1,0:T(1,128)S(1)}, u32[]{:S(2)}, u32[]{:S(2)}) async-start(f32[32,1,3456]{2,1,0:T(1,128)} %lookup.1), calls=%async_computation.1 | async-start | bytes 884736 | tf_op jit(solution)/shard_map/all_to_all | solution.py:596
  38.4 0.0 copy-done.4
  38.4 0.6 copy.12
  39.0 10.2 %all-to-all-done.1.fetched_ref = f32[32,1,3456]{2,1,0:T(1,128)S(1)} async-done(((f32[32,1,3456]{2,1,0:T(1,128)}), f32[32,1,3456]{2,1,0:T(1,128)S(1)}, u32[]{:S(2)}, u32[]{:S(2)}) %all-to-all-start.1) | async-done | bytes 442400 | tf_op jit(solution)/shard_map/all_to_all | solution.py:596
  49.1 0.0 copy-start
  49.1 0.8 copy-done
  49.9 49.9 %render.1 = (f32[8,3,256]{2,1,0:T(4,128)}, f32[32,1,3456]{2,1,0:T(1,128)}) custom-call(s32[8]{0:T(128)} %bitcast.23, s32[1]{0:T(128)} %bitcast.1.place_ref, s32[8,1024]{1,0:T(8,128)} %bitcast.20, s32[8,1024]{1,0:T(8,128)} %get-tuple-element.6.rank_ref, f32[32,1,3456]{2,1,0:T(1,128)} %copy-done, f32[8,3,256]{2,1,0:T(4,128)} %bitcast.18), custom_call_target="tpu_custom_call" | custom-call | tf_op jit(solution)/shard_map/render/pallas_call | solution.py:597
  99.8 0.0 copy-start.3
  99.8 24.2 %all_to_all.20.returned_ref = f32[32,1,3456]{2,1,0:T(1,128)} all-to-all(f32[32,1,3456]{2,1,0:T(1,128)} %get-tuple-element.9), channel_id=1, replica_groups=mesh['tiles'=32,'views'=4] {'tiles'}, dimensions={0} | all-to-all | bytes 884736 | tf_op jit(solution)/shard_map/all_to_all | solution.py:618
  124.0 9.0 %collect.1 = f32[4,80,256]{2,1,0:T(8,128)} custom-call(f32[8]{0:T(128)} %pad_maximum_fusion.camera_ref, s32[32,1,384]{2,1,0:T(1,128)} %copy-done.2, f32[32,1,3456]{2,1,0:T(1,128)} %all_to_all.20.returned_ref), custom_call_target="tpu_custom_call" | custom-call | tf_op jit(solution)/shard_map/collect/pallas_call | solution.py:619
  133.0 4.1 %all-to-all-start.3 = ((f32[4,80,256]{2,1,0:T(8,128)}), f32[4,80,256]{2,1,0:T(8,128)S(1)}, u32[]{:S(2)}, u32[]{:S(2)}) async-start(f32[4,80,256]{2,1,0:T(8,128)} %collect.1), calls=%async_computation.3 | async-start | bytes 655360 | tf_op jit(solution)/shard_map/all_to_all | solution.py:628
  137.1 0.0 copy-done.3
  137.1 0.6 copy.9
  137.7 6.9 %all-to-all-done.3.sums_ref = f32[4,80,256]{2,1,0:T(8,128)S(1)} async-done(((f32[4,80,256]{2,1,0:T(8,128)}), f32[4,80,256]{2,1,0:T(8,128)S(1)}, u32[]{:S(2)}, u32[]{:S(2)}) %all-to-all-start.3) | async-done | bytes 327712 | tf_op jit(solution)/shard_map/all_to_all | solution.py:628
  144.6 0.0 copy-start.1
  144.6 0.7 copy-done.1
  145.3 2.9 %pull.1 = f32[59,2048]{1,0:T(8,128)} custom-call(s32[1]{0:T(128)} %bitcast.8.place_ref, f32[4,80,256]{2,1,0:T(8,128)} %copy-done.1, f32[59,32,256]{2,1,0:T(8,128)} %slice.9.params_ref), custom_call_target="tpu_custom_call" | custom-call | tf_op jit(solution)/shard_map/pull/pallas_call | solution.py:629
Async XLA Ops:
  4.6 18.4 %all-to-all-start = ((s32[32,1,384]{2,1,0:T(1,128)}), s32[32,1,384]{2,1,0:T(1,128)S(1)}, u32[]{:S(2)}, u32[]{:S(2)}) async-start(s32[32,1,384]{2,1,0:T(1,128)} %get-tuple-element.7), calls=%async_computation | async-start | bytes 98304 | tf_op jit(solution)/shard_map/all_to_all | solution.py:578
  20.3 18.1 %copy-start.4 = (f32[1,8,3,256]{3,1,2,0:T(8,128)S(1)}, f32[1,8,3,256]{3,1,2,0:T(8,128)}, u32[]{:S(2)}) copy-start(f32[1,8,3,256]{3,1,2,0:T(8,128)} %param.10) | copy-start | bytes 73732
  23.0 0.6 copy-start.2
  31.0 18.2 %all-to-all-start.1 = ((f32[32,1,3456]{2,1,0:T(1,128)}), f32[32,1,3456]{2,1,0:T(1,128)S(1)}, u32[]{:S(2)}, u32[]{:S(2)}) async-start(f32[32,1,3456]{2,1,0:T(1,128)} %lookup.1), calls=%async_computation.1 | async-start | bytes 884736 | tf_op jit(solution)/shard_map/all_to_all | solution.py:596
  49.1 0.8 copy-start
  99.8 37.3 %copy-start.3 = (f32[8,3,256]{2,1,0:T(4,128)S(1)}, f32[8,3,256]{2,1,0:T(4,128)}, u32[]{:S(2)}) copy-start(f32[8,3,256]{2,1,0:T(4,128)} %get-tuple-element.8) | copy-start | bytes 73732
  133.0 11.6 %all-to-all-start.3 = ((f32[4,80,256]{2,1,0:T(8,128)}), f32[4,80,256]{2,1,0:T(8,128)S(1)}, u32[]{:S(2)}, u32[]{:S(2)}) async-start(f32[4,80,256]{2,1,0:T(8,128)} %collect.1), calls=%async_computation.3 | async-start | bytes 655360 | tf_op jit(solution)/shard_map/all_to_all | solution.py:628
  144.6 0.7 copy-start.1

commit v2 on v1

--- a/solution.py
+++ b/solution.py
@@ -327,8 +327,18 @@
     d_image_ref,
     image_ref,
     outgoing_ref,
+    item_ref,
+    rows_ref,
     fetch_ref,
     value_ref,
+    polynomial_ref,
+    color_rows_ref,
+    color_left_ref,
+    d_columns_ref,
+    d_left_ref,
+    earlier_ref,
+    later_ref,
+    picture_ref,
     blend_ref,
     ratio_ref,
     color_grad_ref,
@@ -341,17 +351,46 @@
     tiles, slots = lists_ref.shape
     owners, _, width = fetched_ref.shape
     capacity = width // fields
-    blocks = slots // 256
+    spare = tiles * slots // 256
     pixels = d_image_ref.shape[2]
+
+    def list_tile(tile, base):
+        live_blocks = (counts_ref[tile] + 255) // 256
+
+        def list_block(block, carry):
+            item_ref[0, base + block] = tile
+            item_ref[1, base + block] = block
+            item_ref[2, base + block] = base + live_blocks - 1 - block
+            return carry
+
+        lax.fori_loop(0, live_blocks, list_block, 0)
+        return base + live_blocks
+
+    items = lax.fori_loop(0, tiles, list_tile, 0)
+    for owner in range(owners):
+        for field in range(fields):
+            row = field * owners + owner
+            rows_ref[row : row + 1, :] = fetched_ref[owner, :, field * capacity : (field + 1) * capacity]
+    center_v = place_ref[0].astype(f32) * 16.0 + 8.0
     for field in range(fields):
-        values = fetched_ref[:, 0, field * capacity : (field + 1) * capacity]
+        values = rows_ref[field * owners : (field + 1) * owners, :]
+        if field == 1:
+            values = values - center_v
         pieces = split_three(values)
         fetch_ref[field * owners : (field + 1) * owners, :] = pieces[0]
         fetch_ref[(fields + field) * owners : (fields + field + 1) * owners, :] = pieces[1]
         if field < 2:
             at = (2 * fields + field) * owners
             fetch_ref[at : at + owners, :] = pieces[2]
+    for tile in range(tiles):
+        d_rows = d_image_ref[tile]
+        d_upper, d_lower = [piece.astype(f32) for piece in split_two(d_rows)]
+        d_stack = jnp.concatenate([d_upper, d_lower, d_upper, d_lower, jnp.zeros((4, pixels), f32)], axis=0)
+        d_columns_ref[tile] = jnp.transpose(d_stack).astype(bf16)
+        d_left_ref[tile] = jnp.concatenate([d_upper, d_lower, jnp.zeros((10, pixels), f32)], axis=0).astype(bf16)
     outgo_ref[...] = jnp.zeros_like(outgo_ref)
+    placed_ref[spare] = jnp.zeros(placed_ref.shape[1:], bf16)
+    at_rank_ref[spare] = jnp.zeros(at_rank_ref.shape[1:], bf16)
     row_index = lax.broadcasted_iota(i32, (256, 256), 0)
     lane_index = lax.broadcasted_iota(i32, (256, 256), 1)
     before = (row_index < lane_index).astype(f32).astype(bf16)
@@ -366,171 +405,163 @@
     ).astype(bf16)
     rank_rows = lax.broadcasted_iota(i32, (capacity, 256), 0)
     owner_rows = lax.broadcasted_iota(i32, (owners, 256), 0)
-    lane = lax.broadcasted_iota(i32, (1, 256), 1)
-    center_v = place_ref[0].astype(f32) * 16.0 + 8.0
-
-    def one_tile(tile, carry):
-        live_count = counts_ref[tile]
-        live_blocks = (live_count + 255) // 256
-        center_u = tile.astype(f32) * 16.0 + 8.0
-        d_rows = d_image_ref[tile]
-        d_pieces = split_two(d_rows)
-        d_upper, d_lower = d_pieces[0].astype(f32), d_pieces[1].astype(f32)
-        zeros = jnp.zeros((4, pixels), f32)
-        d_stack = jnp.concatenate([d_upper, d_lower, d_upper, d_lower, zeros], axis=0)
-        d_columns = jnp.transpose(d_stack).astype(bf16)
-        d_left = jnp.concatenate(
-            [d_upper, d_lower, jnp.zeros((10, pixels), f32)], axis=0
+
+    def owner_and_rank(item):
+        tile = item_ref[0, item]
+        at = pl.multiple_of(item_ref[1, item] * 256, 256)
+        owner = lists_ref[pl.ds(tile, 1), pl.ds(at, 256)] >> shift
+        rank = rank_ref[pl.ds(tile, 1), pl.ds(at, 256)]
+        return owner, rank
+
+    def fetch(item):
+        owner, rank = owner_and_rank(item)
+        tile = item_ref[0, item]
+        at_rank = jnp.where(rank_rows == rank, 1.0, 0.0).astype(bf16)
+        at_rank_ref[item] = at_rank
+        fetched = jnp.dot(fetch_ref[...], at_rank, preferred_element_type=f32)
+        mask = owner_rows == owner
+        found = []
+        for field in range(fields):
+            values = fetched[field * owners : (field + 1) * owners]
+            low = (fields + field) * owners
+            values = values + fetched[low : low + owners]
+            if field < 2:
+                low = (2 * fields + field) * owners
+                values = values + fetched[low : low + owners]
+            found.append(jnp.sum(jnp.where(mask, values, 0.0), axis=0, keepdims=True))
+        pos_u = found[0] - (tile.astype(f32) * 16.0 + 8.0)
+        pos_v = found[1]
+        coef_a, coef_b, coef_c, log_opacity = found[2:6]
+        log_opacity = jnp.where(rank >= 0, log_opacity, -1.0e4)
+        slope_u = coef_a * pos_u * 2.0 + coef_b * pos_v
+        slope_v = coef_c * pos_v * 2.0 + coef_b * pos_u
+        constant = log_opacity + 0.5 * (slope_u * pos_u + slope_v * pos_v)
+        blank = jnp.zeros((3, 256), f32)
+        value_ref[item] = jnp.concatenate([pos_u, pos_v, coef_a, coef_b, coef_c, blank], axis=0)
+        polynomial = jnp.concatenate(
+            [constant, -slope_u, -slope_v, coef_a, coef_b, coef_c, blank[0:2]], axis=0
+        )
+        pieces = [piece.astype(f32) for piece in split_three(polynomial)]
+        polynomial_ref[item] = jnp.concatenate(pieces, axis=0).astype(bf16)
+        upper, lower = [piece.astype(f32) for piece in split_two(jnp.concatenate(found[6:9], axis=0))]
+        color_rows_ref[item] = jnp.concatenate(
+            [upper, upper, lower, lower, jnp.zeros((4, 256), f32)], axis=0
         ).astype(bf16)
-
-        def owner_and_rank(block):
-            at = pl.multiple_of(block * 256, 256)
-            owner = lists_ref[pl.ds(tile, 1), pl.ds(at, 256)] >> shift
-            return owner, rank_ref[pl.ds(tile, 1), pl.ds(at, 256)]
-
-        def forward(block, carried):
-            earlier, picture = carried
-            at = pl.multiple_of(block * 256, 256)
-            owner, rank = owner_and_rank(block)
-            live = rank >= 0
-            at_rank = jnp.where(rank_rows == rank, 1.0, 0.0).astype(bf16)
-            at_rank_ref[:, pl.ds(at, 256)] = at_rank
-            fetched = jnp.dot(fetch_ref[...], at_rank, preferred_element_type=f32)
-            mask = owner_rows == owner
-            found = []
-            for field in range(fields):
-                values = fetched[field * owners : (field + 1) * owners]
-                low = (fields + field) * owners
-                values = values + fetched[low : low + owners]
-                if field < 2:
-                    low = (2 * fields + field) * owners
-                    values = values + fetched[low : low + owners]
-                found.append(jnp.sum(jnp.where(mask, values, 0.0), axis=0, keepdims=True))
-            pos_u = found[0] - center_u
-            pos_v = found[1] - center_v
-            coef_a, coef_b, coef_c, log_opacity = found[2:6]
-            log_opacity = jnp.where(live, log_opacity, -1.0e4)
-            value_ref[0:1, pl.ds(at, 256)] = pos_u
-            value_ref[1:2, pl.ds(at, 256)] = pos_v
-            for field in range(2, 5):
-                value_ref[field : field + 1, pl.ds(at, 256)] = found[field]
-            slope_u = coef_a * pos_u * 2.0 + coef_b * pos_v
-            slope_v = coef_c * pos_v * 2.0 + coef_b * pos_u
-            constant = log_opacity + 0.5 * (slope_u * pos_u + slope_v * pos_v)
-            blank = jnp.zeros((2, 256), f32)
-            polynomial = jnp.concatenate(
-                [constant, -slope_u, -slope_v, coef_a, coef_b, coef_c, blank], axis=0
-            )
-            pieces = [piece.astype(f32) for piece in split_three(polynomial)]
-            exponent = jnp.dot(
-                monomials,
-                jnp.concatenate(pieces, axis=0).astype(bf16),
-                preferred_element_type=f32,
-            )
-            alpha = jnp.exp2(exponent)
-            keep = 1.0 - alpha
-            log_keep = jnp.log2(keep)
-            upper, lower = split_two(log_keep)
-            within = jnp.dot(upper, before, preferred_element_type=f32) + jnp.dot(
-                lower, before, preferred_element_type=f32
-            )
-            weight = jnp.exp2(within + earlier) * alpha
-            earlier = earlier + within[:, 255:256] + log_keep[:, 255:256]
-            colors = jnp.concatenate(found[6:9], axis=0)
-            color_pieces = [piece.astype(f32) for piece in split_two(colors)]
-            blank = jnp.zeros((4, 256), f32)
-            color_rows = jnp.concatenate(
-                [
-                    color_pieces[0],
-                    color_pieces[0],
-                    color_pieces[1],
-                    color_pieces[1],
-                    blank,
-                ],
-                axis=0,
-            ).astype(bf16)
-            color_left = jnp.concatenate(
-                [color_pieces[0], color_pieces[1], jnp.zeros((10, 256), f32)], axis=0
-            ).astype(bf16)
-            pull = jnp.dot(d_columns, color_rows, preferred_element_type=f32)
-            blend_ref[:, pl.ds(at, 256)] = weight * pull
-            ratio_ref[:, pl.ds(at, 256)] = alpha / keep
-            upper, lower = split_two(weight)
-            one = jnp.dot(d_left, upper, preferred_element_type=f32)
-            two = jnp.dot(d_left, lower, preferred_element_type=f32)
-            color_grad_ref[0:3, pl.ds(at, 256)] = one[0:3] + one[3:6] + two[0:3]
-            one = lax.dot_general(color_left, upper, nt_dims, preferred_element_type=f32)
-            two = lax.dot_general(color_left, lower, nt_dims, preferred_element_type=f32)
-            picture = picture + one[0:3] + one[3:6] + two[0:3]
-            return earlier, picture
-
-        _, picture = lax.fori_loop(
-            0,
-            live_blocks,
-            forward,
-            (jnp.zeros((pixels, 1), f32), jnp.zeros((3, pixels), f32)),
+        color_left_ref[item] = jnp.concatenate(
+            [upper, lower, jnp.zeros((10, 256), f32)], axis=0
+        ).astype(bf16)
+
+    def forward(item):
+        live = item >= 0
+        at = jnp.where(live, item, spare)
+        item = jnp.maximum(item, 0)
+        tile = item_ref[0, item]
+        first = item_ref[1, item] == 0
+        exponent = jnp.dot(monomials, polynomial_ref[at], preferred_element_type=f32)
+        earlier = jnp.where(first, 0.0, earlier_ref[...])
+        earlier = jnp.concatenate([earlier, earlier], axis=1)
+        alpha = jnp.exp2(exponent)
+        keep = 1.0 - alpha
+        log_keep = jnp.log2(keep)
+        upper, lower = split_two(log_keep)
+        within = jnp.dot(upper, before, preferred_element_type=f32) + jnp.dot(
+            lower, before, preferred_element_type=f32
         )
-        image_ref[tile] = picture
-
-        def backward(step, later):
-            block = live_blocks - 1 - step
-            at = pl.multiple_of(block * 256, 256)
-            owner, rank = owner_and_rank(block)
-            blend = blend_ref[:, pl.ds(at, 256)]
-            upper, lower = split_two(blend)
-            within = jnp.dot(upper, after, preferred_element_type=f32) + jnp.dot(
-                lower, after, preferred_element_type=f32
-            )
-            gradient = blend - (within + later) * ratio_ref[:, pl.ds(at, 256)]
-            later = later + within[:, 0:1] + blend[:, 0:1]
-            pieces = split_three(gradient)
-            moments = (
-                jnp.dot(moments_of, pieces[0], preferred_element_type=f32)
-                + jnp.dot(moments_of, pieces[1], preferred_element_type=f32)
-                + jnp.dot(moments_of, pieces[2], preferred_element_type=f32)
-            ) * ln_2
-            plain, first_x, first_y = moments[0:1], moments[1:2], moments[2:3]
-            pos_u = value_ref[0:1, pl.ds(at, 256)]
-            pos_v = value_ref[1:2, pl.ds(at, 256)]
-            coef_a = value_ref[2:3, pl.ds(at, 256)]
-            coef_b = value_ref[3:4, pl.ds(at, 256)]
-            coef_c = value_ref[4:5, pl.ds(at, 256)]
-            from_u = first_x - pos_u * plain
-            from_v = first_y - pos_v * plain
-            outputs = [
-                -2.0 * coef_a * from_u - coef_b * from_v,
-                -2.0 * coef_c * from_v - coef_b * from_u,
-                moments[3:4] - pos_u * (first_x + from_u),
-                moments[4:5] - pos_v * first_x - pos_u * from_v,
-                moments[5:6] - pos_v * (first_y + from_v),
-                plain,
-            ] + [color_grad_ref[k : k + 1, pl.ds(at, 256)] for k in range(3)]
-            mask = owner_rows == jnp.where(rank >= 0, owner, -1)
-            for field, values in enumerate(outputs):
-                upper = values.astype(bf16).astype(f32)
-                row = field * owners
-                placed_ref[row : row + owners, pl.ds(at, 256)] = jnp.where(mask, upper, 0.0).astype(bf16)
-                row = (fields + field) * owners
-                placed_ref[row : row + owners, pl.ds(at, 256)] = jnp.where(
-                    mask, values - upper, 0.0
-                ).astype(bf16)
-            return later
-
-        lax.fori_loop(0, live_blocks, backward, jnp.zeros((pixels, 1), f32))
-
-        def send(block, carried):
-            at = pl.multiple_of(block * 256, 256)
-            outgo_ref[...] += lax.dot_general(
-                placed_ref[:, pl.ds(at, 256)],
-                at_rank_ref[:, pl.ds(at, 256)],
-                nt_dims,
-                preferred_element_type=f32,
-            )
-            return carried
-
-        return lax.fori_loop(0, live_blocks, send, carry)
-
-    lax.fori_loop(0, tiles, one_tile, 0)
+        within = within + earlier
+        weight = jnp.exp2(within) * alpha
+        earlier_ref[...] = jnp.broadcast_to(within[:, 255:256] + log_keep[:, 255:256], (pixels, 128))
+        pull = jnp.dot(d_columns_ref[tile], color_rows_ref[at], preferred_element_type=f32)
+        blend_ref[at] = weight * pull
+        ratio_ref[at] = alpha / keep
+        upper, lower = split_two(weight)
+        d_left = d_left_ref[tile]
+        one = jnp.dot(d_left, upper, preferred_element_type=f32)
+        two = jnp.dot(d_left, lower, preferred_element_type=f32)
+        color_grad_ref[at, 0:3] = one[0:3] + one[3:6] + two[0:3]
+        color_left = color_left_ref[at]
+        one = lax.dot_general(color_left, upper, nt_dims, preferred_element_type=f32)
+        two = lax.dot_general(color_left, lower, nt_dims, preferred_element_type=f32)
+        picture = one[0:3] + one[3:6] + two[0:3]
+        at_tile = jnp.where(live, tile, tiles)
+        picture_ref[at_tile, 0:3] = jnp.where(first, 0.0, picture_ref[at_tile, 0:3]) + picture
+
+    def backward(step):
+        step = jnp.minimum(step, items)
+        live = step < items
+        at = jnp.where(live, item_ref[2, jnp.minimum(step, items - 1)], spare)
+        item = jnp.where(live, at, 0)
+        first = item_ref[1, jnp.minimum(step, items - 1)] == 0
+        owner, rank = owner_and_rank(item)
+        blend = blend_ref[at]
+        upper, lower = split_two(blend)
+        within = jnp.dot(upper, after, preferred_element_type=f32) + jnp.dot(
+            lower, after, preferred_element_type=f32
+        )
+        later = jnp.where(first, 0.0, later_ref[...])
+        within = within + jnp.concatenate([later, later], axis=1)
+        later_ref[...] = jnp.broadcast_to(within[:, 0:1] + blend[:, 0:1], (pixels, 128))
+        gradient = blend - within * ratio_ref[at]
+        pieces = split_two(gradient)
+        moments = (
+            jnp.dot(moments_of, pieces[0], preferred_element_type=f32)
+            + jnp.dot(moments_of, pieces[1], preferred_element_type=f32)
+        ) * ln_2
+        plain, first_x, first_y = moments[0:1], moments[1:2], moments[2:3]
+        pos_u, pos_v, coef_a, coef_b, coef_c = (value_ref[at, k : k + 1] for k in range(5))
+        from_u = first_x - pos_u * plain
+        from_v = first_y - pos_v * plain
+        outputs = [
+            -2.0 * coef_a * from_u - coef_b * from_v,
+            -2.0 * coef_c * from_v - coef_b * from_u,
+            moments[3:4] - pos_u * (first_x + from_u),
+            moments[4:5] - pos_v * first_x - pos_u * from_v,
+            moments[5:6] - pos_v * (first_y + from_v),
+            plain,
+        ] + [color_grad_ref[at, k : k + 1] for k in range(3)]
+        mask = owner_rows == jnp.where(rank >= 0, owner, -1)
+        for field, values in enumerate(outputs):
+            upper = values.astype(bf16).astype(f32)
+            row = field * owners
+            placed_ref[at, row : row + owners, :] = jnp.where(mask, upper, 0.0).astype(bf16)
+            row = (fields + field) * owners
+            placed_ref[at, row : row + owners, :] = jnp.where(mask, values - upper, 0.0).astype(bf16)
+
+    def send(item):
+        at = jnp.where(item < 0, spare, item)
+        outgo_ref[...] += lax.dot_general(
+            placed_ref[at], at_rank_ref[at], nt_dims, preferred_element_type=f32
+        )
+
+    def send_step(step):
+        send(jnp.where(step < 0, -1, item_ref[2, jnp.maximum(step, 0)]))
+
+    lag = 6
+
+    def ramp_up(step, carry):
+        forward(step - 1)
+        fetch(step)
+        return carry
+
+    def steady(step, carry):
+        send_step(step - lag - 1)
+        backward(step - lag)
+        forward(step - 1)
+        fetch(step)
+        return carry
+
+    def ramp_down(step, carry):
+        send_step(step - lag - 1)
+        backward(step - lag)
+        return carry
+
+    lax.fori_loop(0, lag, ramp_up, 0)
+    lax.fori_loop(lag, items, steady, 0)
+    send_step(items - lag - 1)
+    backward(items - lag)
+    forward(items - 1)
+    lax.fori_loop(items + 1, items + lag + 1, ramp_down, 0)
+    for tile in range(tiles):
+        image_ref[tile] = picture_ref[tile, 0:3]
     for owner in range(owners):
         for field in range(fields):
             row = field * owners + owner
@@ -538,6 +569,47 @@
             outgoing_ref[owner, :, field * capacity : (field + 1) * capacity] = (
                 outgo_ref[row : row + 1, :] + outgo_ref[low : low + 1, :]
             )
+
+
+def render_call(counts, tile_row, lists, rank, fetched, d_image, shift):
+    owners, _, width = fetched.shape
+    capacity = width // fields
+    tiles, slots = lists.shape
+    pixels = d_image.shape[2]
+    kept = tiles * slots // 256 + 1
+    smem = pl.BlockSpec(memory_space=pltpu.SMEM)
+    vmem = pl.BlockSpec(memory_space=pltpu.VMEM)
+    return pl.pallas_call(
+        functools.partial(render_kernel, shift=shift),
+        out_shape=(
+            jax.ShapeDtypeStruct((tiles, 3, pixels), f32),
+            jax.ShapeDtypeStruct((owners, 1, fields * capacity), f32),
+        ),
+        in_specs=[smem, smem, vmem, vmem, vmem, vmem],
+        out_specs=(vmem, vmem),
+        scratch_shapes=[
+            pltpu.SMEM((3, kept), i32),
+            pltpu.VMEM((fields * owners, capacity), f32),
+            pltpu.VMEM(((2 * fields + 2) * owners, capacity), bf16),
+            pltpu.VMEM((kept, 8, 256), f32),
+            pltpu.VMEM((kept, 24, 256), bf16),
+            pltpu.VMEM((kept, 16, 256), bf16),
+            pltpu.VMEM((kept, 16, 256), bf16),
+            pltpu.VMEM((tiles, pixels, 16), bf16),
+            pltpu.VMEM((tiles, 16, pixels), bf16),
+            pltpu.VMEM((pixels, 128), f32),
+            pltpu.VMEM((pixels, 128), f32),
+            pltpu.VMEM((tiles + 1, 8, pixels), f32),
+            pltpu.VMEM((kept, pixels, 256), f32),
+            pltpu.VMEM((kept, pixels, 256), f32),
+            pltpu.VMEM((kept, 8, 256), f32),
+            pltpu.VMEM((kept, 2 * fields * owners, 256), bf16),
+            pltpu.VMEM((kept, capacity, 256), bf16),
+            pltpu.VMEM((2 * fields * owners, capacity), f32),
+        ],
+        compiler_params=pltpu.CompilerParams(vmem_limit_bytes=vmem_bytes),
+        name="render",
+    )(counts, tile_row, lists, rank, fetched, d_image)
 
 
 def body(params, camera, tile_lists, tile_counts, d_image):
@@ -594,27 +666,7 @@
         name="lookup",
     )(asked, table)
     fetched = lax.all_to_all(found, "tiles", split_axis=0, concat_axis=0, tiled=True)
-    picture, outgoing = pl.pallas_call(
-        functools.partial(render_kernel, shift=shift),
-        out_shape=(
-            jax.ShapeDtypeStruct((tiles, 3, pixels), f32),
-            jax.ShapeDtypeStruct((owners, 1, fields * capacity), f32),
-        ),
-        in_specs=[smem, smem, vmem, vmem, vmem, vmem],
-        out_specs=(vmem, vmem),
-        scratch_shapes=[
-            pltpu.VMEM(((2 * fields + 2) * owners, capacity), bf16),
-            pltpu.VMEM((8, slots), f32),
-            pltpu.VMEM((pixels, slots), f32),
-            pltpu.VMEM((pixels, slots), f32),
-            pltpu.VMEM((8, slots), f32),
-            pltpu.VMEM((2 * fields * owners, slots), bf16),
-            pltpu.VMEM((capacity, slots), bf16),
-            pltpu.VMEM((2 * fields * owners, capacity), f32),
-        ],
-        compiler_params=settings,
-        name="render",
-    )(counts, tile_row, lists, rank, fetched, d_image[0])
+    picture, outgoing = render_call(counts, tile_row, lists, rank, fetched, d_image[0], shift)
     returned = lax.all_to_all(outgoing, "tiles", split_axis=0, concat_axis=0, tiled=True)
     sums = pl.pallas_call(
         functools.partial(collect_kernel, rows=rows, group=2),

time: 149 us -> 134 us (0.90)
  Pallas kernels: 75.7 us -> 63 us
  blocking collectives: 24.2 us -> 21 us
  starting transfers between devices: 20.1 us -> 21.6 us
    pallas_call x1, Pallas kernels: 49.9 us -> 37.2 us  [render_call(): pl.pallas_call(functools.partial(render_kernel, shift=shift), out_shape=(...]
    all_to_all x1, blocking collectives: 24.2 us -> 21 us  [body(): lax.all_to_all(outgoing, 'tiles', split_axis=0, concat_axis=0, tiled=True)]
    all_to_all x1, starting transfers between devices: 4.1 us -> 5.64 us  [body(): lax.all_to_all(sums, 'views', split_axis=0, concat_axis=0, tiled=True)]
where the time goes in v2:
time: 134 us
  Pallas kernels  63 us (47%)
  starting transfers between devices  21.6 us (16%)
  blocking collectives  21 us (16%)
  waiting for transfers between devices  17 us (13%)
  local copies, waits for them, and re-layouts  7.72 us (6%)
  between operations  2.12 us (2%)
    pallas_call x1, Pallas kernels, render_call(): pl.pallas_call(functools.partial(render_kernel, shift=shift), out_shape=(...  37.2 us
    all_to_all x1, blocking collectives, body(): lax.all_to_all(outgoing, 'tiles', split_axis=0, concat_axis=0, tiled=True)  21 us
    all_to_all x1, waiting for transfers between devices, body(): lax.all_to_all(found, 'tiles', split_axis=0, concat_axis=0, tiled=True)  10.2 us
    pallas_call x1, Pallas kernels, body(): pl.pallas_call(functools.partial(collect_kernel, rows=rows, group=2), out...  8.97 us
    all_to_all x1, starting transfers between devices, body(): lax.all_to_all(requests, 'tiles', split_axis=0, concat_axis=0, tiled=True)  8.59 us
    all_to_all x1, starting transfers between devices, body(): lax.all_to_all(found, 'tiles', split_axis=0, concat_axis=0, tiled=True)  7.38 us
    pallas_call x1, Pallas kernels, body(): pl.pallas_call(functools.partial(lookup_kernel, group=4), out_shape=jax.S...  7.34 us
    all_to_all x1, waiting for transfers between devices, body(): lax.all_to_all(sums, 'views', split_axis=0, concat_axis=0, tiled=True)  6.87 us
  transfers between devices with their start and end apart: 3, of which 2 were waited for; matrix products, arithmetic and copies ran while one was open for 5% of the time, Pallas kernels for 2%

profile of v2, /device:TPU:1, one launch (start us, length us, event | category | flops | bytes accessed | tf_op | source)
XLA Modules:
  0.0 133.9 jit_solution(11636692169207401478)
XLA Ops:
  0.6 3.9 %bucket.1 = (s32[32,1,384]{2,1,0:T(1,128)}, s32[8,1024]{1,0:T(8,128)}) custom-call(s32[8]{0:T(128)} %bitcast.22, s32[8,1024]{1,0:T(8,128)} %bitcast.19), custom_call_target="tpu_custom_call" | custom-call | tf_op jit(solution)/shard_map/bucket/pallas_call | solution.py:635
  4.6 8.6 %all-to-all-start = ((s32[32,1,384]{2,1,0:T(1,128)}), s32[32,1,384]{2,1,0:T(1,128)S(1)}, u32[]{:S(2)}, u32[]{:S(2)}) async-start(s32[32,1,384]{2,1,0:T(1,128)} %get-tuple-element.7), calls=%async_computation | async-start | bytes 98304 | tf_op jit(solution)/shard_map/all_to_all | solution.py:650
  14.6 0.7 slice_bitcast_fusion
  15.3 1.3 pad_maximum_fusion.camera_ref
  16.7 2.2 %copy.10 = f32[8,8,32,256]{3,2,1,0:T(8,128)S(1)} copy(f32[8,8,32,256]{3,1,2,0:T(8,128)} %bitcast.17) | data formatting | bytes 4194304
  18.9 1.4 %slice.9.params_ref = f32[59,32,256]{2,1,0:T(8,128)} slice(f32[64,32,256]{2,1,0:T(8,128)S(1)} %bitcast.16), slice={[0:59], [0:32], [0:256]} | slice | bytes 3866624 | tf_op jit(solution)/shard_map/reshape | solution.py:651
  20.3 0.0 copy-start.4
  20.3 2.7 %project.1.table_ref = bf16[640,256]{1,0:T(8,128)(2,1)} custom-call(f32[8]{0:T(128)} %pad_maximum_fusion.camera_ref, f32[59,32,256]{2,1,0:T(8,128)} %slice.9.params_ref), custom_call_target="tpu_custom_call" | custom-call | tf_op jit(solution)/shard_map/project/pallas_call | solution.py:652
  23.0 0.0 all-to-all-done.asked_ref
  23.0 0.0 copy-start.2
  23.0 0.6 copy-done.2
  23.6 7.3 %lookup.1 = f32[32,1,3456]{2,1,0:T(1,128)} custom-call(s32[32,1,384]{2,1,0:T(1,128)} %copy-done.2, bf16[640,256]{1,0:T(8,128)(2,1)} %project.1.table_ref), custom_call_target="tpu_custom_call" | custom-call | tf_op jit(solution)/shard_map/lookup/pallas_call | solution.py:660
  31.0 7.4 %all-to-all-start.1 = ((f32[32,1,3456]{2,1,0:T(1,128)}), f32[32,1,3456]{2,1,0:T(1,128)S(1)}, u32[]{:S(2)}, u32[]{:S(2)}) async-start(f32[32,1,3456]{2,1,0:T(1,128)} %lookup.1), calls=%async_computation.1 | async-start | bytes 884736 | tf_op jit(solution)/shard_map/all_to_all | solution.py:668
  38.4 0.0 copy-done.4
  38.4 0.6 copy.12
  39.0 10.2 %all-to-all-done.1.fetched_ref = f32[32,1,3456]{2,1,0:T(1,128)S(1)} async-done(((f32[32,1,3456]{2,1,0:T(1,128)}), f32[32,1,3456]{2,1,0:T(1,128)S(1)}, u32[]{:S(2)}, u32[]{:S(2)}) %all-to-all-start.1) | async-done | bytes 442400 | tf_op jit(solution)/shard_map/all_to_all | solution.py:668
  49.1 0.0 copy-start
  49.1 0.8 copy-done
  49.9 37.2 %render.1 = (f32[8,3,256]{2,1,0:T(4,128)}, f32[32,1,3456]{2,1,0:T(1,128)}) custom-call(s32[8]{0:T(128)} %bitcast.23, s32[1]{0:T(128)} %bitcast.1.place_ref, s32[8,1024]{1,0:T(8,128)} %bitcast.20, s32[8,1024]{1,0:T(8,128)} %get-tuple-element.6.rank_ref, f32[32,1,3456]{2,1,0:T(1,128)} %copy-done, f32[8,3,256]{2,1,0:T(4,128)} %bitcast.18), custom_call_target="tpu_custom_call" | custom-call | tf_op jit(solution)/shard_map/render/pallas_call | solution.py:582
  87.1 0.0 copy-start.3
  87.1 21.0 %all_to_all.20.returned_ref = f32[32,1,3456]{2,1,0:T(1,128)} all-to-all(f32[32,1,3456]{2,1,0:T(1,128)} %get-tuple-element.9), channel_id=1, replica_groups=mesh['tiles'=32,'views'=4] {'tiles'}, dimensions={0} | all-to-all | bytes 884736 | tf_op jit(solution)/shard_map/all_to_all | solution.py:670
  108.2 9.0 %collect.1 = f32[4,80,256]{2,1,0:T(8,128)} custom-call(f32[8]{0:T(128)} %pad_maximum_fusion.camera_ref, s32[32,1,384]{2,1,0:T(1,128)} %copy-done.2, f32[32,1,3456]{2,1,0:T(1,128)} %all_to_all.20.returned_ref), custom_call_target="tpu_custom_call" | custom-call | tf_op jit(solution)/shard_map/collect/pallas_call | solution.py:671
  117.1 5.6 %all-to-all-start.3 = ((f32[4,80,256]{2,1,0:T(8,128)}), f32[4,80,256]{2,1,0:T(8,128)S(1)}, u32[]{:S(2)}, u32[]{:S(2)}) async-start(f32[4,80,256]{2,1,0:T(8,128)} %collect.1), calls=%async_computation.3 | async-start | bytes 655360 | tf_op jit(solution)/shard_map/all_to_all | solution.py:680
  122.8 0.0 copy-done.3
  122.8 0.6 copy.9
  123.4 6.9 %all-to-all-done.3.sums_ref = f32[4,80,256]{2,1,0:T(8,128)S(1)} async-done(((f32[4,80,256]{2,1,0:T(8,128)}), f32[4,80,256]{2,1,0:T(8,128)S(1)}, u32[]{:S(2)}, u32[]{:S(2)}) %all-to-all-start.3) | async-done | bytes 327712 | tf_op jit(solution)/shard_map/all_to_all | solution.py:680
  130.3 0.0 copy-start.1
  130.3 0.7 copy-done.1
  131.0 2.9 %pull.1 = f32[59,2048]{1,0:T(8,128)} custom-call(s32[1]{0:T(128)} %bitcast.8.place_ref, f32[4,80,256]{2,1,0:T(8,128)} %copy-done.1, f32[59,32,256]{2,1,0:T(8,128)} %slice.9.params_ref), custom_call_target="tpu_custom_call" | custom-call | tf_op jit(solution)/shard_map/pull/pallas_call | solution.py:681
Async XLA Ops:
  4.6 18.4 %all-to-all-start = ((s32[32,1,384]{2,1,0:T(1,128)}), s32[32,1,384]{2,1,0:T(1,128)S(1)}, u32[]{:S(2)}, u32[]{:S(2)}) async-start(s32[32,1,384]{2,1,0:T(1,128)} %get-tuple-element.7), calls=%async_computation | async-start | bytes 98304 | tf_op jit(solution)/shard_map/all_to_all | solution.py:650
  20.3 18.1 %copy-start.4 = (f32[1,8,3,256]{3,1,2,0:T(8,128)S(1)}, f32[1,8,3,256]{3,1,2,0:T(8,128)}, u32[]{:S(2)}) copy-start(f32[1,8,3,256]{3,1,2,0:T(8,128)} %param.10) | copy-start | bytes 73732
  23.0 0.6 copy-start.2
  31.0 18.2 %all-to-all-start.1 = ((f32[32,1,3456]{2,1,0:T(1,128)}), f32[32,1,3456]{2,1,0:T(1,128)S(1)}, u32[]{:S(2)}, u32[]{:S(2)}) async-start(f32[32,1,3456]{2,1,0:T(1,128)} %lookup.1), calls=%async_computation.1 | async-start | bytes 884736 | tf_op jit(solution)/shard_map/all_to_all | solution.py:668
  49.1 0.8 copy-start
  87.1 35.6 %copy-start.3 = (f32[8,3,256]{2,1,0:T(4,128)S(1)}, f32[8,3,256]{2,1,0:T(4,128)}, u32[]{:S(2)}) copy-start(f32[8,3,256]{2,1,0:T(4,128)} %get-tuple-element.8) | copy-start | bytes 73732
  117.1 13.1 %all-to-all-start.3 = ((f32[4,80,256]{2,1,0:T(8,128)}), f32[4,80,256]{2,1,0:T(8,128)S(1)}, u32[]{:S(2)}, u32[]{:S(2)}) async-start(f32[4,80,256]{2,1,0:T(8,128)} %collect.1), calls=%async_computation.3 | async-start | bytes 655360 | tf_op jit(solution)/shard_map/all_to_all | solution.py:680
  130.3 0.7 copy-start.1

commit v3 on v2

--- a/solution.py
+++ b/solution.py
@@ -34,7 +34,7 @@
 log2_e = 1.0 / math.log(2.0)
 ln_2 = math.log(2.0)
 nt_dims = (((1,), (1,)), ((), ()))
-vmem_bytes = 56 * 1024 * 1024
+render_vmem_bytes = 48 * 1024 * 1024
 fields = 9
 
 
@@ -149,24 +149,31 @@
     return (pos_u, pos_v, coef_a, coef_b, coef_c, log_opacity, *colors)
 
 
-def project_kernel(camera_ref, params_ref, table_ref):
-    rows = params_ref.shape[1]
+def project_kernel(camera_ref, place_ref, params_ref, table_ref, third_ref, part_ref, dense_ref):
+    channels, rows, _ = dense_ref.shape
+    part_rows = part_ref.shape[1]
     camera_row = [camera_ref[entry] for entry in range(5)]
     center_x, center_y = camera_ref[5], camera_ref[6]
+    for channel in range(channels):
+        for row in range(rows):
+            dense_ref[channel, row : row + 1, :] = params_ref[channel : channel + 1, row * 256 : row * 256 + 256]
 
     def step(part, carry):
         at = pl.multiple_of(part * 16, 16)
-        gauss_rows = [params_ref[channel, pl.ds(at, 16), :] for channel in range(params_ref.shape[0])]
+        gauss_rows = [dense_ref[channel, pl.ds(at, 16), :] for channel in range(channels)]
         outputs = project(gauss_rows, camera_row, center_x, center_y)
         for field, values in enumerate(outputs):
             pieces = split_three(values)
-            table_ref[pl.ds(field * rows + at, 16), :] = pieces[0]
-            table_ref[pl.ds((fields + field) * rows + at, 16), :] = pieces[1]
+            table_ref[pl.ds(field * rows + at, 16), :256] = pieces[0]
+            table_ref[pl.ds(field * rows + at, 16), 256:] = pieces[1]
             if field < 2:
-                table_ref[pl.ds((2 * fields + field) * rows + at, 16), :] = pieces[2]
+                third_ref[pl.ds(field * rows + at, 16), :] = pieces[2]
         return carry
 
     lax.fori_loop(0, rows // 16, step, 0)
+    at = pl.multiple_of(place_ref[0] * part_rows, part_rows)
+    for channel in range(channels):
+        part_ref[channel] = dense_ref[channel, pl.ds(at, part_rows), :]
 
 
 def bucket_kernel(counts_ref, lists_ref, requests_ref, rank_ref, hits_ref, earlier_ref, *, owners, capacity, shift):
@@ -209,9 +216,9 @@
         requests_ref[owner] = requests[owner : owner + 1]
 
 
-def lookup_kernel(asked_ref, table_ref, found_ref, *, group):
+def lookup_kernel(asked_ref, table_ref, third_ref, found_ref, *, group):
     askers, _, capacity = asked_ref.shape
-    rows = table_ref.shape[0] // (2 * fields + 2)
+    rows = table_ref.shape[0] // fields
     width = group * capacity
     low_rows = lax.broadcasted_iota(i32, (256, width), 0)
     high_rows = lax.broadcasted_iota(i32, (rows, width), 0)
@@ -220,13 +227,14 @@
         asked = jnp.concatenate([asked_ref[group * part + k] for k in range(group)], axis=1)
         pick = jnp.where(low_rows == (asked & 255), 1.0, 0.0).astype(bf16)
         mask = high_rows == (asked >> 8)
-        result = jnp.dot(table_ref[...], pick, preferred_element_type=f32)
+        result = jnp.dot(
+            table_ref[...], jnp.concatenate([pick, pick], axis=0), preferred_element_type=f32
+        )
+        third = jnp.dot(third_ref[...], pick, preferred_element_type=f32)
         for field in range(fields):
             values = result[field * rows : (field + 1) * rows]
-            values = values + result[(fields + field) * rows : (fields + field + 1) * rows]
             if field < 2:
-                at = (2 * fields + field) * rows
-                values = values + result[at : at + rows]
+                values = values + third[field * rows : (field + 1) * rows]
             found = jnp.sum(jnp.where(mask, values, 0.0), axis=0, keepdims=True)
             for k in range(group):
                 found_ref[group * part + k, :, field * capacity : (field + 1) * capacity] = found[
@@ -237,9 +245,10 @@
     lax.fori_loop(0, askers // group, step, 0)
 
 
-def collect_kernel(camera_ref, asked_ref, returned_ref, sums_ref, total_ref, *, rows, group):
+def collect_kernel(camera_ref, place_ref, asked_ref, returned_ref, *rest, rows, group):
+    *sums_refs, total_ref = rest
     askers, _, capacity = asked_ref.shape
-    views = sums_ref.shape[0]
+    views = len(sums_refs)
     width = group * capacity
     low_rows = lax.broadcasted_iota(i32, (256, width), 0)
     high_rows = lax.broadcasted_iota(i32, (rows, width), 0)
@@ -262,40 +271,41 @@
             upper = values.astype(bf16).astype(f32)
             uppers.append(jnp.where(mask, upper, 0.0).astype(bf16))
             lowers.append(jnp.where(mask, values - upper, 0.0).astype(bf16))
-        placed = jnp.concatenate(uppers + lowers, axis=0)
-        total_ref[...] += lax.dot_general(placed, pick, nt_dims, preferred_element_type=f32)
+        placed = jnp.concatenate(
+            [jnp.concatenate(uppers, axis=0), jnp.concatenate(lowers, axis=0)], axis=1
+        )
+        total_ref[...] += lax.dot_general(
+            placed, jnp.concatenate([pick, pick], axis=1), nt_dims, preferred_element_type=f32
+        )
         return carry
 
     lax.fori_loop(0, askers // group, step, 0)
     part_rows = rows // views
-    for view in range(views):
+    for offset, sums_ref in enumerate(sums_refs):
+        view = lax.rem(place_ref[0] + offset, views)
         for field in range(fields):
-            at = field * rows + view * part_rows
-            sums_ref[view, field * part_rows : (field + 1) * part_rows, :] = (
-                total_ref[at : at + part_rows, :]
-                + total_ref[fields * rows + at : fields * rows + at + part_rows, :]
-            )
+            at = pl.multiple_of(field * rows + view * part_rows, part_rows)
+            sums_ref[field * part_rows : (field + 1) * part_rows, :] = total_ref[pl.ds(at, part_rows), :]
         for entry in range(8):
             at = fields * part_rows + entry
-            sums_ref[view, at : at + 1, :] = jnp.full((1, 256), camera_ref[entry], f32)
-
-
-def pull_kernel(place_ref, sums_ref, params_ref, grads_ref):
-    views = sums_ref.shape[0]
-    part_rows = params_ref.shape[1]
-    channels = params_ref.shape[0]
+            sums_ref[at : at + 1, :] = jnp.full((1, 256), camera_ref[entry], f32)
+
+
+def pull_kernel(*refs):
+    *sums_refs, params_ref, grads_ref = refs
+    channels, part_rows, _ = params_ref.shape
     gauss_rows = [params_ref[channel] for channel in range(channels)]
     totals = None
-    for view in range(views):
+    for sums_ref in sums_refs:
         at = fields * part_rows
         camera_row = [
-            jnp.broadcast_to(sums_ref[view, at + entry : at + entry + 1, :], (part_rows, 256))
+            jnp.broadcast_to(sums_ref[at + entry : at + entry + 1, :], (part_rows, 256))
             for entry in range(5)
         ]
         _, pull = jax.vjp(lambda rows_in: project(rows_in, camera_row, 0.0, 0.0), gauss_rows)
         (one,) = pull(
             tuple(
-                sums_ref[view, field * part_rows : (field + 1) * part_rows, :]
+                sums_ref[field * part_rows : (field + 1) * part_rows, :]
                 for field in range(fields)
             )
         )
@@ -376,12 +386,9 @@
         values = rows_ref[field * owners : (field + 1) * owners, :]
         if field == 1:
             values = values - center_v
-        pieces = split_three(values)
-        fetch_ref[field * owners : (field + 1) * owners, :] = pieces[0]
-        fetch_ref[(fields + field) * owners : (fields + field + 1) * owners, :] = pieces[1]
-        if field < 2:
-            at = (2 * fields + field) * owners
-            fetch_ref[at : at + owners, :] = pieces[2]
+        upper, lower = split_two(values)
+        fetch_ref[field * owners : (field + 1) * owners, :capacity] = upper
+        fetch_ref[field * owners : (field + 1) * owners, capacity:] = lower
     for tile in range(tiles):
         d_rows = d_image_ref[tile]
         d_upper, d_lower = [piece.astype(f32) for piece in split_two(d_rows)]
@@ -418,16 +425,15 @@
         tile = item_ref[0, item]
         at_rank = jnp.where(rank_rows == rank, 1.0, 0.0).astype(bf16)
         at_rank_ref[item] = at_rank
-        fetched = jnp.dot(fetch_ref[...], at_rank, preferred_element_type=f32)
+        yield
+        fetched = jnp.dot(
+            fetch_ref[...], jnp.concatenate([at_rank, at_rank], axis=0), preferred_element_type=f32
+        )
+        yield
         mask = owner_rows == owner
         found = []
         for field in range(fields):
             values = fetched[field * owners : (field + 1) * owners]
-            low = (fields + field) * owners
-            values = values + fetched[low : low + owners]
-            if field < 2:
-                low = (2 * fields + field) * owners
-                values = values + fetched[low : low + owners]
             found.append(jnp.sum(jnp.where(mask, values, 0.0), axis=0, keepdims=True))
         pos_u = found[0] - (tile.astype(f32) * 16.0 + 8.0)
         pos_v = found[1]
@@ -450,6 +456,7 @@
         color_left_ref[item] = jnp.concatenate(
             [upper, lower, jnp.zeros((10, 256), f32)], axis=0
         ).astype(bf16)
+        yield
 
     def forward(item):
         live = item >= 0
@@ -458,22 +465,26 @@
         tile = item_ref[0, item]
         first = item_ref[1, item] == 0
         exponent = jnp.dot(monomials, polynomial_ref[at], preferred_element_type=f32)
+        yield
         earlier = jnp.where(first, 0.0, earlier_ref[...])
         earlier = jnp.concatenate([earlier, earlier], axis=1)
         alpha = jnp.exp2(exponent)
         keep = 1.0 - alpha
         log_keep = jnp.log2(keep)
         upper, lower = split_two(log_keep)
+        yield
         within = jnp.dot(upper, before, preferred_element_type=f32) + jnp.dot(
             lower, before, preferred_element_type=f32
         )
+        pull = jnp.dot(d_columns_ref[tile], color_rows_ref[at], preferred_element_type=f32)
+        yield
         within = within + earlier
         weight = jnp.exp2(within) * alpha
         earlier_ref[...] = jnp.broadcast_to(within[:, 255:256] + log_keep[:, 255:256], (pixels, 128))
-        pull = jnp.dot(d_columns_ref[tile], color_rows_ref[at], preferred_element_type=f32)
         blend_ref[at] = weight * pull
         ratio_ref[at] = alpha / keep
         upper, lower = split_two(weight)
+        yield
         d_left = d_left_ref[tile]
         one = jnp.dot(d_left, upper, preferred_element_type=f32)
         two = jnp.dot(d_left, lower, preferred_element_type=f32)
@@ -484,6 +495,7 @@
         picture = one[0:3] + one[3:6] + two[0:3]
         at_tile = jnp.where(live, tile, tiles)
         picture_ref[at_tile, 0:3] = jnp.where(first, 0.0, picture_ref[at_tile, 0:3]) + picture
+        yield
 
     def backward(step):
         step = jnp.minimum(step, items)
@@ -497,15 +509,18 @@
         within = jnp.dot(upper, after, preferred_element_type=f32) + jnp.dot(
             lower, after, preferred_element_type=f32
         )
+        yield
         later = jnp.where(first, 0.0, later_ref[...])
         within = within + jnp.concatenate([later, later], axis=1)
         later_ref[...] = jnp.broadcast_to(within[:, 0:1] + blend[:, 0:1], (pixels, 128))
         gradient = blend - within * ratio_ref[at]
         pieces = split_two(gradient)
+        yield
         moments = (
             jnp.dot(moments_of, pieces[0], preferred_element_type=f32)
             + jnp.dot(moments_of, pieces[1], preferred_element_type=f32)
         ) * ln_2
+        yield
         plain, first_x, first_y = moments[0:1], moments[1:2], moments[2:3]
         pos_u, pos_v, coef_a, coef_b, coef_c = (value_ref[at, k : k + 1] for k in range(5))
         from_u = first_x - pos_u * plain
@@ -522,53 +537,60 @@
         for field, values in enumerate(outputs):
             upper = values.astype(bf16).astype(f32)
             row = field * owners
-            placed_ref[at, row : row + owners, :] = jnp.where(mask, upper, 0.0).astype(bf16)
-            row = (fields + field) * owners
-            placed_ref[at, row : row + owners, :] = jnp.where(mask, values - upper, 0.0).astype(bf16)
+            placed_ref[at, row : row + owners, :256] = jnp.where(mask, upper, 0.0).astype(bf16)
+            placed_ref[at, row : row + owners, 256:] = jnp.where(mask, values - upper, 0.0).astype(bf16)
+        yield
 
     def send(item):
         at = jnp.where(item < 0, spare, item)
         outgo_ref[...] += lax.dot_general(
-            placed_ref[at], at_rank_ref[at], nt_dims, preferred_element_type=f32
-        )
+            placed_ref[at],
+            jnp.concatenate([at_rank_ref[at], at_rank_ref[at]], axis=1),
+            nt_dims,
+            preferred_element_type=f32,
+        )
+        yield
 
     def send_step(step):
-        send(jnp.where(step < 0, -1, item_ref[2, jnp.maximum(step, 0)]))
+        return send(jnp.where(step < 0, -1, item_ref[2, jnp.maximum(step, 0)]))
 
     lag = 6
 
+    def run(order, **stages):
+        for name in order:
+            next(stages[name])
+        for left in stages.values():
+            for _ in left:
+                raise ValueError(order)
+
     def ramp_up(step, carry):
-        forward(step - 1)
-        fetch(step)
+        run("mmmmmfff", m=forward(step - 1), f=fetch(step))
         return carry
 
     def steady(step, carry):
-        send_step(step - lag - 1)
-        backward(step - lag)
-        forward(step - 1)
-        fetch(step)
+        run(
+            "mbsmfmbfmbmbf",
+            s=send_step(step - lag - 1),
+            b=backward(step - lag),
+            m=forward(step - 1),
+            f=fetch(step),
+        )
         return carry
 
     def ramp_down(step, carry):
-        send_step(step - lag - 1)
-        backward(step - lag)
+        run("sbbbb", s=send_step(step - lag - 1), b=backward(step - lag))
         return carry
 
     lax.fori_loop(0, lag, ramp_up, 0)
     lax.fori_loop(lag, items, steady, 0)
-    send_step(items - lag - 1)
-    backward(items - lag)
-    forward(items - 1)
+    run("sbbbbmmmmm", s=send_step(items - lag - 1), b=backward(items - lag), m=forward(items - 1))
     lax.fori_loop(items + 1, items + lag + 1, ramp_down, 0)
     for tile in range(tiles):
         image_ref[tile] = picture_ref[tile, 0:3]
     for owner in range(owners):
         for field in range(fields):
             row = field * owners + owner
-            low = fields * owners + row
-            outgoing_ref[owner, :, field * capacity : (field + 1) * capacity] = (
-                outgo_ref[row : row + 1, :] + outgo_ref[low : low + 1, :]
-            )
+            outgoing_ref[owner, :, field * capacity : (field + 1) * capacity] = outgo_ref[row : row + 1, :]
 
 
 def render_call(counts, tile_row, lists, rank, fetched, d_image, shift):
@@ -590,7 +612,7 @@
         scratch_shapes=[
             pltpu.SMEM((3, kept), i32),
             pltpu.VMEM((fields * owners, capacity), f32),
-            pltpu.VMEM(((2 * fields + 2) * owners, capacity), bf16),
+            pltpu.VMEM((fields * owners, 2 * capacity), bf16),
             pltpu.VMEM((kept, 8, 256), f32),
             pltpu.VMEM((kept, 24, 256), bf16),
             pltpu.VMEM((kept, 16, 256), bf16),
@@ -603,11 +625,11 @@
             pltpu.VMEM((kept, pixels, 256), f32),
             pltpu.VMEM((kept, pixels, 256), f32),
             pltpu.VMEM((kept, 8, 256), f32),
-            pltpu.VMEM((kept, 2 * fields * owners, 256), bf16),
+            pltpu.VMEM((kept, fields * owners, 512), bf16),
             pltpu.VMEM((kept, capacity, 256), bf16),
-            pltpu.VMEM((2 * fields * owners, capacity), f32),
+            pltpu.VMEM((fields * owners, capacity), f32),
         ],
-        compiler_params=pltpu.CompilerParams(vmem_limit_bytes=vmem_bytes),
+        compiler_params=pltpu.CompilerParams(vmem_limit_bytes=render_vmem_bytes),
         name="render",
     )(counts, tile_row, lists, rank, fetched, d_image)
 
@@ -630,7 +652,9 @@
     view_here = lax.axis_index("views").astype(i32).reshape(1)
     smem = pl.BlockSpec(memory_space=pltpu.SMEM)
     vmem = pl.BlockSpec(memory_space=pltpu.VMEM)
-    settings = pltpu.CompilerParams(vmem_limit_bytes=vmem_bytes)
+
+    def settings(mebibytes):
+        return pltpu.CompilerParams(vmem_limit_bytes=mebibytes * 1024 * 1024)
 
     requests, rank = pl.pallas_call(
         functools.partial(bucket_kernel, owners=owners, capacity=capacity, shift=shift),
@@ -644,55 +668,55 @@
             pltpu.VMEM((tiles * slots // 256 * owners, 256), bf16),
             pltpu.VMEM((tiles * slots // 256 * owners, 256), f32),
         ],
-        compiler_params=settings,
+        compiler_params=settings(16),
         name="bucket",
     )(counts, lists)
     asked = lax.all_to_all(requests, "tiles", split_axis=0, concat_axis=0, tiled=True)
-    dense_params = params.reshape(channels, rows, 256)
-    table = pl.pallas_call(
+    table, third, part_params = pl.pallas_call(
         project_kernel,
-        out_shape=jax.ShapeDtypeStruct(((2 * fields + 2) * rows, 256), bf16),
-        in_specs=[smem, vmem],
-        out_specs=vmem,
-        compiler_params=settings,
+        out_shape=(
+            jax.ShapeDtypeStruct((fields * rows, 512), bf16),
+            jax.ShapeDtypeStruct((2 * rows, 256), bf16),
+            jax.ShapeDtypeStruct((channels, part_rows, 256), f32),
+        ),
+        in_specs=[smem, smem, vmem],
+        out_specs=(vmem, vmem, vmem),
+        scratch_shapes=[pltpu.VMEM((channels, rows, 256), f32)],
+        compiler_params=settings(16),
         name="project",
-    )(camera_row, dense_params)
+    )(camera_row, view_here, params)
     found = pl.pallas_call(
         functools.partial(lookup_kernel, group=4),
         out_shape=jax.ShapeDtypeStruct((owners, 1, fields * capacity), f32),
-        in_specs=[vmem, vmem],
+        in_specs=[vmem, vmem, vmem],
         out_specs=vmem,
-        compiler_params=settings,
+        compiler_params=settings(16),
         name="lookup",
-    )(asked, table)
+    )(asked, table, third)
     fetched = lax.all_to_all(found, "tiles", split_axis=0, concat_axis=0, tiled=True)
     picture, outgoing = render_call(counts, tile_row, lists, rank, fetched, d_image[0], shift)
     returned = lax.all_to_all(outgoing, "tiles", split_axis=0, concat_axis=0, tiled=True)
     sums = pl.pallas_call(
         functools.partial(collect_kernel, rows=rows, group=2),
-        out_shape=jax.ShapeDtypeStruct((views, fields * part_rows + 8, 256), f32),
-        in_specs=[smem, vmem, vmem],
-        out_specs=vmem,
-        scratch_shapes=[pltpu.VMEM((2 * fields * rows, 256), f32)],
-        compiler_params=settings,
+        out_shape=[jax.ShapeDtypeStruct((fields * part_rows + 8, 256), f32)] * views,
+        in_specs=[smem, smem, vmem, vmem],
+        out_specs=[vmem] * views,
+        scratch_shapes=[pltpu.VMEM((fields * rows, 256), f32)],
+        compiler_params=settings(16),
         name="collect",
-    )(camera_row, asked, returned)
-    all_sums = lax.all_to_all(sums, "views", split_axis=0, concat_axis=0, tiled=True)
+    )(camera_row, view_here, asked, returned)
+    all_sums = [sums[0]] + [
+        lax.ppermute(sums[offset], "views", [(view, (view + offset) % views) for view in range(views)])
+        for offset in range(1, views)
+    ]
     grads = pl.pallas_call(
         pull_kernel,
         out_shape=jax.ShapeDtypeStruct((channels, part_rows * 256), f32),
-        grid_spec=pltpu.PrefetchScalarGridSpec(
-            num_scalar_prefetch=1,
-            grid=(1,),
-            in_specs=[
-                pl.BlockSpec((views, fields * part_rows + 8, 256), lambda step, place: (0, 0, 0)),
-                pl.BlockSpec((channels, part_rows, 256), lambda step, place: (0, place[0], 0)),
-            ],
-            out_specs=pl.BlockSpec((channels, part_rows * 256), lambda step, place: (0, 0)),
-        ),
-        compiler_params=settings,
+        in_specs=[vmem] * (views + 1),
+        out_specs=vmem,
+        compiler_params=settings(16),
         name="pull",
-    )(view_here, all_sums, dense_params)
+    )(*all_sums, part_params)
     return picture[None], grads
 
 

time: 134 us -> 108 us (0.81)
  Pallas kernels: 63 us -> 45.4 us
  local copies, waits for them, and re-layouts: 7.72 us -> 4.37 us
  blocking collectives: 21 us -> 17.9 us
  waiting for transfers between devices: 17 us -> 15.3 us
    pallas_call x1, Pallas kernels: 37.2 us -> 22.8 us  [render_call(): pl.pallas_call(functools.partial(render_kernel, shift=shift), out_shape=(...]
    all_to_all x1 -> x0, waiting for transfers between devices: 6.87 us -> none  [body(): lax.all_to_all(sums, 'views', split_axis=0, concat_axis=0, tiled=True)]
    ppermute x0 -> x3, starting transfers between devices: none -> 6.21 us  [body(): lax.ppermute(sums[offset], 'views', [(view, (view + offset) % views) for...]
    all_to_all x1 -> x0, starting transfers between devices: 5.64 us -> none  [body(): lax.all_to_all(sums, 'views', split_axis=0, concat_axis=0, tiled=True)]
    ppermute x0 -> x3, waiting for transfers between devices: none -> 3.67 us  [body(): lax.ppermute(sums[offset], 'views', [(view, (view + offset) % views) for...]
    all_to_all x1, blocking collectives: 21 us -> 17.9 us  [body(): lax.all_to_all(outgoing, 'tiles', split_axis=0, concat_axis=0, tiled=True)]
    unnamed x13 -> x14, local copies, waits for them, and re-layouts: 5.58 us -> 3.64 us
    reshape x1 -> x0, local copies, waits for them, and re-layouts: 1.41 us -> none  [body(): dense_params = params.reshape(channels, rows, 256)]
  transfers between devices with their start and end apart: 3 -> 5, of which waited for: 2 -> 4; matrix products, arithmetic and copies ran while one was open for 5% -> 2% of each run, Pallas kernels for 2% -> 2%
where the time goes in v3:
time: 108 us; the launch traced here: 107 us
  Pallas kernels  45.4 us (42%)
  starting transfers between devices  21.4 us (20%)
  blocking collectives  17.9 us (17%)
  waiting for transfers between devices  15.3 us (14%)
  local copies, waits for them, and re-layouts  4.37 us (4%)
  between operations  2.16 us (2%)
    pallas_call x1, Pallas kernels, render_call(): pl.pallas_call(functools.partial(render_kernel, shift=shift), out_shape=(...  22.8 us
    all_to_all x1, blocking collectives, body(): lax.all_to_all(outgoing, 'tiles', split_axis=0, concat_axis=0, tiled=True)  17.9 us
    all_to_all x1, waiting for transfers between devices, body(): lax.all_to_all(found, 'tiles', split_axis=0, concat_axis=0, tiled=True)  10.8 us
    all_to_all x1, starting transfers between devices, body(): lax.all_to_all(requests, 'tiles', split_axis=0, concat_axis=0, tiled=True)  8.59 us
    pallas_call x1, Pallas kernels, body(): pl.pallas_call(functools.partial(collect_kernel, rows=rows, group=2), out...  7.61 us
    pallas_call x1, Pallas kernels, body(): pl.pallas_call(functools.partial(lookup_kernel, group=4), out_shape=jax.S...  7.52 us
    all_to_all x1, starting transfers between devices, body(): lax.all_to_all(found, 'tiles', split_axis=0, concat_axis=0, tiled=True)  6.56 us
    ppermute x3, starting transfers between devices, body(): lax.ppermute(sums[offset], 'views', [(view, (view + offset) % views) for...  6.21 us
  transfers between devices with their start and end apart: 5, of which 4 were waited for; matrix products, arithmetic and copies ran while one was open for 2% of the time, Pallas kernels for 2%

profile of v3, /device:TPU:1, one launch (start us, length us, event | category | flops | bytes accessed | tf_op | source)
XLA Modules:
  0.0 107.2 jit_solution(1343561564387983024)
XLA Ops:
  0.6 0.0 copy-start.4
  0.6 0.0 copy-start.1
  0.7 0.8 copy-done.1
  1.4 0.0 copy-start.3
  1.4 0.7 copy-done.3
  2.1 0.0 copy-start.5
  2.1 0.0 copy-start.2
  2.1 3.7 %bucket.1 = (s32[32,1,384]{2,1,0:T(1,128)}, s32[8,1024]{1,0:T(8,128)S(1)}) custom-call(s32[8]{0:T(128)S(1)} %bitcast.17, s32[8,1024]{1,0:T(8,128)S(1)} %bitcast.14), custom_call_target="tpu_custom_call" | custom-call | tf_op jit(solution)/shard_map/bucket/pallas_call | solution.py:659
  5.8 8.6 %all-to-all-start = ((s32[32,1,384]{2,1,0:T(1,128)}), s32[32,1,384]{2,1,0:T(1,128)S(1)}, u32[]{:S(2)}, u32[]{:S(2)}) async-start(s32[32,1,384]{2,1,0:T(1,128)} %get-tuple-element.14), calls=%async_computation | async-start | bytes 98304 | tf_op jit(solution)/shard_map/all_to_all | solution.py:674
  15.8 0.7 slice_bitcast_fusion
  16.6 0.7 pad_maximum_fusion.camera_ref
  17.3 0.0 copy-start
  17.3 1.6 %copy-done = f32[59,8192]{1,0:T(8,128)S(1)} copy-done((f32[59,8192]{1,0:T(8,128)S(1)}, f32[59,8192]{1,0:T(8,128)}, u32[]{:S(2)}) %copy-start) | copy-done | bytes 1933336
  18.9 2.0 %project.1 = (bf16[288,512]{1,0:T(8,128)(2,1)S(1)}, bf16[64,256]{1,0:T(8,128)(2,1)S(1)}, f32[59,8,256]{2,1,0:T(8,128)S(1)}) custom-call(f32[8]{0:T(128)S(1)} %pad_maximum_fusion.camera_ref, s32[1]{0:T(128)} %bitcast.6.place_ref, f32[59,8192]{1,0:T(8,128)S(1)} %copy-done), custom_call_target="tpu_custom_call" | custom-call | tf_op jit(solution)/shard_map/project/pallas_call | solution.py:675
  20.9 0.8 all-to-all-done.asked_ref
  21.7 7.5 %lookup.1 = f32[32,1,3456]{2,1,0:T(1,128)} custom-call(s32[32,1,384]{2,1,0:T(1,128)S(1)} %all-to-all-done.asked_ref, bf16[288,512]{1,0:T(8,128)(2,1)S(1)} %get-tuple-element.15.table_ref, bf16[64,256]{1,0:T(8,128)(2,1)S(1)} %get-tuple-element.16.third_ref), custom_call_target="tpu_custom_call" | custom-call | tf_op jit(solution)/shard_map/lookup/pallas_call | solution.py:688
  29.2 6.6 %all-to-all-start.1 = ((f32[32,1,3456]{2,1,0:T(1,128)}), f32[32,1,3456]{2,1,0:T(1,128)S(1)}, u32[]{:S(2)}, u32[]{:S(2)}) async-start(f32[32,1,3456]{2,1,0:T(1,128)} %lookup.1), calls=%async_computation.1 | async-start | bytes 884736 | tf_op jit(solution)/shard_map/all_to_all | solution.py:696
  35.8 0.0 copy-done.5
  35.8 10.8 %all-to-all-done.1.fetched_ref = f32[32,1,3456]{2,1,0:T(1,128)S(1)} async-done(((f32[32,1,3456]{2,1,0:T(1,128)}), f32[32,1,3456]{2,1,0:T(1,128)S(1)}, u32[]{:S(2)}, u32[]{:S(2)}) %all-to-all-start.1) | async-done | bytes 442400 | tf_op jit(solution)/shard_map/all_to_all | solution.py:696
  46.6 0.0 copy-done.4
  46.6 0.0 copy-done.2
  46.6 22.8 %render.1 = (f32[8,3,256]{2,1,0:T(4,128)S(1)}, f32[32,1,3456]{2,1,0:T(1,128)S(1)}) custom-call(s32[8]{0:T(128)S(1)} %bitcast.18, s32[1]{0:T(128)} %bitcast.1.place_ref, s32[8,1024]{1,0:T(8,128)S(1)} %bitcast.15, s32[8,1024]{1,0:T(8,128)S(1)} %get-tuple-element.13.rank_ref, f32[32,1,3456]{2,1,0:T(1,128)S(1)} %all-to-all-done.1.fetched_ref, ...), custom_call_target="tpu_custom_call" | custom-call | tf_op jit(solution)/shard_map/render/pallas_call | solution.py:604
  69.5 17.9 %all_to_all.15.returned_ref = f32[32,1,3456]{2,1,0:T(1,128)S(1)} all-to-all(f32[32,1,3456]{2,1,0:T(1,128)S(1)} %get-tuple-element.18), channel_id=1, replica_groups=mesh['tiles'=32,'views'=4] {'tiles'}, dimensions={0} | all-to-all | bytes 884736 | tf_op jit(solution)/shard_map/all_to_all | solution.py:698
  87.4 7.6 %collect.1 = (f32[80,256]{1,0:T(8,128)S(1)}, f32[80,256]{1,0:T(8,128)S(1)}, f32[80,256]{1,0:T(8,128)S(1)}, f32[80,256]{1,0:T(8,128)S(1)}) custom-call(f32[8]{0:T(128)S(1)} %pad_maximum_fusion.camera_ref, s32[1]{0:T(128)} %bitcast.6.place_ref, s32[32,1,384]{2,1,0:T(1,128)S(1)} %all-to-all-done.asked_ref, f32[32,1,3456]{2,1,0:T(1,128)S(1)} %all_to_all.15.returned_ref), custom_call_target="tpu_custom_call" | custom-call | tf_op jit(solution)/shard_map/collect/pallas_call | solution.py:699
  95.0 2.6 %collective-permute-start = (f32[80,256]{1,0:T(8,128)S(1)}, f32[80,256]{1,0:T(8,128)S(1)}, u32[]{:S(2)}, u32[]{:S(2)}) collective-permute-start(f32[80,256]{1,0:T(8,128)S(1)} %get-tuple-element.20), channel_id=1, source_target_pairs={{0,1},{1,2},{2,3},{3,0},{4,5},{5,6},{6,7},{7,4},{8,9},{9,10},{10,1... | collective-permute-start | bytes 245768 | tf_op jit(solution)/shard_map/ppermute | solution.py:709
  97.6 3.4 %collective-permute-start.1 = (f32[80,256]{1,0:T(8,128)S(1)}, f32[80,256]{1,0:T(8,128)S(1)}, u32[]{:S(2)}, u32[]{:S(2)}) collective-permute-start(f32[80,256]{1,0:T(8,128)S(1)} %get-tuple-element.21), channel_id=1, source_target_pairs={{0,2},{1,3},{2,0},{3,1},{4,6},{5,7},{6,4},{7,5},{8,10},{9,11},{10,... | collective-permute-start | bytes 245768 | tf_op jit(solution)/shard_map/ppermute | solution.py:709
  101.0 0.2 collective-permute-start.2
  101.2 0.6 copy.9
  101.8 1.0 collective-permute-done.refs_1_
  102.8 2.7 %collective-permute-done.1.refs_2_ = f32[80,256]{1,0:T(8,128)S(1)} collective-permute-done((f32[80,256]{1,0:T(8,128)S(1)}, f32[80,256]{1,0:T(8,128)S(1)}, u32[]{:S(2)}, u32[]{:S(2)}) %collective-permute-start.1) | collective-permute-done | bytes 81952 | tf_op jit(solution)/shard_map/ppermute | solution.py:709
  105.5 0.0 collective-permute-done.2.refs_3_
  105.5 1.7 %pull.1 = f32[59,2048]{1,0:T(8,128)} custom-call(f32[80,256]{1,0:T(8,128)S(1)} %get-tuple-element.19.refs_0_, f32[80,256]{1,0:T(8,128)S(1)} %collective-permute-done.refs_1_, f32[80,256]{1,0:T(8,128)S(1)} %collective-permute-done.1.refs_2_, f32[80,256]{1,0:T(8,128)S(1)} %collective-permute-done.2.refs_3_, f32[59,8,256]{2,1,0:T(8,128)S(1)} %get-tuple-element.23.refs_4_), custom_call_target="tpu_custom_call" | custom-call | tf_op jit(solution)/shard_map/pull/pallas_call | solution.py:712
  (1 shorter events, 0.0 us)
Async XLA Ops:
  0.6 46.0 %copy-start.4 = (s32[1,8]{1,0:T(1,128)S(1)}, s32[1,8]{1,0:T(1,128)}, u32[]{:S(2)}) copy-start(s32[1,8]{1,0:T(1,128)} %param.9) | copy-start | bytes 100
  0.6 0.8 copy-start.1
  1.4 0.7 copy-start.3
  2.1 33.8 %copy-start.5 = (f32[1,8,3,256]{3,1,2,0:T(8,128)S(1)}, f32[1,8,3,256]{3,1,2,0:T(8,128)}, u32[]{:S(2)}) copy-start(f32[1,8,3,256]{3,1,2,0:T(8,128)} %param.10) | copy-start | bytes 73732
  2.1 44.5 %copy-start.2 = (s32[1,8,1024]{2,1,0:T(8,128)S(1)}, s32[1,8,1024]{2,1,0:T(8,128)}, u32[]{:S(2)}) copy-start(s32[1,8,1024]{2,1,0:T(8,128)} %param.8) | copy-start | bytes 98308
  5.8 15.9 %all-to-all-start = ((s32[32,1,384]{2,1,0:T(1,128)}), s32[32,1,384]{2,1,0:T(1,128)S(1)}, u32[]{:S(2)}, u32[]{:S(2)}) async-start(s32[32,1,384]{2,1,0:T(1,128)} %get-tuple-element.14), calls=%async_computation | async-start | bytes 98304 | tf_op jit(solution)/shard_map/all_to_all | solution.py:674
  17.3 1.6 %copy-start = (f32[59,8192]{1,0:T(8,128)S(1)}, f32[59,8192]{1,0:T(8,128)}, u32[]{:S(2)}) copy-start(f32[59,8192]{1,0:T(8,128)} %params_ref.1) | copy-start | bytes 5799940
  29.2 17.4 %all-to-all-start.1 = ((f32[32,1,3456]{2,1,0:T(1,128)}), f32[32,1,3456]{2,1,0:T(1,128)S(1)}, u32[]{:S(2)}, u32[]{:S(2)}) async-start(f32[32,1,3456]{2,1,0:T(1,128)} %lookup.1), calls=%async_computation.1 | async-start | bytes 884736 | tf_op jit(solution)/shard_map/all_to_all | solution.py:696
  95.0 7.8 %collective-permute-start = (f32[80,256]{1,0:T(8,128)S(1)}, f32[80,256]{1,0:T(8,128)S(1)}, u32[]{:S(2)}, u32[]{:S(2)}) collective-permute-start(f32[80,256]{1,0:T(8,128)S(1)} %get-tuple-element.20), channel_id=1, source_target_pairs={{0,1},{1,2},{2,3},{3,0},{4,5},{5,6},{6,7},{7,4},{8,9},{9,10},{10,1... | collective-permute-start | bytes 245768 | tf_op jit(solution)/shard_map/ppermute | solution.py:709
  97.6 7.9 %collective-permute-start.1 = (f32[80,256]{1,0:T(8,128)S(1)}, f32[80,256]{1,0:T(8,128)S(1)}, u32[]{:S(2)}, u32[]{:S(2)}) collective-permute-start(f32[80,256]{1,0:T(8,128)S(1)} %get-tuple-element.21), channel_id=1, source_target_pairs={{0,2},{1,3},{2,0},{3,1},{4,6},{5,7},{6,4},{7,5},{8,10},{9,11},{10,... | collective-permute-start | bytes 245768 | tf_op jit(solution)/shard_map/ppermute | solution.py:709
  101.0 4.5 %collective-permute-start.2 = (f32[80,256]{1,0:T(8,128)S(1)}, f32[80,256]{1,0:T(8,128)S(1)}, u32[]{:S(2)}, u32[]{:S(2)}) collective-permute-start(f32[80,256]{1,0:T(8,128)S(1)} %get-tuple-element.22), channel_id=1, source_target_pairs={{0,3},{1,0},{2,1},{3,2},{4,7},{5,4},{6,5},{7,6},{8,11},{9,8},{10,9... | collective-permute-start | bytes 245768 | tf_op jit(solution)/shard_map/ppermute | solution.py:709

commit v4 on v3

--- a/solution.py
+++ b/solution.py
@@ -179,6 +179,7 @@
 def bucket_kernel(counts_ref, lists_ref, requests_ref, rank_ref, hits_ref, earlier_ref, *, owners, capacity, shift):
     tiles, slots = lists_ref.shape
     blocks = slots // 256
+    thirds = capacity // 128
     upper = (
         lax.broadcasted_iota(i32, (256, 256), 0) < lax.broadcasted_iota(i32, (256, 256), 1)
     ).astype(f32).astype(bf16)
@@ -191,46 +192,61 @@
             at = (tile * blocks + block) * owners
             hits_ref[at : at + owners, :] = jnp.where(owner_rows == owner, 1.0, 0.0).astype(bf16)
     earlier_ref[...] = jnp.dot(hits_ref[...], upper, preferred_element_type=f32)
-    rank_rows = lax.broadcasted_iota(i32, (capacity, 256), 0)
+    low_rows = lax.broadcasted_iota(i32, (128, 256), 0)
+    high_rows = lax.broadcasted_iota(i32, (owners * thirds, 256), 0)
     carry = jnp.zeros((owners, 1), f32)
-    total = jnp.zeros((2 * owners, capacity), f32)
+    total = jnp.zeros((2 * owners * thirds, 128), f32)
     for tile in range(tiles):
         for block in range(blocks):
             at = (tile * blocks + block) * owners
             hits = hits_ref[at : at + owners, :].astype(f32)
             earlier = earlier_ref[at : at + owners, :]
-            rank = jnp.sum(hits * (earlier + carry), axis=0, keepdims=True)
+            rank = jnp.sum(hits * (earlier + carry), axis=0, keepdims=True).astype(i32)
             live = lane + block * 256 < counts_ref[tile]
-            rank = jnp.where(live, rank, -1.0).astype(i32)
-            rank_ref[tile : tile + 1, block * 256 : block * 256 + 256] = rank
+            rank_ref[tile : tile + 1, block * 256 : block * 256 + 256] = jnp.where(live, rank, -1)
             carry = carry + earlier[:, 255:256] + hits[:, 255:256]
             ids = lists_ref[tile : tile + 1, block * 256 : block * 256 + 256]
             local = (ids & ((1 << shift) - 1)) + 1
             coarse = (local >> 7).astype(f32)
             fine = (local & 127).astype(f32)
-            placed = jnp.concatenate([hits * coarse, hits * fine], axis=0).astype(bf16)
-            at_rank = jnp.where(rank_rows == rank, 1.0, 0.0).astype(bf16)
+            place = jnp.where(live, (ids >> shift) * thirds + (rank >> 7), -1)
+            mask = high_rows == place
+            placed = jnp.concatenate(
+                [jnp.where(mask, coarse, 0.0), jnp.where(mask, fine, 0.0)], axis=0
+            ).astype(bf16)
+            at_rank = jnp.where(low_rows == (rank & 127), 1.0, 0.0).astype(bf16)
             total = total + lax.dot_general(placed, at_rank, nt_dims, preferred_element_type=f32)
-    requests = (total[:owners] * 128.0 + total[owners:]).astype(i32) - 1
+    requests = (total[: owners * thirds] * 128.0 + total[owners * thirds :]).astype(i32) - 1
     for owner in range(owners):
-        requests_ref[owner] = requests[owner : owner + 1]
-
-
-def lookup_kernel(asked_ref, table_ref, third_ref, found_ref, *, group):
+        for third in range(thirds):
+            row = owner * thirds + third
+            requests_ref[owner, :, third * 128 : third * 128 + 128] = requests[row : row + 1]
+
+
+def lookup_kernel(asked_ref, table_ref, third_ref, found_ref, pick_ref, *, group):
     askers, _, capacity = asked_ref.shape
     rows = table_ref.shape[0] // fields
     width = group * capacity
+    steps = askers // group
     low_rows = lax.broadcasted_iota(i32, (256, width), 0)
     high_rows = lax.broadcasted_iota(i32, (rows, width), 0)
 
-    def step(part, carry):
-        asked = jnp.concatenate([asked_ref[group * part + k] for k in range(group)], axis=1)
-        pick = jnp.where(low_rows == (asked & 255), 1.0, 0.0).astype(bf16)
-        mask = high_rows == (asked >> 8)
+    def asked_of(part):
+        return jnp.concatenate([asked_ref[group * part + k] for k in range(group)], axis=1)
+
+    def prepare(part):
+        pick_ref[part % 2] = jnp.where(low_rows == (asked_of(part) & 255), 1.0, 0.0).astype(bf16)
+
+    def multiply(part):
+        pick = pick_ref[part % 2]
         result = jnp.dot(
             table_ref[...], jnp.concatenate([pick, pick], axis=0), preferred_element_type=f32
         )
         third = jnp.dot(third_ref[...], pick, preferred_element_type=f32)
+        return result, third
+
+    def choose(part, result, third):
+        mask = high_rows == (asked_of(part) >> 8)
         for field in range(fields):
             values = result[field * rows : (field + 1) * rows]
             if field < 2:
@@ -240,26 +256,29 @@
                 found_ref[group * part + k, :, field * capacity : (field + 1) * capacity] = found[
                     :, k * capacity : (k + 1) * capacity
                 ]
-        return carry
-
-    lax.fori_loop(0, askers // group, step, 0)
+
+    prepare(0)
+    for part in range(steps):
+        result, third = multiply(part)
+        if part + 1 < steps:
+            prepare(part + 1)
+        choose(part, result, third)
 
 
 def collect_kernel(camera_ref, place_ref, asked_ref, returned_ref, *rest, rows, group):
-    *sums_refs, total_ref = rest
+    *sums_refs, total_ref, pick_ref, placed_ref = rest
     askers, _, capacity = asked_ref.shape
     views = len(sums_refs)
     width = group * capacity
+    steps = askers // group
     low_rows = lax.broadcasted_iota(i32, (256, width), 0)
     high_rows = lax.broadcasted_iota(i32, (rows, width), 0)
-    total_ref[...] = jnp.zeros_like(total_ref)
-
-    def step(part, carry):
+
+    def prepare(part):
+        at = part % 2
         asked = jnp.concatenate([asked_ref[group * part + k] for k in range(group)], axis=1)
-        pick = jnp.where(low_rows == (asked & 255), 1.0, 0.0).astype(bf16)
+        pick_ref[at] = jnp.where(low_rows == (asked & 255), 1.0, 0.0).astype(bf16)
         mask = high_rows == (asked >> 8)
-        uppers = []
-        lowers = []
         for field in range(fields):
             values = jnp.concatenate(
                 [
@@ -269,17 +288,24 @@
                 axis=1,
             )
             upper = values.astype(bf16).astype(f32)
-            uppers.append(jnp.where(mask, upper, 0.0).astype(bf16))
-            lowers.append(jnp.where(mask, values - upper, 0.0).astype(bf16))
-        placed = jnp.concatenate(
-            [jnp.concatenate(uppers, axis=0), jnp.concatenate(lowers, axis=0)], axis=1
-        )
-        total_ref[...] += lax.dot_general(
-            placed, jnp.concatenate([pick, pick], axis=1), nt_dims, preferred_element_type=f32
-        )
-        return carry
-
-    lax.fori_loop(0, askers // group, step, 0)
+            row = field * rows
+            placed_ref[at, row : row + rows, :width] = jnp.where(mask, upper, 0.0).astype(bf16)
+            placed_ref[at, row : row + rows, width:] = jnp.where(mask, values - upper, 0.0).astype(bf16)
+
+    def multiply(part):
+        at = part % 2
+        pick = pick_ref[at]
+        return lax.dot_general(
+            placed_ref[at], jnp.concatenate([pick, pick], axis=1), nt_dims, preferred_element_type=f32
+        )
+
+    prepare(0)
+    for part in range(steps):
+        product = multiply(part)
+        if part + 1 < steps:
+            prepare(part + 1)
+        total_ref[...] = product if part == 0 else total_ref[...] + product
+
     part_rows = rows // views
     for offset, sums_ref in enumerate(sums_refs):
         view = lax.rem(place_ref[0] + offset, views)
@@ -289,6 +315,14 @@
         for entry in range(8):
             at = fields * part_rows + entry
             sums_ref[at : at + 1, :] = jnp.full((1, 256), camera_ref[entry], f32)
+
+
+def collect_scratch(group, rows, capacity):
+    return [
+        pltpu.VMEM((fields * rows, 256), f32),
+        pltpu.VMEM((2, 256, group * capacity), bf16),
+        pltpu.VMEM((2, fields * rows, 2 * group * capacity), bf16),
+    ]
 
 
 def pull_kernel(*refs):
@@ -429,12 +463,14 @@
         fetched = jnp.dot(
             fetch_ref[...], jnp.concatenate([at_rank, at_rank], axis=0), preferred_element_type=f32
         )
-        yield
         mask = owner_rows == owner
         found = []
         for field in range(fields):
+            if field in (0, 5):
+                yield
             values = fetched[field * owners : (field + 1) * owners]
             found.append(jnp.sum(jnp.where(mask, values, 0.0), axis=0, keepdims=True))
+        yield
         pos_u = found[0] - (tile.astype(f32) * 16.0 + 8.0)
         pos_v = found[1]
         coef_a, coef_b, coef_c, log_opacity = found[2:6]
@@ -564,12 +600,12 @@
                 raise ValueError(order)
 
     def ramp_up(step, carry):
-        run("mmmmmfff", m=forward(step - 1), f=fetch(step))
+        run("mfmmffmfmf", m=forward(step - 1), f=fetch(step))
         return carry
 
     def steady(step, carry):
         run(
-            "mbsmfmbfmbmbf",
+            "mbmsfmbfmfbmbff",
             s=send_step(step - lag - 1),
             b=backward(step - lag),
             m=forward(step - 1),
@@ -578,12 +614,12 @@
         return carry
 
     def ramp_down(step, carry):
-        run("sbbbb", s=send_step(step - lag - 1), b=backward(step - lag))
+        run("bsbbb", s=send_step(step - lag - 1), b=backward(step - lag))
         return carry
 
     lax.fori_loop(0, lag, ramp_up, 0)
     lax.fori_loop(lag, items, steady, 0)
-    run("sbbbbmmmmm", s=send_step(items - lag - 1), b=backward(items - lag), m=forward(items - 1))
+    run("mbsmmbmbmb", s=send_step(items - lag - 1), b=backward(items - lag), m=forward(items - 1))
     lax.fori_loop(items + 1, items + lag + 1, ramp_down, 0)
     for tile in range(tiles):
         image_ref[tile] = picture_ref[tile, 0:3]
@@ -668,7 +704,7 @@
             pltpu.VMEM((tiles * slots // 256 * owners, 256), bf16),
             pltpu.VMEM((tiles * slots // 256 * owners, 256), f32),
         ],
-        compiler_params=settings(16),
+        compiler_params=settings(56),
         name="bucket",
     )(counts, lists)
     asked = lax.all_to_all(requests, "tiles", split_axis=0, concat_axis=0, tiled=True)
@@ -686,10 +722,11 @@
         name="project",
     )(camera_row, view_here, params)
     found = pl.pallas_call(
-        functools.partial(lookup_kernel, group=4),
+        functools.partial(lookup_kernel, group=2),
         out_shape=jax.ShapeDtypeStruct((owners, 1, fields * capacity), f32),
         in_specs=[vmem, vmem, vmem],
         out_specs=vmem,
+        scratch_shapes=[pltpu.VMEM((2, 256, 2 * capacity), bf16)],
         compiler_params=settings(16),
         name="lookup",
     )(asked, table, third)
@@ -701,7 +738,7 @@
         out_shape=[jax.ShapeDtypeStruct((fields * part_rows + 8, 256), f32)] * views,
         in_specs=[smem, smem, vmem, vmem],
         out_specs=[vmem] * views,
-        scratch_shapes=[pltpu.VMEM((fields * rows, 256), f32)],
+        scratch_shapes=collect_scratch(2, rows, capacity),
         compiler_params=settings(16),
         name="collect",
     )(camera_row, view_here, asked, returned)

time: 108 us -> 101 us (0.935); the launches traced: 107 us -> 99.1 us
  Pallas kernels: 45.4 us -> 40.8 us
  local copies, waits for them, and re-layouts: 4.37 us -> 2.96 us
  blocking collectives: 17.9 us -> 16.8 us
    pallas_call x1, Pallas kernels: 7.61 us -> 4.9 us  [body(): pl.pallas_call(functools.partial(collect_kernel, rows=rows, group=2), out...]
    unnamed x14 -> x12, local copies, waits for them, and re-layouts: 3.64 us -> 2.24 us
    pallas_call x1, Pallas kernels: 7.52 us -> 6.13 us  [body(): pl.pallas_call(functools.partial(lookup_kernel, group=2), out_shape=jax.S...]
    all_to_all x1, blocking collectives: 17.9 us -> 16.8 us  [body(): lax.all_to_all(outgoing, 'tiles', split_axis=0, concat_axis=0, tiled=True)]
where the time goes in v4:
time: 101 us; the launch traced here: 99.1 us
  Pallas kernels  40.8 us (40%)
  starting transfers between devices  21.1 us (21%)
  blocking collectives  16.8 us (17%)
  waiting for transfers between devices  14.6 us (14%)
  local copies, waits for them, and re-layouts  2.96 us (3%)
  between operations  2.16 us (2%)
    pallas_call x1, Pallas kernels, render_call(): pl.pallas_call(functools.partial(render_kernel, shift=shift), out_shape=(...  22.7 us
    all_to_all x1, blocking collectives, body(): lax.all_to_all(outgoing, 'tiles', split_axis=0, concat_axis=0, tiled=True)  16.8 us
    all_to_all x1, waiting for transfers between devices, body(): lax.all_to_all(found, 'tiles', split_axis=0, concat_axis=0, tiled=True)  10.8 us
    all_to_all x1, starting transfers between devices, body(): lax.all_to_all(requests, 'tiles', split_axis=0, concat_axis=0, tiled=True)  8.72 us
    all_to_all x1, starting transfers between devices, body(): lax.all_to_all(found, 'tiles', split_axis=0, concat_axis=0, tiled=True)  6.59 us
    pallas_call x1, Pallas kernels, body(): pl.pallas_call(functools.partial(lookup_kernel, group=2), out_shape=jax.S...  6.13 us
    ppermute x3, starting transfers between devices, body(): lax.ppermute(sums[offset], 'views', [(view, (view + offset) % views) for...  5.82 us
    pallas_call x1, Pallas kernels, body(): pl.pallas_call(functools.partial(collect_kernel, rows=rows, group=2), out...  4.9 us
  transfers between devices with their start and end apart: 5, of which 4 were waited for; matrix products, arithmetic and copies ran while one was open for 2% of the time, Pallas kernels for 2%

profile of v4, /device:TPU:1, one launch (start us, length us, event | category | flops | bytes accessed | tf_op | source)
XLA Modules:
  0.0 99.1 jit_solution(9135066060048597792)
XLA Ops:
  0.6 0.0 copy-start.3
  0.6 0.0 copy-start.1
  0.7 0.0 copy-start.4
  0.7 3.2 %bucket.1 = (s32[32,1,384]{2,1,0:T(1,128)}, s32[8,1024]{1,0:T(8,128)}) custom-call(s32[8]{0:T(128)} %bitcast.17, s32[8,1024]{1,0:T(8,128)} %bitcast.14), custom_call_target="tpu_custom_call" | custom-call | tf_op jit(solution)/shard_map/bucket/pallas_call | solution.py:695
  3.9 0.0 copy-start.2
  3.9 8.7 %all-to-all-start = ((s32[32,1,384]{2,1,0:T(1,128)}), s32[32,1,384]{2,1,0:T(1,128)S(1)}, u32[]{:S(2)}, u32[]{:S(2)}) async-start(s32[32,1,384]{2,1,0:T(1,128)} %get-tuple-element.14), calls=%async_computation | async-start | bytes 98304 | tf_op jit(solution)/shard_map/all_to_all | solution.py:710
  14.1 0.7 slice_bitcast_fusion
  14.8 0.7 pad_maximum_fusion.camera_ref
  15.5 0.0 copy-start
  15.5 1.6 %copy-done = f32[59,8192]{1,0:T(8,128)S(1)} copy-done((f32[59,8192]{1,0:T(8,128)S(1)}, f32[59,8192]{1,0:T(8,128)}, u32[]{:S(2)}) %copy-start) | copy-done | bytes 1933336
  17.1 2.0 %project.1 = (bf16[288,512]{1,0:T(8,128)(2,1)S(1)}, bf16[64,256]{1,0:T(8,128)(2,1)S(1)}, f32[59,8,256]{2,1,0:T(8,128)S(1)}) custom-call(f32[8]{0:T(128)S(1)} %pad_maximum_fusion.camera_ref, s32[1]{0:T(128)} %bitcast.6.place_ref, f32[59,8192]{1,0:T(8,128)S(1)} %copy-done), custom_call_target="tpu_custom_call" | custom-call | tf_op jit(solution)/shard_map/project/pallas_call | solution.py:711
  19.1 0.8 all-to-all-done.asked_ref
  20.0 6.1 %lookup.1 = f32[32,1,3456]{2,1,0:T(1,128)} custom-call(s32[32,1,384]{2,1,0:T(1,128)S(1)} %all-to-all-done.asked_ref, bf16[288,512]{1,0:T(8,128)(2,1)S(1)} %get-tuple-element.15.table_ref, bf16[64,256]{1,0:T(8,128)(2,1)S(1)} %get-tuple-element.16.third_ref), custom_call_target="tpu_custom_call" | custom-call | tf_op jit(solution)/shard_map/lookup/pallas_call | solution.py:724
  26.1 6.6 %all-to-all-start.1 = ((f32[32,1,3456]{2,1,0:T(1,128)}), f32[32,1,3456]{2,1,0:T(1,128)S(1)}, u32[]{:S(2)}, u32[]{:S(2)}) async-start(f32[32,1,3456]{2,1,0:T(1,128)} %lookup.1), calls=%async_computation.1 | async-start | bytes 884736 | tf_op jit(solution)/shard_map/all_to_all | solution.py:733
  32.7 0.0 copy-done.4
  32.7 10.8 %all-to-all-done.1.fetched_ref = f32[32,1,3456]{2,1,0:T(1,128)S(1)} async-done(((f32[32,1,3456]{2,1,0:T(1,128)}), f32[32,1,3456]{2,1,0:T(1,128)S(1)}, u32[]{:S(2)}, u32[]{:S(2)}) %all-to-all-start.1) | async-done | bytes 442400 | tf_op jit(solution)/shard_map/all_to_all | solution.py:733
  43.5 0.0 copy-done.3
  43.5 0.0 copy-done.1
  43.5 0.0 copy-done.2
  43.5 22.7 %render.1 = (f32[8,3,256]{2,1,0:T(4,128)S(1)}, f32[32,1,3456]{2,1,0:T(1,128)S(1)}) custom-call(s32[8]{0:T(128)S(1)} %bitcast.18, s32[1]{0:T(128)} %bitcast.1.place_ref, s32[8,1024]{1,0:T(8,128)S(1)} %bitcast.15, s32[8,1024]{1,0:T(8,128)S(1)} %copy-done.2, f32[32,1,3456]{2,1,0:T(1,128)S(1)} %all-to-all-done.1.fetched_ref, f32[8,3,256]{2,1,0:T(4,128)S(1)} %bitcast.13), custom_call_target="tpu_custom_call" | custom-call | tf_op jit(solution)/shard_map/render/pallas_call | solution.py:640
  66.2 16.8 %all_to_all.15.returned_ref = f32[32,1,3456]{2,1,0:T(1,128)S(1)} all-to-all(f32[32,1,3456]{2,1,0:T(1,128)S(1)} %get-tuple-element.18), channel_id=1, replica_groups=mesh['tiles'=32,'views'=4] {'tiles'}, dimensions={0} | all-to-all | bytes 884736 | tf_op jit(solution)/shard_map/all_to_all | solution.py:735
  83.0 4.9 %collect.1 = (f32[80,256]{1,0:T(8,128)S(1)}, f32[80,256]{1,0:T(8,128)S(1)}, f32[80,256]{1,0:T(8,128)S(1)}, f32[80,256]{1,0:T(8,128)S(1)}) custom-call(f32[8]{0:T(128)S(1)} %pad_maximum_fusion.camera_ref, s32[1]{0:T(128)} %bitcast.6.place_ref, s32[32,1,384]{2,1,0:T(1,128)S(1)} %all-to-all-done.asked_ref, f32[32,1,3456]{2,1,0:T(1,128)S(1)} %all_to_all.15.returned_ref), custom_call_target="tpu_custom_call" | custom-call | tf_op jit(solution)/shard_map/collect/pallas_call | solution.py:736
  87.9 2.9 %collective-permute-start = (f32[80,256]{1,0:T(8,128)S(1)}, f32[80,256]{1,0:T(8,128)S(1)}, u32[]{:S(2)}, u32[]{:S(2)}) collective-permute-start(f32[80,256]{1,0:T(8,128)S(1)} %get-tuple-element.20), channel_id=1, source_target_pairs={{0,1},{1,2},{2,3},{3,0},{4,5},{5,6},{6,7},{7,4},{8,9},{9,10},{10,1... | collective-permute-start | bytes 245768 | tf_op jit(solution)/shard_map/ppermute | solution.py:746
  90.7 2.2 %collective-permute-start.1 = (f32[80,256]{1,0:T(8,128)S(1)}, f32[80,256]{1,0:T(8,128)S(1)}, u32[]{:S(2)}, u32[]{:S(2)}) collective-permute-start(f32[80,256]{1,0:T(8,128)S(1)} %get-tuple-element.21), channel_id=1, source_target_pairs={{0,2},{1,3},{2,0},{3,1},{4,6},{5,7},{6,4},{7,5},{8,10},{9,11},{10,... | collective-permute-start | bytes 245768 | tf_op jit(solution)/shard_map/ppermute | solution.py:746
  92.9 0.8 collective-permute-start.2
  93.7 0.6 copy.9
  94.3 0.4 collective-permute-done.refs_1_
  94.7 2.7 %collective-permute-done.1.refs_2_ = f32[80,256]{1,0:T(8,128)S(1)} collective-permute-done((f32[80,256]{1,0:T(8,128)S(1)}, f32[80,256]{1,0:T(8,128)S(1)}, u32[]{:S(2)}, u32[]{:S(2)}) %collective-permute-start.1) | collective-permute-done | bytes 81952 | tf_op jit(solution)/shard_map/ppermute | solution.py:746
  97.3 0.0 collective-permute-done.2.refs_3_
  97.3 1.8 %pull.1 = f32[59,2048]{1,0:T(8,128)} custom-call(f32[80,256]{1,0:T(8,128)S(1)} %get-tuple-element.19.refs_0_, f32[80,256]{1,0:T(8,128)S(1)} %collective-permute-done.refs_1_, f32[80,256]{1,0:T(8,128)S(1)} %collective-permute-done.1.refs_2_, f32[80,256]{1,0:T(8,128)S(1)} %collective-permute-done.2.refs_3_, f32[59,8,256]{2,1,0:T(8,128)S(1)} %get-tuple-element.23.refs_4_), custom_call_target="tpu_custom_call" | custom-call | tf_op jit(solution)/shard_map/pull/pallas_call | solution.py:749
  (1 shorter events, 0.0 us)
Async XLA Ops:
  0.6 42.8 %copy-start.3 = (s32[1,8]{1,0:T(1,128)S(1)}, s32[1,8]{1,0:T(1,128)}, u32[]{:S(2)}) copy-start(s32[1,8]{1,0:T(1,128)} %param.9) | copy-start | bytes 100
  0.6 42.8 %copy-start.1 = (s32[1,8,1024]{2,1,0:T(8,128)S(1)}, s32[1,8,1024]{2,1,0:T(8,128)}, u32[]{:S(2)}) copy-start(s32[1,8,1024]{2,1,0:T(8,128)} %param.8) | copy-start | bytes 98308
  0.7 32.0 %copy-start.4 = (f32[1,8,3,256]{3,1,2,0:T(8,128)S(1)}, f32[1,8,3,256]{3,1,2,0:T(8,128)}, u32[]{:S(2)}) copy-start(f32[1,8,3,256]{3,1,2,0:T(8,128)} %param.10) | copy-start | bytes 73732
  3.9 39.6 %copy-start.2 = (s32[8,1024]{1,0:T(8,128)S(1)}, s32[8,1024]{1,0:T(8,128)}, u32[]{:S(2)}) copy-start(s32[8,1024]{1,0:T(8,128)} %get-tuple-element.13.rank_ref) | copy-start | bytes 98308
  3.9 16.1 %all-to-all-start = ((s32[32,1,384]{2,1,0:T(1,128)}), s32[32,1,384]{2,1,0:T(1,128)S(1)}, u32[]{:S(2)}, u32[]{:S(2)}) async-start(s32[32,1,384]{2,1,0:T(1,128)} %get-tuple-element.14), calls=%async_computation | async-start | bytes 98304 | tf_op jit(solution)/shard_map/all_to_all | solution.py:710
  15.5 1.6 %copy-start = (f32[59,8192]{1,0:T(8,128)S(1)}, f32[59,8192]{1,0:T(8,128)}, u32[]{:S(2)}) copy-start(f32[59,8192]{1,0:T(8,128)} %params_ref.1) | copy-start | bytes 5799940
  26.1 17.4 %all-to-all-start.1 = ((f32[32,1,3456]{2,1,0:T(1,128)}), f32[32,1,3456]{2,1,0:T(1,128)S(1)}, u32[]{:S(2)}, u32[]{:S(2)}) async-start(f32[32,1,3456]{2,1,0:T(1,128)} %lookup.1), calls=%async_computation.1 | async-start | bytes 884736 | tf_op jit(solution)/shard_map/all_to_all | solution.py:733
  87.9 6.8 %collective-permute-start = (f32[80,256]{1,0:T(8,128)S(1)}, f32[80,256]{1,0:T(8,128)S(1)}, u32[]{:S(2)}, u32[]{:S(2)}) collective-permute-start(f32[80,256]{1,0:T(8,128)S(1)} %get-tuple-element.20), channel_id=1, source_target_pairs={{0,1},{1,2},{2,3},{3,0},{4,5},{5,6},{6,7},{7,4},{8,9},{9,10},{10,1... | collective-permute-start | bytes 245768 | tf_op jit(solution)/shard_map/ppermute | solution.py:746
  90.7 6.6 %collective-permute-start.1 = (f32[80,256]{1,0:T(8,128)S(1)}, f32[80,256]{1,0:T(8,128)S(1)}, u32[]{:S(2)}, u32[]{:S(2)}) collective-permute-start(f32[80,256]{1,0:T(8,128)S(1)} %get-tuple-element.21), channel_id=1, source_target_pairs={{0,2},{1,3},{2,0},{3,1},{4,6},{5,7},{6,4},{7,5},{8,10},{9,11},{10,... | collective-permute-start | bytes 245768 | tf_op jit(solution)/shard_map/ppermute | solution.py:746
  92.9 4.4 %collective-permute-start.2 = (f32[80,256]{1,0:T(8,128)S(1)}, f32[80,256]{1,0:T(8,128)S(1)}, u32[]{:S(2)}, u32[]{:S(2)}) collective-permute-start(f32[80,256]{1,0:T(8,128)S(1)} %get-tuple-element.22), channel_id=1, source_target_pairs={{0,3},{1,0},{2,1},{3,2},{4,7},{5,4},{6,5},{7,6},{8,11},{9,8},{10,9... | collective-permute-start | bytes 245768 | tf_op jit(solution)/shard_map/ppermute | solution.py:746

commit v5 on v4

--- a/solution.py
+++ b/solution.py
@@ -34,7 +34,7 @@
 log2_e = 1.0 / math.log(2.0)
 ln_2 = math.log(2.0)
 nt_dims = (((1,), (1,)), ((), ()))
-render_vmem_bytes = 48 * 1024 * 1024
+render_vmem_bytes = 36 * 1024 * 1024
 fields = 9
 
 
@@ -223,6 +223,33 @@
             requests_ref[owner, :, third * 128 : third * 128 + 128] = requests[row : row + 1]
 
 
+def rank_picks_kernel(rank_ref, at_rank_ref):
+    kept, capacity, _ = at_rank_ref.shape
+    blocks = rank_ref.shape[1] // 256
+    rank_rows = lax.broadcasted_iota(i32, (capacity, 256), 0)
+
+    def step(place, carry):
+        at = pl.multiple_of(place % blocks * 256, 256)
+        rank = rank_ref[pl.ds(place // blocks, 1), pl.ds(at, 256)]
+        at_rank_ref[place] = jnp.where(rank_rows == rank, 1.0, 0.0).astype(bf16)
+        return carry
+
+    lax.fori_loop(0, kept - 1, step, 0)
+    at_rank_ref[kept - 1] = jnp.zeros((capacity, 256), bf16)
+
+
+def asked_picks_kernel(asked_ref, pick_ref, *, group):
+    steps, _, width = pick_ref.shape
+    low_rows = lax.broadcasted_iota(i32, (256, width), 0)
+
+    def step(part, carry):
+        asked = jnp.concatenate([asked_ref[group * part + k] for k in range(group)], axis=1)
+        pick_ref[part] = jnp.where(low_rows == (asked & 255), 1.0, 0.0).astype(bf16)
+        return carry
+
+    lax.fori_loop(0, steps, step, 0)
+
+
 def lookup_kernel(asked_ref, table_ref, third_ref, found_ref, pick_ref, *, group):
     askers, _, capacity = asked_ref.shape
     rows = table_ref.shape[0] // fields
@@ -265,19 +292,17 @@
         choose(part, result, third)
 
 
-def collect_kernel(camera_ref, place_ref, asked_ref, returned_ref, *rest, rows, group):
-    *sums_refs, total_ref, pick_ref, placed_ref = rest
+def collect_kernel(camera_ref, place_ref, asked_ref, pick_ref, returned_ref, *rest, rows, group):
+    *sums_refs, total_ref, placed_ref = rest
     askers, _, capacity = asked_ref.shape
     views = len(sums_refs)
     width = group * capacity
     steps = askers // group
-    low_rows = lax.broadcasted_iota(i32, (256, width), 0)
     high_rows = lax.broadcasted_iota(i32, (rows, width), 0)
 
     def prepare(part):
         at = part % 2
         asked = jnp.concatenate([asked_ref[group * part + k] for k in range(group)], axis=1)
-        pick_ref[at] = jnp.where(low_rows == (asked & 255), 1.0, 0.0).astype(bf16)
         mask = high_rows == (asked >> 8)
         for field in range(fields):
             values = jnp.concatenate(
@@ -294,7 +319,7 @@
 
     def multiply(part):
         at = part % 2
-        pick = pick_ref[at]
+        pick = pick_ref[part]
         return lax.dot_general(
             placed_ref[at], jnp.concatenate([pick, pick], axis=1), nt_dims, preferred_element_type=f32
         )
@@ -320,7 +345,6 @@
 def collect_scratch(group, rows, capacity):
     return [
         pltpu.VMEM((fields * rows, 256), f32),
-        pltpu.VMEM((2, 256, group * capacity), bf16),
         pltpu.VMEM((2, fields * rows, 2 * group * capacity), bf16),
     ]
 
@@ -367,6 +391,7 @@
     place_ref,
     lists_ref,
     rank_ref,
+    at_rank_ref,
     fetched_ref,
     d_image_ref,
     image_ref,
@@ -382,12 +407,10 @@
     d_left_ref,
     earlier_ref,
     later_ref,
-    picture_ref,
     blend_ref,
     ratio_ref,
     color_grad_ref,
     placed_ref,
-    at_rank_ref,
     outgo_ref,
     *,
     shift,
@@ -431,7 +454,7 @@
         d_left_ref[tile] = jnp.concatenate([d_upper, d_lower, jnp.zeros((10, pixels), f32)], axis=0).astype(bf16)
     outgo_ref[...] = jnp.zeros_like(outgo_ref)
     placed_ref[spare] = jnp.zeros(placed_ref.shape[1:], bf16)
-    at_rank_ref[spare] = jnp.zeros(at_rank_ref.shape[1:], bf16)
+    blocks = slots // 256
     row_index = lax.broadcasted_iota(i32, (256, 256), 0)
     lane_index = lax.broadcasted_iota(i32, (256, 256), 1)
     before = (row_index < lane_index).astype(f32).astype(bf16)
@@ -444,8 +467,10 @@
     moments_of = monomial(
         lax.broadcasted_iota(i32, (16, pixels), 0), pixel_lane & 15, pixel_lane >> 4
     ).astype(bf16)
-    rank_rows = lax.broadcasted_iota(i32, (capacity, 256), 0)
     owner_rows = lax.broadcasted_iota(i32, (owners, 256), 0)
+
+    def place_of(item):
+        return item_ref[0, item] * blocks + item_ref[1, item]
 
     def owner_and_rank(item):
         tile = item_ref[0, item]
@@ -457,8 +482,7 @@
     def fetch(item):
         owner, rank = owner_and_rank(item)
         tile = item_ref[0, item]
-        at_rank = jnp.where(rank_rows == rank, 1.0, 0.0).astype(bf16)
-        at_rank_ref[item] = at_rank
+        at_rank = at_rank_ref[place_of(item)]
         yield
         fetched = jnp.dot(
             fetch_ref[...], jnp.concatenate([at_rank, at_rank], axis=0), preferred_element_type=f32
@@ -495,9 +519,7 @@
         yield
 
     def forward(item):
-        live = item >= 0
-        at = jnp.where(live, item, spare)
-        item = jnp.maximum(item, 0)
+        at = item
         tile = item_ref[0, item]
         first = item_ref[1, item] == 0
         exponent = jnp.dot(monomials, polynomial_ref[at], preferred_element_type=f32)
@@ -529,17 +551,13 @@
         one = lax.dot_general(color_left, upper, nt_dims, preferred_element_type=f32)
         two = lax.dot_general(color_left, lower, nt_dims, preferred_element_type=f32)
         picture = one[0:3] + one[3:6] + two[0:3]
-        at_tile = jnp.where(live, tile, tiles)
-        picture_ref[at_tile, 0:3] = jnp.where(first, 0.0, picture_ref[at_tile, 0:3]) + picture
+        image_ref[tile] = jnp.where(first, 0.0, image_ref[tile]) + picture
         yield
 
     def backward(step):
-        step = jnp.minimum(step, items)
-        live = step < items
-        at = jnp.where(live, item_ref[2, jnp.minimum(step, items - 1)], spare)
-        item = jnp.where(live, at, 0)
-        first = item_ref[1, jnp.minimum(step, items - 1)] == 0
-        owner, rank = owner_and_rank(item)
+        at = item_ref[2, step]
+        first = item_ref[1, step] == 0
+        owner, rank = owner_and_rank(at)
         blend = blend_ref[at]
         upper, lower = split_two(blend)
         within = jnp.dot(upper, after, preferred_element_type=f32) + jnp.dot(
@@ -579,9 +597,10 @@
 
     def send(item):
         at = jnp.where(item < 0, spare, item)
+        place = jnp.where(item < 0, spare, place_of(jnp.maximum(item, 0)))
         outgo_ref[...] += lax.dot_general(
             placed_ref[at],
-            jnp.concatenate([at_rank_ref[at], at_rank_ref[at]], axis=1),
+            jnp.concatenate([at_rank_ref[place], at_rank_ref[place]], axis=1),
             nt_dims,
             preferred_element_type=f32,
         )
@@ -590,7 +609,7 @@
     def send_step(step):
         return send(jnp.where(step < 0, -1, item_ref[2, jnp.maximum(step, 0)]))
 
-    lag = 6
+    lag = 5
 
     def run(order, **stages):
         for name in order:
@@ -605,7 +624,7 @@
 
     def steady(step, carry):
         run(
-            "mbmsfmbfmfbmbff",
+            "bmmsfmbfmfbmbff",
             s=send_step(step - lag - 1),
             b=backward(step - lag),
             m=forward(step - 1),
@@ -617,19 +636,19 @@
         run("bsbbb", s=send_step(step - lag - 1), b=backward(step - lag))
         return carry
 
-    lax.fori_loop(0, lag, ramp_up, 0)
+    run("fffff", f=fetch(0))
+    lax.fori_loop(1, lag, ramp_up, 0)
     lax.fori_loop(lag, items, steady, 0)
     run("mbsmmbmbmb", s=send_step(items - lag - 1), b=backward(items - lag), m=forward(items - 1))
-    lax.fori_loop(items + 1, items + lag + 1, ramp_down, 0)
-    for tile in range(tiles):
-        image_ref[tile] = picture_ref[tile, 0:3]
+    lax.fori_loop(items + 1, items + lag, ramp_down, 0)
+    run("s", s=send_step(items - 1))
     for owner in range(owners):
         for field in range(fields):
             row = field * owners + owner
             outgoing_ref[owner, :, field * capacity : (field + 1) * capacity] = outgo_ref[row : row + 1, :]
 
 
-def render_call(counts, tile_row, lists, rank, fetched, d_image, shift):
+def render_call(counts, tile_row, lists, rank, at_rank, fetched, d_image, shift):
     owners, _, width = fetched.shape
     capacity = width // fields
     tiles, slots = lists.shape
@@ -643,7 +662,7 @@
             jax.ShapeDtypeStruct((tiles, 3, pixels), f32),
             jax.ShapeDtypeStruct((owners, 1, fields * capacity), f32),
         ),
-        in_specs=[smem, smem, vmem, vmem, vmem, vmem],
+        in_specs=[smem, smem, vmem, vmem, vmem, vmem, vmem],
         out_specs=(vmem, vmem),
         scratch_shapes=[
             pltpu.SMEM((3, kept), i32),
@@ -657,17 +676,15 @@
             pltpu.VMEM((tiles, 16, pixels), bf16),
             pltpu.VMEM((pixels, 128), f32),
             pltpu.VMEM((pixels, 128), f32),
-            pltpu.VMEM((tiles + 1, 8, pixels), f32),
             pltpu.VMEM((kept, pixels, 256), f32),
             pltpu.VMEM((kept, pixels, 256), f32),
             pltpu.VMEM((kept, 8, 256), f32),
             pltpu.VMEM((kept, fields * owners, 512), bf16),
-            pltpu.VMEM((kept, capacity, 256), bf16),
             pltpu.VMEM((fields * owners, capacity), f32),
         ],
         compiler_params=pltpu.CompilerParams(vmem_limit_bytes=render_vmem_bytes),
         name="render",
-    )(counts, tile_row, lists, rank, fetched, d_image)
+    )(counts, tile_row, lists, rank, at_rank, fetched, d_image)
 
 
 def body(params, camera, tile_lists, tile_counts, d_image):
@@ -730,18 +747,36 @@
         compiler_params=settings(16),
         name="lookup",
     )(asked, table, third)
+    late_rank, found = lax.optimization_barrier((rank, found))
     fetched = lax.all_to_all(found, "tiles", split_axis=0, concat_axis=0, tiled=True)
-    picture, outgoing = render_call(counts, tile_row, lists, rank, fetched, d_image[0], shift)
+    at_rank = pl.pallas_call(
+        rank_picks_kernel,
+        out_shape=jax.ShapeDtypeStruct((tiles * slots // 256 + 1, capacity, 256), bf16),
+        in_specs=[vmem],
+        out_specs=vmem,
+        compiler_params=settings(16),
+        name="rank_picks",
+    )(late_rank)
+    picture, outgoing = render_call(counts, tile_row, lists, rank, at_rank, fetched, d_image[0], shift)
+    late_asked, outgoing = lax.optimization_barrier((asked, outgoing))
+    asked_pick = pl.pallas_call(
+        functools.partial(asked_picks_kernel, group=2),
+        out_shape=jax.ShapeDtypeStruct((owners // 2, 256, 2 * capacity), bf16),
+        in_specs=[vmem],
+        out_specs=vmem,
+        compiler_params=settings(16),
+        name="asked_picks",
+    )(late_asked)
     returned = lax.all_to_all(outgoing, "tiles", split_axis=0, concat_axis=0, tiled=True)
     sums = pl.pallas_call(
         functools.partial(collect_kernel, rows=rows, group=2),
         out_shape=[jax.ShapeDtypeStruct((fields * part_rows + 8, 256), f32)] * views,
-        in_specs=[smem, smem, vmem, vmem],
+        in_specs=[smem, smem, vmem, vmem, vmem],
         out_specs=[vmem] * views,
         scratch_shapes=collect_scratch(2, rows, capacity),
         compiler_params=settings(16),
         name="collect",
-    )(camera_row, view_here, asked, returned)
+    )(camera_row, view_here, asked, asked_pick, returned)
     all_sums = [sums[0]] + [
         lax.ppermute(sums[offset], "views", [(view, (view + offset) % views) for view in range(views)])
         for offset in range(1, views)

time: 101 us -> 104 us (1.030); the launches traced: 99.1 us -> 104 us
  blocking collectives: 16.8 us -> 0 us
  local copies, waits for them, and re-layouts: 2.96 us -> 15.4 us
  starting transfers between devices: 21.1 us -> 28.5 us
  waiting for transfers between devices: 14.6 us -> 16.1 us
    all_to_all x1 -> x0, blocking collectives: 16.8 us -> none  [body(): lax.all_to_all(outgoing, 'tiles', split_axis=0, concat_axis=0, tiled=True)]
    unnamed x12 -> x20, local copies, waits for them, and re-layouts: 2.24 us -> 14.7 us
    all_to_all x0 -> x1, starting transfers between devices: none -> 9.36 us  [body(): lax.all_to_all(outgoing, 'tiles', split_axis=0, concat_axis=0, tiled=True)]
    all_to_all x0 -> x1, waiting for transfers between devices: none -> 7.01 us  [body(): lax.all_to_all(outgoing, 'tiles', split_axis=0, concat_axis=0, tiled=True)]
    all_to_all x1, waiting for transfers between devices: 10.8 us -> 5.16 us  [body(): lax.all_to_all(found, 'tiles', split_axis=0, concat_axis=0, tiled=True)]
    pallas_call x0 -> x2, Pallas kernels: none -> 2.53 us  [the longest x1 1.41 us: body(): pl.pallas_call(rank_picks_kernel, out_shape=jax.ShapeDtypeStruct((tiles *...]
    pallas_call x1, Pallas kernels: 22.7 us -> 20.5 us  [render_call(): pl.pallas_call(functools.partial(render_kernel, shift=shift), out_shape=(...]
    ppermute x3, starting transfers between devices: 5.82 us -> 3.87 us  [body(): lax.ppermute(sums[offset], 'views', [(view, (view + offset) % views) for...]
  transfers between devices with their start and end apart: 5 -> 6, of which waited for: 4 -> 6; matrix products, arithmetic and copies ran while one was open for 2% -> 3% of each run, Pallas kernels for 2% -> 4%
where the time goes in v5:
time: 104 us
  Pallas kernels  40.7 us (39%)
  starting transfers between devices  28.5 us (27%)
  waiting for transfers between devices  16.1 us (15%)
  local copies, waits for them, and re-layouts  15.4 us (15%)
  between operations  2.2 us (2%)
    pallas_call x1, Pallas kernels, render_call(): pl.pallas_call(functools.partial(render_kernel, shift=shift), out_shape=(...  20.5 us
    unnamed x20, local copies, waits for them, and re-layouts  14.7 us
    all_to_all x1, starting transfers between devices, body(): lax.all_to_all(outgoing, 'tiles', split_axis=0, concat_axis=0, tiled=True)  9.36 us
    all_to_all x1, starting transfers between devices, body(): lax.all_to_all(requests, 'tiles', split_axis=0, concat_axis=0, tiled=True)  8.72 us
    all_to_all x1, waiting for transfers between devices, body(): lax.all_to_all(outgoing, 'tiles', split_axis=0, concat_axis=0, tiled=True)  7.01 us
    all_to_all x1, starting transfers between devices, body(): lax.all_to_all(found, 'tiles', split_axis=0, concat_axis=0, tiled=True)  6.58 us
    pallas_call x1, Pallas kernels, body(): pl.pallas_call(functools.partial(lookup_kernel, group=2), out_shape=jax.S...  6.12 us
    all_to_all x1, waiting for transfers between devices, body(): lax.all_to_all(found, 'tiles', split_axis=0, concat_axis=0, tiled=True)  5.16 us
  transfers between devices with their start and end apart: 6, of which 6 were waited for; matrix products, arithmetic and copies ran while one was open for 3% of the time, Pallas kernels for 4%

profile of v5, /device:TPU:1, one launch (start us, length us, event | category | flops | bytes accessed | tf_op | source)
XLA Modules:
  0.0 103.7 jit_solution(16766336261104611132)
XLA Ops:
  0.6 0.0 copy-start.8
  0.6 0.0 copy-start.7
  0.6 3.3 %bucket.1 = (s32[32,1,384]{2,1,0:T(1,128)}, s32[8,1024]{1,0:T(8,128)}) custom-call(s32[8]{0:T(128)} %bitcast.17, s32[8,1024]{1,0:T(8,128)} %bitcast.14), custom_call_target="tpu_custom_call" | custom-call | tf_op jit(solution)/shard_map/bucket/pallas_call | solution.py:712
  3.9 8.7 %all-to-all-start = ((s32[32,1,384]{2,1,0:T(1,128)}), s32[32,1,384]{2,1,0:T(1,128)S(1)}, u32[]{:S(2)}, u32[]{:S(2)}) async-start(s32[32,1,384]{2,1,0:T(1,128)} %get-tuple-element.18), calls=%async_computation | async-start | bytes 98304 | tf_op jit(solution)/shard_map/all_to_all | solution.py:727
  14.1 0.7 slice_bitcast_fusion
  14.8 0.7 pad_maximum_fusion.camera_ref
  15.5 1.6 %copy-done.4 = f32[59,8192]{1,0:T(8,128)S(1)} copy-done((f32[59,8192]{1,0:T(8,128)S(1)}, f32[59,8192]{1,0:T(8,128)}, u32[]{:S(2)}) %copy-start.4) | copy-done | bytes 1933336
  17.1 2.0 %project.1 = (bf16[288,512]{1,0:T(8,128)(2,1)S(1)}, bf16[64,256]{1,0:T(8,128)(2,1)S(1)}, f32[59,8,256]{2,1,0:T(8,128)S(1)}) custom-call(f32[8]{0:T(128)S(1)} %pad_maximum_fusion.camera_ref, s32[1]{0:T(128)} %bitcast.6.place_ref, f32[59,8192]{1,0:T(8,128)S(1)} %copy-done.4), custom_call_target="tpu_custom_call" | custom-call | tf_op jit(solution)/shard_map/project/pallas_call | solution.py:728
  19.1 0.8 all-to-all-done.asked_ref
  20.0 6.1 %lookup.1 = f32[32,1,3456]{2,1,0:T(1,128)} custom-call(s32[32,1,384]{2,1,0:T(1,128)S(1)} %all-to-all-done.asked_ref, bf16[288,512]{1,0:T(8,128)(2,1)S(1)} %get-tuple-element.19.table_ref, bf16[64,256]{1,0:T(8,128)(2,1)S(1)} %get-tuple-element.20.third_ref), custom_call_target="tpu_custom_call" | custom-call | tf_op jit(solution)/shard_map/lookup/pallas_call | solution.py:741
  26.1 6.6 %all-to-all-start.1 = ((f32[32,1,3456]{2,1,0:T(1,128)}), f32[32,1,3456]{2,1,0:T(1,128)S(1)}, u32[]{:S(2)}, u32[]{:S(2)}) async-start(f32[32,1,3456]{2,1,0:T(1,128)} %lookup.1), calls=%async_computation.1 | async-start | bytes 884736 | tf_op jit(solution)/shard_map/all_to_all | solution.py:751
  32.7 0.8 copy.11
  33.4 0.7 copy-done.5
  34.2 1.4 %rank_picks.1.at_rank_ref = bf16[33,384,256]{2,1,0:T(8,128)(2,1)S(1)} custom-call(s32[8,1024]{1,0:T(8,128)S(1)} %copy-done.5), custom_call_target="tpu_custom_call" | custom-call | tf_op jit(solution)/shard_map/rank_picks/pallas_call | solution.py:752
  35.6 2.7 %copy-done = bf16[33,384,256]{2,1,0:T(8,128)(2,1)} copy-done((bf16[33,384,256]{2,1,0:T(8,128)(2,1)}, bf16[33,384,256]{2,1,0:T(8,128)(2,1)S(1)}, u32[]{:S(2)}) %copy-start) | copy-done | bytes 6488088
  38.3 5.2 %all-to-all-done.1.fetched_ref = f32[32,1,3456]{2,1,0:T(1,128)S(1)} async-done(((f32[32,1,3456]{2,1,0:T(1,128)}), f32[32,1,3456]{2,1,0:T(1,128)S(1)}, u32[]{:S(2)}, u32[]{:S(2)}) %all-to-all-start.1) | async-done | bytes 442400 | tf_op jit(solution)/shard_map/all_to_all | solution.py:751
  43.5 2.8 %copy-done.1 = bf16[33,384,256]{2,1,0:T(8,128)(2,1)S(1)} copy-done((bf16[33,384,256]{2,1,0:T(8,128)(2,1)S(1)}, bf16[33,384,256]{2,1,0:T(8,128)(2,1)}, u32[]{:S(2)}) %copy-start.1) | copy-done | bytes 6488088
  46.3 20.5 %render.1 = (f32[8,3,256]{2,1,0:T(4,128)S(1)}, f32[32,1,3456]{2,1,0:T(1,128)}) custom-call(s32[8]{0:T(128)S(1)} %bitcast.18, s32[1]{0:T(128)} %bitcast.1.place_ref, s32[8,1024]{1,0:T(8,128)S(1)} %bitcast.15, s32[8,1024]{1,0:T(8,128)S(1)} %copy-done.6, bf16[33,384,256]{2,1,0:T(8,128)(2,1)S(1)} %copy-done.1, f32[32,1,3456]{2,1,0:T(1,128)S(1)} %all-to-all-done.1.fetched_ref, ...), custom_call_target="tpu_custom_call" | custom-call | tf_op jit(solution)/shard_map/render/pallas_call | solution.py:659
  66.8 9.4 %all-to-all-start.2 = ((f32[32,1,3456]{2,1,0:T(1,128)}), f32[32,1,3456]{2,1,0:T(1,128)S(1)}, u32[]{:S(2)}, u32[]{:S(2)}) async-start(f32[32,1,3456]{2,1,0:T(1,128)} %get-tuple-element.26), calls=%async_computation.2 | async-start | bytes 884736 | tf_op jit(solution)/shard_map/all_to_all | solution.py:770
  76.2 1.1 %asked_picks.1.pick_ref = bf16[16,256,768]{2,1,0:T(8,128)(2,1)S(1)} custom-call(s32[32,1,384]{2,1,0:T(1,128)S(1)} %all-to-all-done.asked_ref), custom_call_target="tpu_custom_call" | custom-call | tf_op jit(solution)/shard_map/asked_picks/pallas_call | solution.py:762
  77.3 2.7 %copy-done.2 = bf16[16,256,768]{2,1,0:T(8,128)(2,1)} copy-done((bf16[16,256,768]{2,1,0:T(8,128)(2,1)}, bf16[16,256,768]{2,1,0:T(8,128)(2,1)S(1)}, u32[]{:S(2)}) %copy-start.2) | copy-done | bytes 6291480
  80.0 7.0 %all-to-all-done.2.returned_ref = f32[32,1,3456]{2,1,0:T(1,128)S(1)} async-done(((f32[32,1,3456]{2,1,0:T(1,128)}), f32[32,1,3456]{2,1,0:T(1,128)S(1)}, u32[]{:S(2)}, u32[]{:S(2)}) %all-to-all-start.2) | async-done | bytes 442400 | tf_op jit(solution)/shard_map/all_to_all | solution.py:770
  87.0 2.8 %copy-done.3 = bf16[16,256,768]{2,1,0:T(8,128)(2,1)S(1)} copy-done((bf16[16,256,768]{2,1,0:T(8,128)(2,1)S(1)}, bf16[16,256,768]{2,1,0:T(8,128)(2,1)}, u32[]{:S(2)}) %copy-start.3) | copy-done | bytes 6291480
  89.8 4.5 %collect.1 = (f32[80,256]{1,0:T(8,128)S(1)}, f32[80,256]{1,0:T(8,128)S(1)}, f32[80,256]{1,0:T(8,128)S(1)}, f32[80,256]{1,0:T(8,128)S(1)}) custom-call(f32[8]{0:T(128)S(1)} %pad_maximum_fusion.camera_ref, s32[1]{0:T(128)} %bitcast.6.place_ref, s32[32,1,384]{2,1,0:T(1,128)S(1)} %all-to-all-done.asked_ref, bf16[16,256,768]{2,1,0:T(8,128)(2,1)S(1)} %copy-done.3, ...), custom_call_target="tpu_custom_call" | custom-call | tf_op jit(solution)/shard_map/collect/pallas_call | solution.py:771
  94.3 0.1 collective-permute-start
  94.4 2.7 %collective-permute-start.1 = (f32[80,256]{1,0:T(8,128)S(1)}, f32[80,256]{1,0:T(8,128)S(1)}, u32[]{:S(2)}, u32[]{:S(2)}) collective-permute-start(f32[80,256]{1,0:T(8,128)S(1)} %get-tuple-element.29), channel_id=1, source_target_pairs={{0,2},{1,3},{2,0},{3,1},{4,6},{5,7},{6,4},{7,5},{8,10},{9,11},{10,... | collective-permute-start | bytes 245768 | tf_op jit(solution)/shard_map/ppermute | solution.py:781
  97.1 1.1 %collective-permute-start.2 = (f32[80,256]{1,0:T(8,128)S(1)}, f32[80,256]{1,0:T(8,128)S(1)}, u32[]{:S(2)}, u32[]{:S(2)}) collective-permute-start(f32[80,256]{1,0:T(8,128)S(1)} %get-tuple-element.30), channel_id=1, source_target_pairs={{0,3},{1,0},{2,1},{3,2},{4,7},{5,4},{6,5},{7,6},{8,11},{9,8},{10,9... | collective-permute-start | bytes 245768 | tf_op jit(solution)/shard_map/ppermute | solution.py:781
  98.2 0.6 copy.9
  98.8 1.0 collective-permute-done.refs_1_
  99.7 1.8 %collective-permute-done.1.refs_2_ = f32[80,256]{1,0:T(8,128)S(1)} collective-permute-done((f32[80,256]{1,0:T(8,128)S(1)}, f32[80,256]{1,0:T(8,128)S(1)}, u32[]{:S(2)}, u32[]{:S(2)}) %collective-permute-start.1) | collective-permute-done | bytes 81952 | tf_op jit(solution)/shard_map/ppermute | solution.py:781
  101.5 0.4 collective-permute-done.2.refs_3_
  101.9 1.8 %pull.1 = f32[59,2048]{1,0:T(8,128)} custom-call(f32[80,256]{1,0:T(8,128)S(1)} %get-tuple-element.27.refs_0_, f32[80,256]{1,0:T(8,128)S(1)} %collective-permute-done.refs_1_, f32[80,256]{1,0:T(8,128)S(1)} %collective-permute-done.1.refs_2_, f32[80,256]{1,0:T(8,128)S(1)} %collective-permute-done.2.refs_3_, f32[59,8,256]{2,1,0:T(8,128)S(1)} %get-tuple-element.31.refs_4_), custom_call_target="tpu_custom_call" | custom-call | tf_op jit(solution)/shard_map/pull/pallas_call | solution.py:784
  (10 shorter events, 0.0 us)
Async XLA Ops:
  0.6 42.8 %copy-start.8 = (s32[1,8]{1,0:T(1,128)S(1)}, s32[1,8]{1,0:T(1,128)}, u32[]{:S(2)}) copy-start(s32[1,8]{1,0:T(1,128)} %param.9) | copy-start | bytes 100
  0.6 42.8 %copy-start.7 = (s32[1,8,1024]{2,1,0:T(8,128)S(1)}, s32[1,8,1024]{2,1,0:T(8,128)}, u32[]{:S(2)}) copy-start(s32[1,8,1024]{2,1,0:T(8,128)} %param.8) | copy-start | bytes 98308
  3.9 39.6 %copy-start.6 = (s32[8,1024]{1,0:T(8,128)S(1)}, s32[8,1024]{1,0:T(8,128)}, u32[]{:S(2)}) copy-start(s32[8,1024]{1,0:T(8,128)} %get-tuple-element.21.rank_ref) | copy-start | bytes 98308
  3.9 16.0 %all-to-all-start = ((s32[32,1,384]{2,1,0:T(1,128)}), s32[32,1,384]{2,1,0:T(1,128)S(1)}, u32[]{:S(2)}, u32[]{:S(2)}) async-start(s32[32,1,384]{2,1,0:T(1,128)} %get-tuple-element.18), calls=%async_computation | async-start | bytes 98304 | tf_op jit(solution)/shard_map/all_to_all | solution.py:727
  15.5 1.6 %copy-start.4 = (f32[59,8192]{1,0:T(8,128)S(1)}, f32[59,8192]{1,0:T(8,128)}, u32[]{:S(2)}) copy-start(f32[59,8192]{1,0:T(8,128)} %params_ref.1) | copy-start | bytes 5799940
  26.1 17.4 %all-to-all-start.1 = ((f32[32,1,3456]{2,1,0:T(1,128)}), f32[32,1,3456]{2,1,0:T(1,128)S(1)}, u32[]{:S(2)}, u32[]{:S(2)}) async-start(f32[32,1,3456]{2,1,0:T(1,128)} %lookup.1), calls=%async_computation.1 | async-start | bytes 884736 | tf_op jit(solution)/shard_map/all_to_all | solution.py:751
  33.4 0.8 copy-start.5
  35.6 2.7 %copy-start = (bf16[33,384,256]{2,1,0:T(8,128)(2,1)}, bf16[33,384,256]{2,1,0:T(8,128)(2,1)S(1)}, u32[]{:S(2)}) copy-start(bf16[33,384,256]{2,1,0:T(8,128)(2,1)S(1)} %rank_picks.1.at_rank_ref) | copy-start | bytes 19464196
  43.5 2.8 %copy-start.1 = (bf16[33,384,256]{2,1,0:T(8,128)(2,1)S(1)}, bf16[33,384,256]{2,1,0:T(8,128)(2,1)}, u32[]{:S(2)}) copy-start(bf16[33,384,256]{2,1,0:T(8,128)(2,1)} %copy-done) | copy-start | bytes 19464196
  66.8 20.2 %all-to-all-start.2 = ((f32[32,1,3456]{2,1,0:T(1,128)}), f32[32,1,3456]{2,1,0:T(1,128)S(1)}, u32[]{:S(2)}, u32[]{:S(2)}) async-start(f32[32,1,3456]{2,1,0:T(1,128)} %get-tuple-element.26), calls=%async_computation.2 | async-start | bytes 884736 | tf_op jit(solution)/shard_map/all_to_all | solution.py:770
  77.3 2.7 %copy-start.2 = (bf16[16,256,768]{2,1,0:T(8,128)(2,1)}, bf16[16,256,768]{2,1,0:T(8,128)(2,1)S(1)}, u32[]{:S(2)}) copy-start(bf16[16,256,768]{2,1,0:T(8,128)(2,1)S(1)} %asked_picks.1.pick_ref) | copy-start | bytes 18874372
  87.0 2.8 %copy-start.3 = (bf16[16,256,768]{2,1,0:T(8,128)(2,1)S(1)}, bf16[16,256,768]{2,1,0:T(8,128)(2,1)}, u32[]{:S(2)}) copy-start(bf16[16,256,768]{2,1,0:T(8,128)(2,1)} %copy-done.2) | copy-start | bytes 18874372
  94.3 5.4 %collective-permute-start = (f32[80,256]{1,0:T(8,128)S(1)}, f32[80,256]{1,0:T(8,128)S(1)}, u32[]{:S(2)}, u32[]{:S(2)}) collective-permute-start(f32[80,256]{1,0:T(8,128)S(1)} %get-tuple-element.28), channel_id=1, source_target_pairs={{0,1},{1,2},{2,3},{3,0},{4,5},{5,6},{6,7},{7,4},{8,9},{9,10},{10,1... | collective-permute-start | bytes 245768 | tf_op jit(solution)/shard_map/ppermute | solution.py:781
  94.4 7.2 %collective-permute-start.1 = (f32[80,256]{1,0:T(8,128)S(1)}, f32[80,256]{1,0:T(8,128)S(1)}, u32[]{:S(2)}, u32[]{:S(2)}) collective-permute-start(f32[80,256]{1,0:T(8,128)S(1)} %get-tuple-element.29), channel_id=1, source_target_pairs={{0,2},{1,3},{2,0},{3,1},{4,6},{5,7},{6,4},{7,5},{8,10},{9,11},{10,... | collective-permute-start | bytes 245768 | tf_op jit(solution)/shard_map/ppermute | solution.py:781
  97.1 4.8 %collective-permute-start.2 = (f32[80,256]{1,0:T(8,128)S(1)}, f32[80,256]{1,0:T(8,128)S(1)}, u32[]{:S(2)}, u32[]{:S(2)}) collective-permute-start(f32[80,256]{1,0:T(8,128)S(1)} %get-tuple-element.30), channel_id=1, source_target_pairs={{0,3},{1,0},{2,1},{3,2},{4,7},{5,4},{6,5},{7,6},{8,11},{9,8},{10,9... | collective-permute-start | bytes 245768 | tf_op jit(solution)/shard_map/ppermute | solution.py:781

commit v6 on v4

--- a/solution.py
+++ b/solution.py
@@ -382,7 +382,6 @@
     d_left_ref,
     earlier_ref,
     later_ref,
-    picture_ref,
     blend_ref,
     ratio_ref,
     color_grad_ref,
@@ -495,9 +494,7 @@
         yield
 
     def forward(item):
-        live = item >= 0
-        at = jnp.where(live, item, spare)
-        item = jnp.maximum(item, 0)
+        at = item
         tile = item_ref[0, item]
         first = item_ref[1, item] == 0
         exponent = jnp.dot(monomials, polynomial_ref[at], preferred_element_type=f32)
@@ -529,17 +526,13 @@
         one = lax.dot_general(color_left, upper, nt_dims, preferred_element_type=f32)
         two = lax.dot_general(color_left, lower, nt_dims, preferred_element_type=f32)
         picture = one[0:3] + one[3:6] + two[0:3]
-        at_tile = jnp.where(live, tile, tiles)
-        picture_ref[at_tile, 0:3] = jnp.where(first, 0.0, picture_ref[at_tile, 0:3]) + picture
+        image_ref[tile] = jnp.where(first, 0.0, image_ref[tile]) + picture
         yield
 
     def backward(step):
-        step = jnp.minimum(step, items)
-        live = step < items
-        at = jnp.where(live, item_ref[2, jnp.minimum(step, items - 1)], spare)
-        item = jnp.where(live, at, 0)
-        first = item_ref[1, jnp.minimum(step, items - 1)] == 0
-        owner, rank = owner_and_rank(item)
+        at = item_ref[2, step]
+        first = item_ref[1, step] == 0
+        owner, rank = owner_and_rank(at)
         blend = blend_ref[at]
         upper, lower = split_two(blend)
         within = jnp.dot(upper, after, preferred_element_type=f32) + jnp.dot(
@@ -590,7 +583,7 @@
     def send_step(step):
         return send(jnp.where(step < 0, -1, item_ref[2, jnp.maximum(step, 0)]))
 
-    lag = 6
+    lag = 5
 
     def run(order, **stages):
         for name in order:
@@ -605,7 +598,7 @@
 
     def steady(step, carry):
         run(
-            "mbmsfmbfmfbmbff",
+            "bmmsfmbfmfbmbff",
             s=send_step(step - lag - 1),
             b=backward(step - lag),
             m=forward(step - 1),
@@ -617,12 +610,12 @@
         run("bsbbb", s=send_step(step - lag - 1), b=backward(step - lag))
         return carry
 
-    lax.fori_loop(0, lag, ramp_up, 0)
+    run("fffff", f=fetch(0))
+    lax.fori_loop(1, lag, ramp_up, 0)
     lax.fori_loop(lag, items, steady, 0)
     run("mbsmmbmbmb", s=send_step(items - lag - 1), b=backward(items - lag), m=forward(items - 1))
-    lax.fori_loop(items + 1, items + lag + 1, ramp_down, 0)
-    for tile in range(tiles):
-        image_ref[tile] = picture_ref[tile, 0:3]
+    lax.fori_loop(items + 1, items + lag, ramp_down, 0)
+    run("s", s=send_step(items - 1))
     for owner in range(owners):
         for field in range(fields):
             row = field * owners + owner
@@ -657,7 +650,6 @@
             pltpu.VMEM((tiles, 16, pixels), bf16),
             pltpu.VMEM((pixels, 128), f32),
             pltpu.VMEM((pixels, 128), f32),
-            pltpu.VMEM((tiles + 1, 8, pixels), f32),
             pltpu.VMEM((kept, pixels, 256), f32),
             pltpu.VMEM((kept, pixels, 256), f32),
             pltpu.VMEM((kept, 8, 256), f32),

time: 101 us -> 98.3 us (0.973); the launches traced: 99.1 us -> 98.1 us
  blocking collectives: 16.8 us -> 14.3 us
  Pallas kernels: 40.8 us -> 43.1 us
  starting transfers between devices: 21.1 us -> 19.8 us
    all_to_all x1, blocking collectives: 16.8 us -> 14.3 us  [body(): lax.all_to_all(outgoing, 'tiles', split_axis=0, concat_axis=0, tiled=True)]
    pallas_call x1, Pallas kernels: 22.7 us -> 25.1 us  [render_call(): pl.pallas_call(functools.partial(render_kernel, shift=shift), out_shape=(...]
    ppermute x3, starting transfers between devices: 5.82 us -> 4.47 us  [body(): lax.ppermute(sums[offset], 'views', [(view, (view + offset) % views) for...]
where the time goes in v6:
time: 98.3 us; the launch traced here: 98.1 us
  Pallas kernels  43.1 us (44%)
  starting transfers between devices  19.8 us (20%)
  waiting for transfers between devices  15 us (15%)
  blocking collectives  14.3 us (15%)
  local copies, waits for them, and re-layouts  2.96 us (3%)
  between operations  2.16 us (2%)
    pallas_call x1, Pallas kernels, render_call(): pl.pallas_call(functools.partial(render_kernel, shift=shift), out_shape=(...  25.1 us
    all_to_all x1, blocking collectives, body(): lax.all_to_all(outgoing, 'tiles', split_axis=0, concat_axis=0, tiled=True)  14.3 us
    all_to_all x1, waiting for transfers between devices, body(): lax.all_to_all(found, 'tiles', split_axis=0, concat_axis=0, tiled=True)  10.8 us
    all_to_all x1, starting transfers between devices, body(): lax.all_to_all(requests, 'tiles', split_axis=0, concat_axis=0, tiled=True)  8.72 us
    all_to_all x1, starting transfers between devices, body(): lax.all_to_all(found, 'tiles', split_axis=0, concat_axis=0, tiled=True)  6.59 us
    pallas_call x1, Pallas kernels, body(): pl.pallas_call(functools.partial(lookup_kernel, group=2), out_shape=jax.S...  6.13 us
    pallas_call x1, Pallas kernels, body(): pl.pallas_call(functools.partial(collect_kernel, rows=rows, group=2), out...  4.9 us
    ppermute x3, starting transfers between devices, body(): lax.ppermute(sums[offset], 'views', [(view, (view + offset) % views) for...  4.47 us
  transfers between devices with their start and end apart: 5, of which 4 were waited for; matrix products, arithmetic and copies ran while one was open for 2% of the time, Pallas kernels for 2%

profile of v6, /device:TPU:1, one launch (start us, length us, event | category | flops | bytes accessed | tf_op | source)
XLA Modules:
  0.0 98.1 jit_solution(1991000182709401139)
XLA Ops:
  0.6 0.0 copy-start.3
  0.6 0.0 copy-start.1
  0.7 0.0 copy-start.4
  0.7 3.2 %bucket.1 = (s32[32,1,384]{2,1,0:T(1,128)}, s32[8,1024]{1,0:T(8,128)}) custom-call(s32[8]{0:T(128)} %bitcast.17, s32[8,1024]{1,0:T(8,128)} %bitcast.14), custom_call_target="tpu_custom_call" | custom-call | tf_op jit(solution)/shard_map/bucket/pallas_call | solution.py:687
  3.9 0.0 copy-start.2
  3.9 8.7 %all-to-all-start = ((s32[32,1,384]{2,1,0:T(1,128)}), s32[32,1,384]{2,1,0:T(1,128)S(1)}, u32[]{:S(2)}, u32[]{:S(2)}) async-start(s32[32,1,384]{2,1,0:T(1,128)} %get-tuple-element.14), calls=%async_computation | async-start | bytes 98304 | tf_op jit(solution)/shard_map/all_to_all | solution.py:702
  14.1 0.7 slice_bitcast_fusion
  14.8 0.7 pad_maximum_fusion.camera_ref
  15.5 0.0 copy-start
  15.5 1.6 %copy-done = f32[59,8192]{1,0:T(8,128)S(1)} copy-done((f32[59,8192]{1,0:T(8,128)S(1)}, f32[59,8192]{1,0:T(8,128)}, u32[]{:S(2)}) %copy-start) | copy-done | bytes 1933336
  17.1 2.0 %project.1 = (bf16[288,512]{1,0:T(8,128)(2,1)S(1)}, bf16[64,256]{1,0:T(8,128)(2,1)S(1)}, f32[59,8,256]{2,1,0:T(8,128)S(1)}) custom-call(f32[8]{0:T(128)S(1)} %pad_maximum_fusion.camera_ref, s32[1]{0:T(128)} %bitcast.6.place_ref, f32[59,8192]{1,0:T(8,128)S(1)} %copy-done), custom_call_target="tpu_custom_call" | custom-call | tf_op jit(solution)/shard_map/project/pallas_call | solution.py:703
  19.1 0.8 all-to-all-done.asked_ref
  20.0 6.1 %lookup.1 = f32[32,1,3456]{2,1,0:T(1,128)} custom-call(s32[32,1,384]{2,1,0:T(1,128)S(1)} %all-to-all-done.asked_ref, bf16[288,512]{1,0:T(8,128)(2,1)S(1)} %get-tuple-element.15.table_ref, bf16[64,256]{1,0:T(8,128)(2,1)S(1)} %get-tuple-element.16.third_ref), custom_call_target="tpu_custom_call" | custom-call | tf_op jit(solution)/shard_map/lookup/pallas_call | solution.py:716
  26.1 6.6 %all-to-all-start.1 = ((f32[32,1,3456]{2,1,0:T(1,128)}), f32[32,1,3456]{2,1,0:T(1,128)S(1)}, u32[]{:S(2)}, u32[]{:S(2)}) async-start(f32[32,1,3456]{2,1,0:T(1,128)} %lookup.1), calls=%async_computation.1 | async-start | bytes 884736 | tf_op jit(solution)/shard_map/all_to_all | solution.py:725
  32.7 0.0 copy-done.4
  32.7 10.8 %all-to-all-done.1.fetched_ref = f32[32,1,3456]{2,1,0:T(1,128)S(1)} async-done(((f32[32,1,3456]{2,1,0:T(1,128)}), f32[32,1,3456]{2,1,0:T(1,128)S(1)}, u32[]{:S(2)}, u32[]{:S(2)}) %all-to-all-start.1) | async-done | bytes 442400 | tf_op jit(solution)/shard_map/all_to_all | solution.py:725
  43.5 0.0 copy-done.3
  43.5 0.0 copy-done.1
  43.5 0.0 copy-done.2
  43.5 25.1 %render.1 = (f32[8,3,256]{2,1,0:T(4,128)S(1)}, f32[32,1,3456]{2,1,0:T(1,128)S(1)}) custom-call(s32[8]{0:T(128)S(1)} %bitcast.18, s32[1]{0:T(128)} %bitcast.1.place_ref, s32[8,1024]{1,0:T(8,128)S(1)} %bitcast.15, s32[8,1024]{1,0:T(8,128)S(1)} %copy-done.2, f32[32,1,3456]{2,1,0:T(1,128)S(1)} %all-to-all-done.1.fetched_ref, f32[8,3,256]{2,1,0:T(4,128)S(1)} %bitcast.13), custom_call_target="tpu_custom_call" | custom-call | tf_op jit(solution)/shard_map/render/pallas_call | solution.py:633
  68.6 14.3 %all_to_all.15.returned_ref = f32[32,1,3456]{2,1,0:T(1,128)S(1)} all-to-all(f32[32,1,3456]{2,1,0:T(1,128)S(1)} %get-tuple-element.18), channel_id=1, replica_groups=mesh['tiles'=32,'views'=4] {'tiles'}, dimensions={0} | all-to-all | bytes 884736 | tf_op jit(solution)/shard_map/all_to_all | solution.py:727
  82.9 4.9 %collect.1 = (f32[80,256]{1,0:T(8,128)S(1)}, f32[80,256]{1,0:T(8,128)S(1)}, f32[80,256]{1,0:T(8,128)S(1)}, f32[80,256]{1,0:T(8,128)S(1)}) custom-call(f32[8]{0:T(128)S(1)} %pad_maximum_fusion.camera_ref, s32[1]{0:T(128)} %bitcast.6.place_ref, s32[32,1,384]{2,1,0:T(1,128)S(1)} %all-to-all-done.asked_ref, f32[32,1,3456]{2,1,0:T(1,128)S(1)} %all_to_all.15.returned_ref), custom_call_target="tpu_custom_call" | custom-call | tf_op jit(solution)/shard_map/collect/pallas_call | solution.py:728
  87.8 1.3 %collective-permute-start = (f32[80,256]{1,0:T(8,128)S(1)}, f32[80,256]{1,0:T(8,128)S(1)}, u32[]{:S(2)}, u32[]{:S(2)}) collective-permute-start(f32[80,256]{1,0:T(8,128)S(1)} %get-tuple-element.20), channel_id=1, source_target_pairs={{0,1},{1,2},{2,3},{3,0},{4,5},{5,6},{6,7},{7,4},{8,9},{9,10},{10,1... | collective-permute-start | bytes 245768 | tf_op jit(solution)/shard_map/ppermute | solution.py:738
  89.1 2.8 %collective-permute-start.1 = (f32[80,256]{1,0:T(8,128)S(1)}, f32[80,256]{1,0:T(8,128)S(1)}, u32[]{:S(2)}, u32[]{:S(2)}) collective-permute-start(f32[80,256]{1,0:T(8,128)S(1)} %get-tuple-element.21), channel_id=1, source_target_pairs={{0,2},{1,3},{2,0},{3,1},{4,6},{5,7},{6,4},{7,5},{8,10},{9,11},{10,... | collective-permute-start | bytes 245768 | tf_op jit(solution)/shard_map/ppermute | solution.py:738
  91.9 0.4 collective-permute-start.2
  92.3 0.6 copy.9
  92.9 0.7 collective-permute-done.refs_1_
  93.5 2.8 %collective-permute-done.1.refs_2_ = f32[80,256]{1,0:T(8,128)S(1)} collective-permute-done((f32[80,256]{1,0:T(8,128)S(1)}, f32[80,256]{1,0:T(8,128)S(1)}, u32[]{:S(2)}, u32[]{:S(2)}) %collective-permute-start.1) | collective-permute-done | bytes 81952 | tf_op jit(solution)/shard_map/ppermute | solution.py:738
  96.3 0.0 collective-permute-done.2.refs_3_
  96.3 1.8 %pull.1 = f32[59,2048]{1,0:T(8,128)} custom-call(f32[80,256]{1,0:T(8,128)S(1)} %get-tuple-element.19.refs_0_, f32[80,256]{1,0:T(8,128)S(1)} %collective-permute-done.refs_1_, f32[80,256]{1,0:T(8,128)S(1)} %collective-permute-done.1.refs_2_, f32[80,256]{1,0:T(8,128)S(1)} %collective-permute-done.2.refs_3_, f32[59,8,256]{2,1,0:T(8,128)S(1)} %get-tuple-element.23.refs_4_), custom_call_target="tpu_custom_call" | custom-call | tf_op jit(solution)/shard_map/pull/pallas_call | solution.py:741
  (1 shorter events, 0.0 us)
Async XLA Ops:
  0.6 42.8 %copy-start.3 = (s32[1,8]{1,0:T(1,128)S(1)}, s32[1,8]{1,0:T(1,128)}, u32[]{:S(2)}) copy-start(s32[1,8]{1,0:T(1,128)} %param.9) | copy-start | bytes 100
  0.6 42.8 %copy-start.1 = (s32[1,8,1024]{2,1,0:T(8,128)S(1)}, s32[1,8,1024]{2,1,0:T(8,128)}, u32[]{:S(2)}) copy-start(s32[1,8,1024]{2,1,0:T(8,128)} %param.8) | copy-start | bytes 98308
  0.7 32.0 %copy-start.4 = (f32[1,8,3,256]{3,1,2,0:T(8,128)S(1)}, f32[1,8,3,256]{3,1,2,0:T(8,128)}, u32[]{:S(2)}) copy-start(f32[1,8,3,256]{3,1,2,0:T(8,128)} %param.10) | copy-start | bytes 73732
  3.9 39.6 %copy-start.2 = (s32[8,1024]{1,0:T(8,128)S(1)}, s32[8,1024]{1,0:T(8,128)}, u32[]{:S(2)}) copy-start(s32[8,1024]{1,0:T(8,128)} %get-tuple-element.13.rank_ref) | copy-start | bytes 98308
  3.9 16.1 %all-to-all-start = ((s32[32,1,384]{2,1,0:T(1,128)}), s32[32,1,384]{2,1,0:T(1,128)S(1)}, u32[]{:S(2)}, u32[]{:S(2)}) async-start(s32[32,1,384]{2,1,0:T(1,128)} %get-tuple-element.14), calls=%async_computation | async-start | bytes 98304 | tf_op jit(solution)/shard_map/all_to_all | solution.py:702
  15.5 1.6 %copy-start = (f32[59,8192]{1,0:T(8,128)S(1)}, f32[59,8192]{1,0:T(8,128)}, u32[]{:S(2)}) copy-start(f32[59,8192]{1,0:T(8,128)} %params_ref.1) | copy-start | bytes 5799940
  26.1 17.4 %all-to-all-start.1 = ((f32[32,1,3456]{2,1,0:T(1,128)}), f32[32,1,3456]{2,1,0:T(1,128)S(1)}, u32[]{:S(2)}, u32[]{:S(2)}) async-start(f32[32,1,3456]{2,1,0:T(1,128)} %lookup.1), calls=%async_computation.1 | async-start | bytes 884736 | tf_op jit(solution)/shard_map/all_to_all | solution.py:725
  87.8 5.8 %collective-permute-start = (f32[80,256]{1,0:T(8,128)S(1)}, f32[80,256]{1,0:T(8,128)S(1)}, u32[]{:S(2)}, u32[]{:S(2)}) collective-permute-start(f32[80,256]{1,0:T(8,128)S(1)} %get-tuple-element.20), channel_id=1, source_target_pairs={{0,1},{1,2},{2,3},{3,0},{4,5},{5,6},{6,7},{7,4},{8,9},{9,10},{10,1... | collective-permute-start | bytes 245768 | tf_op jit(solution)/shard_map/ppermute | solution.py:738
  89.1 7.2 %collective-permute-start.1 = (f32[80,256]{1,0:T(8,128)S(1)}, f32[80,256]{1,0:T(8,128)S(1)}, u32[]{:S(2)}, u32[]{:S(2)}) collective-permute-start(f32[80,256]{1,0:T(8,128)S(1)} %get-tuple-element.21), channel_id=1, source_target_pairs={{0,2},{1,3},{2,0},{3,1},{4,6},{5,7},{6,4},{7,5},{8,10},{9,11},{10,... | collective-permute-start | bytes 245768 | tf_op jit(solution)/shard_map/ppermute | solution.py:738
  91.9 4.4 %collective-permute-start.2 = (f32[80,256]{1,0:T(8,128)S(1)}, f32[80,256]{1,0:T(8,128)S(1)}, u32[]{:S(2)}, u32[]{:S(2)}) collective-permute-start(f32[80,256]{1,0:T(8,128)S(1)} %get-tuple-element.22), channel_id=1, source_target_pairs={{0,3},{1,0},{2,1},{3,2},{4,7},{5,4},{6,5},{7,6},{8,11},{9,8},{10,9... | collective-permute-start | bytes 245768 | tf_op jit(solution)/shard_map/ppermute | solution.py:738
